TPU v7x, 512 devices: a whole 4x8x8 slice. The times are simulated.
512 devices in a mesh: grp: 64 (over x, z, core), sub: 8 (over y).
Axes of the slice: x: 4, y: 8, z: 8, core: 2. Of those that a mesh axis runs over, the one named last changes fastest.
Arguments:
- dual_coeffs: bfloat16 [32, 196608], P(None, ('grp', 'sub')), may hold values from -6 to 6
- refine_select: int32 [196608], P(('grp', 'sub')), may hold values from 0 to 3
- refine_tiles: bfloat16 [4, 128, 32], replicated, may hold values from -1 to 1
- near_list: int32 [196608, 27], P(('grp', 'sub')), may hold values from -1 to 1151, as said below
- near_tiles: bfloat16 [27, 128, 128], replicated, may hold values from -0.25 to 0.25
- leaf_list: int32 [196608, 32], P(('grp', 'sub')), may hold values from -1 to 1151
- p2m: bfloat16 [169, 128], replicated, may hold values from -0.5 to 0.5
- m2m: bfloat16 [8, 169, 169], replicated, may hold values from -0.15625 to 0.15625
- leaf_m2l: bfloat16 [32, 169, 169], replicated, may hold values from -0.078125 to 0.078125
- coarse_list: int32 [24576, 16], P(('grp', 'sub')), may hold values from -1 to 1151
- coarse_m2l: bfloat16 [16, 169, 169], replicated, may hold values from -0.125 to 0.125
Outputs:
- tested: bfloat16 [32, 196608], P(None, ('grp', 'sub'))
Inputs may be any that keep to these rules, and one draw needn't show every extreme that they name: `near_list`: direction 13 of every box but box 0 names the box itself, 384 plus its index within its device.
All inputs are finite; a program needn't handle non-finite values.
Results may differ from a plain program's by a relative error of at most 0.007.
Values may be sent and summed in bfloat16 or wider, within the bound.
No kernel may reach another device: no remote copies, remote signals or barrier semaphores. Data moves between devices by JAX's collectives and lax.ppermute only.
A program may use at most 64 MiB of HBM per device.

v0:
```python
import jax
import jax.numpy as jnp
from jax import lax
from jax.sharding import PartitionSpec as P


def extended(block, sides, width):
    for axis, dim in sides:
        count = lax.axis_size(axis)
        forward = [(i, i + 1) for i in range(count - 1)]
        backward = [(target, source) for source, target in forward]
        low = lax.ppermute(
            lax.slice_in_dim(block, block.shape[dim] - width, None, axis=dim), axis, forward
        )
        high = lax.ppermute(lax.slice_in_dim(block, 0, width, axis=dim), axis, backward)
        block = jnp.concatenate([low, block, high], axis=dim)
    return block


def select_apply(tiles, select, vectors, transpose):
    total = None
    for kind in range(tiles.shape[0]):
        if transpose:
            term = jnp.einsum("si,sb->ib", tiles[kind], vectors, preferred_element_type=jnp.float32)
        else:
            term = jnp.dot(tiles[kind], vectors, preferred_element_type=jnp.float32)
        term = jnp.where(select[None, :] == kind, term, 0.0)
        total = term if total is None else total + term
    return total


def class_sum(tables, window, lists):
    window_rows = jnp.transpose(window)
    indices = jnp.transpose(lists)
    picked = jnp.take(window_rows, jnp.maximum(indices, 0), axis=0)
    picked = jnp.where(indices[:, :, None] >= 0, picked, jnp.zeros_like(picked))
    return jnp.einsum("kij,kbj->ib", tables, picked, preferred_element_type=jnp.float32)


def body(
    dual_coeffs,
    refine_select,
    refine_tiles,
    near_list,
    near_tiles,
    leaf_list,
    p2m,
    m2m,
    leaf_m2l,
    coarse_list,
    coarse_m2l,
):
    width = dual_coeffs.shape[1]
    order = p2m.shape[0]
    coarse_width = width // 8
    refined = select_apply(refine_tiles, refine_select, dual_coeffs, False).astype(jnp.bfloat16)
    multipoles = jnp.dot(p2m, refined, preferred_element_type=jnp.float32).astype(jnp.bfloat16)
    refined_window = extended(refined, ((("grp", "sub"), 1),), width)
    mult_window = extended(multipoles, ((("grp", "sub"), 1),), width)
    children = multipoles.reshape(order, coarse_width, 8)
    coarse_mult = jnp.einsum(
        "jqr,rpj->qp", m2m, children, preferred_element_type=jnp.float32
    ).astype(jnp.bfloat16)
    slab = lax.all_gather(coarse_mult, "sub", axis=1, tiled=True)
    coarse_window = extended(slab, (("grp", 1),), slab.shape[1])
    near_part = class_sum(near_tiles, refined_window, near_list)
    leaf_local = class_sum(leaf_m2l, mult_window, leaf_list)
    coarse_local = class_sum(coarse_m2l, coarse_window, coarse_list).astype(jnp.bfloat16)
    downward = jnp.einsum(
        "jrq,rp->qpj", m2m, coarse_local, preferred_element_type=jnp.float32
    ).reshape(order, width)
    local_exp = (leaf_local + downward).astype(jnp.bfloat16)
    field = near_part + jnp.einsum("qs,qb->sb", p2m, local_exp, preferred_element_type=jnp.float32)
    field = field.astype(jnp.bfloat16)
    return select_apply(refine_tiles, refine_select, field, True).astype(jnp.bfloat16)


def solution(mesh):
    placed = (
        P(None, ("grp", "sub")),
        P(("grp", "sub")),
        P(),
        P(("grp", "sub"), None),
        P(),
        P(("grp", "sub"), None),
        P(),
        P(),
        P(),
        P(("grp", "sub"), None),
        P(),
    )
    return jax.shard_map(
        body, mesh=mesh, in_specs=placed, out_specs=P(None, ("grp", "sub")), check_vma=False
    )
```

profile of v0, /device:TPU:6, one launch (start us, length us, event | category | flops | bytes accessed | tf_op | source)
XLA Modules:
  0.0 166.0 jit_solution(14119550411286508540)
XLA Ops:
  0.0 0.8 broadcast_compare_fusion.3
  0.9 1.0 convolution_select_fusion.3
  1.9 1.0 fusion.37
  2.9 1.0 fusion.36
  3.8 1.0 fusion.42
  4.8 13.6 %collective-permute-start.1 = (bf16[128,384]{1,0:T(8,128)(2,1)S(1)}, bf16[128,384]{1,0:T(8,128)(2,1)S(1)}, u32[]{:S(2)}, u32[]{:S(2)}) collective-permute-start(bf16[128,384]{1,0:T(8,128)(2,1)S(1)} %fusion.42), channel_id=1, source_target_pairs={{1,0},{2,1},{3,2},{4,3},{5,4},{6,5},{7,6},{8,7},{9,8},{10,9},{11,1... | collective-permute-start | bytes 294920 | tf_op jit(solution)/shard_map/ppermute | solution.py:15
  18.4 1.9 %collective-permute-start = (bf16[128,384]{1,0:T(8,128)(2,1)S(1)}, bf16[128,384]{1,0:T(8,128)(2,1)}, u32[]{:S(2)}, u32[]{:S(2)}) collective-permute-start(bf16[128,384]{1,0:T(8,128)(2,1)S(1)} %fusion.42), channel_id=1, source_target_pairs={{0,1},{1,2},{2,3},{3,4},{4,5},{5,6},{6,7},{7,8},{8,9},{9,10},{10,1... | collective-permute-start | bytes 294920 | tf_op jit(solution)/shard_map/ppermute | solution.py:12
  20.3 1.0 fusion.48
  21.3 7.9 %collective-permute-start.3 = (bf16[169,384]{1,0:T(8,128)(2,1)S(1)}, bf16[169,384]{1,0:T(8,128)(2,1)}, u32[]{:S(2)}, u32[]{:S(2)}) collective-permute-start(bf16[169,384]{1,0:T(8,128)(2,1)S(1)} %fusion.48), channel_id=1, source_target_pairs={{1,0},{2,1},{3,2},{4,3},{5,4},{6,5},{7,6},{8,7},{9,8},{10,9},{11,1... | collective-permute-start | bytes 389384 | tf_op jit(solution)/shard_map/ppermute | solution.py:15
  29.2 1.9 %collective-permute-start.2 = (bf16[169,384]{1,0:T(8,128)(2,1)S(1)}, bf16[169,384]{1,0:T(8,128)(2,1)}, u32[]{:S(2)}, u32[]{:S(2)}) collective-permute-start(bf16[169,384]{1,0:T(8,128)(2,1)S(1)} %fusion.48), channel_id=1, source_target_pairs={{0,1},{1,2},{2,3},{3,4},{4,5},{5,6},{6,7},{7,8},{8,9},{9,10},{10,1... | collective-permute-start | bytes 389384 | tf_op jit(solution)/shard_map/ppermute | solution.py:12
  31.3 1.4 fusion.64
  32.7 26.7 %all_gather.3 = bf16[169,384]{0,1:T(8,128)(2,1)} all-gather(bf16[169,48]{0,1:T(8,128)(2,1)S(1)} %fusion.64), channel_id=1, replica_groups=mesh['grp'=64,'sub'=8] {'sub'}, dimensions={1}, use_global_device_ids=true | all-gather | bytes 146016 | tf_op jit(solution)/shard_map/all_gather | solution.py:64
  59.4 1.9 %collective-permute-start.5 = (bf16[169,384]{0,1:T(8,128)(2,1)}, bf16[169,384]{0,1:T(8,128)(2,1)}, u32[]{:S(2)}, u32[]{:S(2)}) collective-permute-start(bf16[169,384]{0,1:T(8,128)(2,1)} %all_gather.3), channel_id=1, source_target_pairs={{8,0},{16,8},{24,16},{32,24},{40,32},{48,40},{56,48},{64,56},{72,6... | collective-permute-start | bytes 389384 | tf_op jit(solution)/shard_map/ppermute | solution.py:15
  65.1 2.4 %collective-permute-start.4 = (bf16[169,384]{0,1:T(8,128)(2,1)}, bf16[169,384]{0,1:T(8,128)(2,1)}, u32[]{:S(2)}, u32[]{:S(2)}) collective-permute-start(bf16[169,384]{0,1:T(8,128)(2,1)} %all_gather.3), channel_id=1, source_target_pairs={{0,8},{8,16},{16,24},{24,32},{32,40},{40,48},{48,56},{56,64},{64,7... | collective-permute-start | bytes 389384 | tf_op jit(solution)/shard_map/ppermute | solution.py:12
  67.6 1.0 maximum_bitcast_fusion.2
  68.8 21.7 %gather_fusion = bf16[10368,128]{1,0:T(8,128)(2,1)} fusion(bf16[1152,128]{1,0:T(8,128)(2,1)S(1)} %copy.17, s32[11264]{0:T(1024)S(1)} %pad_clamp_fusion), kind=kCustom, calls=%fused_computation | custom fusion | bytes 5349888 | tf_op jit(solution)/shard_map/jit(_take)/gather | solution.py:35
  90.5 5.5 %fusion.32 = f32[384,128]{1,0:T(8,128)} fusion(bf16[27,128,128]{2,1,0:T(8,128)(2,1)} %param.15, bf16[27,384,128]{2,1,0:T(8,128)(2,1)} %bitcast.106, pred[27,384]{1,0:T(8,128)(4,1)S(1)} %copy-done.9, pred[27,384]{1,0:T(8,128)(4,1)S(1)} %copy-done.10), kind=kOutput, calls=%fused_computation.26 | convolution fusion | flops 342392832 | bytes 3756288 | tf_op jit(solution)/shard_map/kij,kbj->ib/dot_general | solution.py:37
  96.0 1.8 %maximum_bitcast_fusion.1 = bf16[1152,169]{0,1:T(8,128)(2,1)} fusion(bf16[169,384]{1,0:T(8,128)(2,1)} %collective-permute-done.3, bf16[169,384]{1,0:T(8,128)(2,1)S(1)} %fusion.48, bf16[169,384]{1,0:T(8,128)(2,1)} %collective-permute-done.2), kind=kLoop, calls=%fused_computation.55 | loop fusion | flops 1168128 | bytes 778752 | tf_op jit(solution)/shard_map/transpose | solution.py:33
  97.8 1.2 copy.18
  99.1 2.1 %maximum_bitcast_fusion = bf16[1152,169]{1,0:T(8,128)(2,1)} fusion(bf16[169,384]{0,1:T(8,128)(2,1)} %collective-permute-done.5, bf16[169,384]{0,1:T(8,128)(2,1)} %all_gather.3, bf16[169,384]{0,1:T(8,128)(2,1)} %collective-permute-done.4), kind=kLoop, calls=%fused_computation.54 | loop fusion | flops 1168128 | bytes 778752 | tf_op jit(solution)/shard_map/transpose | solution.py:33
  101.2 3.9 %gather_fusion.2 = bf16[768,169]{1,0:T(8,128)(2,1)} fusion(bf16[1152,169]{1,0:T(8,128)(2,1)} %maximum_bitcast_fusion, s32[1024]{0:T(1024)S(1)} %pad_clamp_fusion.1), kind=kCustom, calls=%fused_computation.2 | custom fusion | bytes 522240 | tf_op jit(solution)/shard_map/jit(_take)/gather | solution.py:35
  105.1 48.9 %gather_fusion.1 = bf16[12288,169]{1,0:T(8,128)(2,1)} fusion(bf16[1152,169]{1,0:T(8,128)(2,1)S(1)} %copy.18, s32[12288]{0:T(1024)S(1)} %copy-done.3), kind=kCustom, calls=%fused_computation.1 | custom fusion | bytes 8355840 | tf_op jit(solution)/shard_map/jit(_take)/gather | solution.py:35
  154.0 2.9 %convolution_bitcast_fusion = f32[169,48,8]{0,1,2:T(8,128)S(1)} fusion(bf16[16,169,169]{2,0,1:T(8,128)(2,1)} %param.21, bf16[8,169,169]{2,0,1:T(8,128)(2,1)} %param.18, bf16[16,48,169]{2,1,0:T(8,128)(2,1)} %bitcast.107, pred[16,48]{1,0:T(8,128)(4,1)S(1)} %copy-done.19, pred[16,48]{1,0:T(8,128)(4,1)S(1)} %copy-done.20), kind=kOutput, calls=%fused_computation.20 | convolution fusion | flops 66072240 | bytes 1891632 | tf_op jit(solution)/shard_map/jrq,rp->qpj/dot_general | solution.py:69
  157.0 7.7 %fusion.43 = bf16[384,128]{1,0:T(8,128)(2,1)S(1)} fusion(f32[384,128]{1,0:T(8,128)} %fusion.32, bf16[169,128]{1,0:T(8,128)(2,1)S(1)} %copy-done.7, bf16[32,169,169]{2,0,1:T(8,128)(2,1)S(1)} %copy-done, bf16[32,384,169]{2,1,0:T(8,128)(2,1)} %bitcast.105, pred[32,384]{1,0:T(8,128)(4,1)S(1)} %broadcast_compare_fusion, pred[32,384]{1,0:T(8,128)(4,1)S(1)} %copy-done.8, ...), kind=kOutput, calls=%fused_computation.35 | convolution fusion | flops 722909952 | bytes 6603584 | tf_op jit(solution)/shard_map/qs,qb->sb/dot_general | solution.py:73
  (69 shorter events, 5.4 us)
Async XLA Ops:
  0.0 156.9 %copy-start = (bf16[32,169,169]{2,0,1:T(8,128)(2,1)S(1)}, bf16[32,169,169]{2,0,1:T(8,128)(2,1)}, u32[]{:S(2)}) copy-start(bf16[32,169,169]{2,0,1:T(8,128)(2,1)} %param.19) | copy-start | bytes 5483716
  0.0 61.3 %copy-start.6 = (s32[48,16]{0,1:T(8,128)S(1)}, s32[48,16]{0,1:T(8,128)}, u32[]{:S(2)}) copy-start(s32[48,16]{0,1:T(8,128)} %param.20) | copy-start | bytes 9220
  0.0 62.5 %copy-start.1 = (s32[384,27]{0,1:T(8,128)S(1)}, s32[384,27]{0,1:T(8,128)}, u32[]{:S(2)}) copy-start(s32[384,27]{0,1:T(8,128)} %param.14) | copy-start | bytes 124420
  0.0 63.7 %copy-start.2 = (s32[384,32]{0,1:T(8,128)S(1)}, s32[384,32]{0,1:T(8,128)}, u32[]{:S(2)}) copy-start(s32[384,32]{0,1:T(8,128)} %param.16) | copy-start | bytes 147460
  0.9 28.3 %copy-start.11 = (pred[384]{0:T(512)(128)(4,1)}, pred[384]{0:T(512)(128)(4,1)S(1)}, u32[]{:S(2)}) copy-start(pred[384]{0:T(512)(128)(4,1)S(1)} %get-tuple-element.5) | copy-start | bytes 1156
  0.9 28.3 %copy-start.13 = (pred[384]{0:T(512)(128)(4,1)}, pred[384]{0:T(512)(128)(4,1)S(1)}, u32[]{:S(2)}) copy-start(pred[384]{0:T(512)(128)(4,1)S(1)} %get-tuple-element.8) | copy-start | bytes 1156
  0.9 28.3 %copy-start.15 = (pred[384]{0:T(512)(128)(4,1)}, pred[384]{0:T(512)(128)(4,1)S(1)}, u32[]{:S(2)}) copy-start(pred[384]{0:T(512)(128)(4,1)S(1)} %get-tuple-element.6) | copy-start | bytes 1156
  4.8 60.3 %collective-permute-start.1 = (bf16[128,384]{1,0:T(8,128)(2,1)S(1)}, bf16[128,384]{1,0:T(8,128)(2,1)S(1)}, u32[]{:S(2)}, u32[]{:S(2)}) collective-permute-start(bf16[128,384]{1,0:T(8,128)(2,1)S(1)} %fusion.42), channel_id=1, source_target_pairs={{1,0},{2,1},{3,2},{4,3},{5,4},{6,5},{7,6},{8,7},{9,8},{10,9},{11,1... | collective-permute-start | bytes 294920 | tf_op jit(solution)/shard_map/ppermute | solution.py:15
  18.4 49.2 %collective-permute-start = (bf16[128,384]{1,0:T(8,128)(2,1)S(1)}, bf16[128,384]{1,0:T(8,128)(2,1)}, u32[]{:S(2)}, u32[]{:S(2)}) collective-permute-start(bf16[128,384]{1,0:T(8,128)(2,1)S(1)} %fusion.42), channel_id=1, source_target_pairs={{0,1},{1,2},{2,3},{3,4},{4,5},{5,6},{6,7},{7,8},{8,9},{9,10},{10,1... | collective-permute-start | bytes 294920 | tf_op jit(solution)/shard_map/ppermute | solution.py:12
  21.3 74.8 %collective-permute-start.3 = (bf16[169,384]{1,0:T(8,128)(2,1)S(1)}, bf16[169,384]{1,0:T(8,128)(2,1)}, u32[]{:S(2)}, u32[]{:S(2)}) collective-permute-start(bf16[169,384]{1,0:T(8,128)(2,1)S(1)} %fusion.48), channel_id=1, source_target_pairs={{1,0},{2,1},{3,2},{4,3},{5,4},{6,5},{7,6},{8,7},{9,8},{10,9},{11,1... | collective-permute-start | bytes 389384 | tf_op jit(solution)/shard_map/ppermute | solution.py:15
  29.2 66.9 %collective-permute-start.2 = (bf16[169,384]{1,0:T(8,128)(2,1)S(1)}, bf16[169,384]{1,0:T(8,128)(2,1)}, u32[]{:S(2)}, u32[]{:S(2)}) collective-permute-start(bf16[169,384]{1,0:T(8,128)(2,1)S(1)} %fusion.48), channel_id=1, source_target_pairs={{0,1},{1,2},{2,3},{3,4},{4,5},{5,6},{6,7},{7,8},{8,9},{9,10},{10,1... | collective-permute-start | bytes 389384 | tf_op jit(solution)/shard_map/ppermute | solution.py:12
  59.4 39.7 %collective-permute-start.5 = (bf16[169,384]{0,1:T(8,128)(2,1)}, bf16[169,384]{0,1:T(8,128)(2,1)}, u32[]{:S(2)}, u32[]{:S(2)}) collective-permute-start(bf16[169,384]{0,1:T(8,128)(2,1)} %all_gather.3), channel_id=1, source_target_pairs={{8,0},{16,8},{24,16},{32,24},{40,32},{48,40},{56,48},{64,56},{72,6... | collective-permute-start | bytes 389384 | tf_op jit(solution)/shard_map/ppermute | solution.py:15
  65.1 34.0 %collective-permute-start.4 = (bf16[169,384]{0,1:T(8,128)(2,1)}, bf16[169,384]{0,1:T(8,128)(2,1)}, u32[]{:S(2)}, u32[]{:S(2)}) collective-permute-start(bf16[169,384]{0,1:T(8,128)(2,1)} %all_gather.3), channel_id=1, source_target_pairs={{0,8},{8,16},{16,24},{24,32},{32,40},{40,48},{48,56},{56,64},{64,7... | collective-permute-start | bytes 389384 | tf_op jit(solution)/shard_map/ppermute | solution.py:12
  68.7 21.8 %copy-start.9 = (pred[27,384]{1,0:T(8,128)(4,1)S(1)}, pred[27,384]{1,0:T(8,128)(4,1)}, u32[]{:S(2)}) copy-start(pred[27,384]{1,0:T(8,128)(4,1)} %broadcast_compare_fusion.1) | copy-start | bytes 31108
  68.8 21.7 %copy-start.10 = (pred[27,384]{1,0:T(8,128)(4,1)S(1)}, pred[27,384]{1,0:T(8,128)(4,1)}, u32[]{:S(2)}) copy-start(pred[27,384]{1,0:T(8,128)(4,1)} %compare_bitcast_fusion.1) | copy-start | bytes 31108
  97.8 7.3 %copy-start.3 = (s32[12288]{0:T(1024)S(1)}, s32[12288]{0:T(1024)}, u32[]{:S(2)}) copy-start(s32[12288]{0:T(1024)} %broadcast_clamp_fusion) | copy-start | bytes 147460
  105.1 48.9 %copy-start.19 = (pred[16,48]{1,0:T(8,128)(4,1)S(1)}, pred[16,48]{1,0:T(8,128)(4,1)}, u32[]{:S(2)}) copy-start(pred[16,48]{1,0:T(8,128)(4,1)} %broadcast_compare_fusion.2) | copy-start | bytes 2308
  105.1 48.9 %copy-start.20 = (pred[16,48]{1,0:T(8,128)(4,1)S(1)}, pred[16,48]{1,0:T(8,128)(4,1)}, u32[]{:S(2)}) copy-start(pred[16,48]{1,0:T(8,128)(4,1)} %compare_bitcast_fusion.2) | copy-start | bytes 2308
  154.0 2.9 %copy-start.8 = (pred[32,384]{1,0:T(8,128)(4,1)S(1)}, pred[32,384]{1,0:T(8,128)(4,1)}, u32[]{:S(2)}) copy-start(pred[32,384]{1,0:T(8,128)(4,1)} %compare_bitcast_fusion) | copy-start | bytes 36868
  156.9 7.8 %copy-start.4 = (bf16[4,128,32]{1,2,0:T(8,128)(2,1)S(1)}, bf16[4,128,32]{1,2,0:T(8,128)(2,1)}, u32[]{:S(2)}) copy-start(bf16[4,128,32]{1,2,0:T(8,128)(2,1)} %param.13) | copy-start | bytes 98308
  156.9 7.8 %copy-start.18 = (pred[384]{0:T(512)(128)(4,1)S(1)}, pred[384]{0:T(512)(128)(4,1)}, u32[]{:S(2)}) copy-start(pred[384]{0:T(512)(128)(4,1)} %copy-done.17) | copy-start | bytes 1156
  157.0 7.9 %copy-start.16 = (pred[384]{0:T(512)(128)(4,1)S(1)}, pred[384]{0:T(512)(128)(4,1)}, u32[]{:S(2)}) copy-start(pred[384]{0:T(512)(128)(4,1)} %copy-done.15) | copy-start | bytes 1156
  157.0 8.1 %copy-start.14 = (pred[384]{0:T(512)(128)(4,1)S(1)}, pred[384]{0:T(512)(128)(4,1)}, u32[]{:S(2)}) copy-start(pred[384]{0:T(512)(128)(4,1)} %copy-done.13) | copy-start | bytes 1156
  157.0 8.2 %copy-start.12 = (pred[384]{0:T(512)(128)(4,1)S(1)}, pred[384]{0:T(512)(128)(4,1)}, u32[]{:S(2)}) copy-start(pred[384]{0:T(512)(128)(4,1)} %copy-done.11) | copy-start | bytes 1156
  (3 other events, 6.4 us)
where the time goes:
time: 167 us; the launch traced here: 166 us
  local copies, waits for them, and re-layouts  76.4 us (46%)
  starting transfers between devices  29.6 us (18%)
  blocking collectives  26.7 us (16%)
  matrix products  23.6 us (14%)
  other arithmetic  9.3 us (6%)
    gather x3, local copies, waits for them, and re-layouts, class_sum(): picked = jnp.take(window_rows, jnp.maximum(indices, 0), axis=0)  74.6 us
    all_gather x1, blocking collectives, body(): slab = lax.all_gather(coarse_mult, 'sub', axis=1, tiled=True)  26.7 us
    ppermute x3, starting transfers between devices, extended(): lax.ppermute(lax.slice_in_dim(block, 0, width, axis=dim), axis, backward)  23.3 us
    dot_general x1, matrix products, body(): jnp.einsum('qs,qb->sb', p2m, local_exp, preferred_element_type=jnp.float32)  7.74 us
    ppermute x3, starting transfers between devices, extended(): lax.ppermute(lax.slice_in_dim(block, block.shape[dim] - width, None, axis...  6.25 us
    dot_general x1, matrix products, class_sum(): jnp.einsum('kij,kbj->ib', tables, picked, preferred_element_type=jnp.floa...  5.54 us
    transpose x3, other arithmetic, class_sum(): window_rows = jnp.transpose(window)  4.8 us
    dot_general x4, matrix products, select_apply(): term = jnp.dot(tiles[kind], vectors, preferred_element_type=jnp.float32)  3.89 us
  transfers between devices with their start and end apart: 6, of which 0 were waited for; matrix products, arithmetic and copies ran while one was open for 23% of the time, Pallas kernels for 0%

commit v1 on v0

v1 whole, which is shorter than its diff:
```python
import functools

import jax
import jax.numpy as jnp
from jax import lax
from jax.experimental import pallas as pl
from jax.experimental.pallas import tpu as pltpu
from jax.sharding import PartitionSpec as P

F32 = jnp.float32
BF16 = jnp.bfloat16
NT = (((1,), (1,)), ((), ()))
TN = (((0,), (0,)), ((), ()))


def dot(a, b, dims=(((1,), (0,)), ((), ()))):
    return lax.dot_general(a, b, dims, preferred_element_type=F32)


def refine_rows(payload, joined):
    span = joined.shape[1] // 4
    values = payload[:span, :].astype(F32)
    kind = payload[span : span + 1, :].astype(F32)
    spread = jnp.concatenate([jnp.where(kind == k, values, 0.0) for k in range(4)], axis=0)
    return dot(jnp.transpose(spread).astype(BF16), joined, NT).astype(BF16)


def join_tiles(tiles_ref):
    return jnp.concatenate([tiles_ref[k] for k in range(4)], axis=1)


def upward_kernel(payload_ref, tiles_ref, p2m_ref, m2m_ref, out_ref, mult_ref):
    copies, coarse, _ = out_ref.shape
    order = p2m_ref.shape[0]
    refined = refine_rows(payload_ref[...], join_tiles(tiles_ref))
    mult = dot(refined, p2m_ref[...], NT).astype(BF16).astype(F32)
    mult_ref[0] = mult[:, :128]
    mult_ref[1, :, : order - 128] = mult[:, 128:]
    total = jnp.zeros((coarse, order), F32)
    for j in range(8):
        rows = [mult_ref[half, pl.ds(j, coarse, stride=8), :] for half in range(2)]
        rows = jnp.concatenate(rows, axis=1)[:, :order].astype(BF16)
        total = total + dot(rows, m2m_ref[j], NT)
    out_ref[...] = jnp.zeros_like(out_ref)
    for d in range(copies):
        out_ref[d, :, :order] = total.astype(BF16)


def near_leaf_kernel(
    own_ref, low_ref, high_ref, near_list_ref, leaf_list_ref, tiles_ref, near_ref, m2l_ref, p2m_ref,
    near_out, leaf_out, window, tail, lists, near_tab, leaf_tab, hot,
):
    boxes = own_ref.shape[1]
    order, width = p2m_ref.shape
    n_near, n_leaf = near_list_ref.shape[1], leaf_list_ref.shape[1]
    near_groups, leaf_groups = -(-n_near // 4), -(-n_leaf // 4)
    joined = join_tiles(tiles_ref)
    rows = jnp.concatenate(
        [refine_rows(ref[...], joined) for ref in (low_ref, own_ref, high_ref)], axis=0
    )
    for b in range(4):
        window[:, b * width : (b + 1) * width] = rows[b * 256 : (b + 1) * 256]
    tail[...] = jnp.zeros_like(tail)
    tail[:128, :width] = rows[1024:]
    tail[128:, width:] = rows[1024:]
    near_tab[...] = jnp.zeros_like(near_tab)
    for k in range(n_near):
        near_tab[k // 4, :, (k % 4) * width : (k % 4 + 1) * width] = near_ref[k]
    for c in range(n_leaf):
        leaf_tab[c // 4, :order, (c % 4) * width : (c % 4 + 1) * width] = dot(
            m2l_ref[c], p2m_ref[...]
        ).astype(BF16)
    lists[...] = jnp.full_like(lists, -1)
    lists[0, :, :n_near] = near_list_ref[...]
    lists[1, :, :n_leaf] = leaf_list_ref[...]
    near_out[...] = jnp.zeros_like(near_out)
    leaf_out[...] = jnp.zeros_like(leaf_out)
    spot = lax.broadcasted_iota(jnp.int32, (boxes, 256), 1)

    def group(which, g, table, out):
        columns = pltpu.roll(lists[which], lax.rem(128 - 4 * g, 128), 1)
        index = [columns[:, c : c + 1] for c in range(4)]
        for c in range(4):
            hot[c * boxes : (c + 1) * boxes, :] = jnp.where(
                (index[c] & 255) == spot, 1.0, 0.0
            ).astype(BF16)
        first = dot(hot[...], window[:, : 2 * width])
        second = dot(hot[...], window[:, 2 * width :])
        picked = []
        for c in range(4):
            if c % 2 == 0:
                pair = jnp.concatenate(
                    [hot[c * boxes : (c + 1) * boxes, :128], hot[(c + 1) * boxes : (c + 2) * boxes, :128]],
                    axis=1,
                )
                last = dot(pair, tail[...])
            at = slice(c * boxes, (c + 1) * boxes)
            block = jnp.broadcast_to(index[c] >> 8, (boxes, width))
            value = jnp.where(block == 4, last[:, (c % 2) * width : (c % 2 + 1) * width], 0.0)
            value = jnp.where(block == 3, second[at, width:], value)
            value = jnp.where(block == 2, second[at, :width], value)
            value = jnp.where(block == 1, first[at, width:], value)
            value = jnp.where(block == 0, first[at, :width], value)
            picked.append(value.astype(BF16))
        out[...] += dot(jnp.concatenate(picked, axis=1), table[g], NT)

    def near_step(g, carry):
        group(0, g, near_tab, near_out)
        return carry

    def leaf_step(g, carry):
        group(1, g, leaf_tab, leaf_out)
        return carry

    lax.fori_loop(0, near_groups, near_step, 0)
    lax.fori_loop(0, leaf_groups, leaf_step, 0)


def downward_kernel(
    near_part_ref, leaf_local_ref, slab_ref, low_ref, high_ref, list_ref, payload_ref,
    tiles_ref, p2m_ref, m2m_ref, m2l_ref, out_ref, down,
):
    order = p2m_ref.shape[0]
    coarse, classes = list_ref.shape
    span = out_ref.shape[0]
    index = list_ref[...]
    window = jnp.concatenate([low_ref[...], slab_ref[...], high_ref[...]], axis=0)
    spot = lax.broadcasted_iota(jnp.int32, (coarse, window.shape[0]), 1)
    hot = jnp.concatenate(
        [jnp.where(index[:, c : c + 1] == spot, 1.0, 0.0).astype(BF16) for c in range(classes)], axis=0
    )
    picked = dot(hot, window).astype(BF16)
    total = jnp.zeros((coarse, order), F32)
    for c in range(classes):
        total = total + dot(picked[c * coarse : (c + 1) * coarse, :order], m2l_ref[c], NT)
    local = total.astype(BF16)
    for j in range(8):
        part = dot(local, m2m_ref[j])
        down[0, pl.ds(j, coarse, stride=8), :] = part[:, :128]
        down[1, pl.ds(j, coarse, stride=8), : order - 128] = part[:, 128:]
    expansion = jnp.concatenate([down[0], down[1]], axis=1)[:, :order]
    expansion = (leaf_local_ref[:, :order] + expansion).astype(BF16)
    field = (near_part_ref[...] + dot(expansion, p2m_ref[...])).astype(BF16)
    by_kind = dot(join_tiles(tiles_ref), field, (((0,), (1,)), ((), ())))
    kind = payload_ref[span : span + 1, :].astype(F32)
    tested = jnp.zeros(out_ref.shape, F32)
    for k in range(4):
        tested = jnp.where(kind == k, by_kind[k * span : (k + 1) * span], tested)
    out_ref[...] = tested.astype(BF16)


def call(kernel, outs, scratch, args, flops, megabytes):
    return pl.pallas_call(
        kernel,
        out_shape=outs,
        in_specs=[pl.BlockSpec(memory_space=pltpu.VMEM)] * len(args),
        out_specs=jax.tree.map(lambda _: pl.BlockSpec(memory_space=pltpu.VMEM), outs),
        scratch_shapes=scratch,
        compiler_params=pltpu.CompilerParams(vmem_limit_bytes=40 * 1024 * 1024),
        cost_estimate=pl.CostEstimate(
            flops=flops, bytes_accessed=int(megabytes * 1e6), transcendentals=0
        ),
    )(*args)


def shifted(block, axis, step):
    count = lax.axis_size(axis)
    return lax.ppermute(block, axis, [(i, i + step) for i in range(count) if 0 <= i + step < count])


def body(
    dual_coeffs, refine_select, refine_tiles, near_list, near_tiles, leaf_list, p2m, m2m, leaf_m2l,
    coarse_list, coarse_m2l,
):
    span, boxes = dual_coeffs.shape
    order, width = p2m.shape
    coarse = boxes // 8
    subs = lax.axis_size("sub")
    kinds = jnp.broadcast_to(refine_select[None, :], (8, boxes)).astype(BF16)
    payload = jnp.concatenate([dual_coeffs, kinds], axis=0)
    low = shifted(payload, ("grp", "sub"), 1)
    high = shifted(payload, ("grp", "sub"), -1)
    mine = call(
        upward_kernel,
        jax.ShapeDtypeStruct((subs, coarse, 256), BF16),
        [pltpu.VMEM((2, boxes, 128), F32)],
        (payload, refine_tiles, p2m, m2m),
        100_000_000, 1.0,
    )
    slab = lax.all_to_all(mine, "sub", 0, 0).reshape(subs * coarse, 256)
    near_part, leaf_local = call(
        near_leaf_kernel,
        (jax.ShapeDtypeStruct((boxes, width), F32), jax.ShapeDtypeStruct((boxes, 176), F32)),
        [
            pltpu.VMEM((256, 4 * width), BF16),
            pltpu.VMEM((256, 2 * width), BF16),
            pltpu.VMEM((2, boxes, 128), jnp.int32),
            pltpu.VMEM((7, width, 4 * width), BF16),
            pltpu.VMEM((8, 176, 4 * width), BF16),
            pltpu.VMEM((4 * boxes, 256), BF16),
        ],
        (payload, low, high, near_list, leaf_list, refine_tiles, near_tiles, leaf_m2l, p2m),
        10_000_000_000, 5.0,
    )
    slab_low = shifted(slab, "grp", 1)
    slab_high = shifted(slab, "grp", -1)
    return call(
        downward_kernel,
        jax.ShapeDtypeStruct((span, boxes), BF16),
        [pltpu.VMEM((2, boxes, 128), F32)],
        (
            near_part, leaf_local, slab, slab_low, slab_high, coarse_list, payload, refine_tiles, p2m,
            m2m, coarse_m2l,
        ),
        1_000_000_000, 3.0,
    )


def solution(mesh):
    placed = (
        P(None, ("grp", "sub")),
        P(("grp", "sub")),
        P(),
        P(("grp", "sub"), None),
        P(),
        P(("grp", "sub"), None),
        P(),
        P(),
        P(),
        P(("grp", "sub"), None),
        P(),
    )
    return jax.shard_map(
        body, mesh=mesh, in_specs=placed, out_specs=P(None, ("grp", "sub")), check_vma=False
    )
```

time: 167 us -> 70.4 us (0.42)
  local copies, waits for them, and re-layouts: 76.4 us -> 14.8 us
  blocking collectives: 26.7 us -> 0 us
  matrix products: 23.6 us -> 0 us
  Pallas kernels: 0 us -> 23.6 us
  other arithmetic: 9.3 us -> 1.43 us
    gather x3 -> x0, local copies, waits for them, and re-layouts: 74.6 us -> none  [class_sum(): picked = jnp.take(window_rows, jnp.maximum(indices, 0), axis=0)]
    all_gather x1 -> x0, blocking collectives: 26.7 us -> none  [body(): slab = lax.all_gather(coarse_mult, 'sub', axis=1, tiled=True)]
    dot_general x13 -> x0, matrix products: 23.6 us -> none  [the longest x1 7.74 us: body(): jnp.einsum('qs,qb->sb', p2m, local_exp, preferred_element_type=jnp.float32)]
    pallas_call x0 -> x3, Pallas kernels: none -> 23.6 us  [call(): pl.pallas_call(kernel, out_shape=outs, in_specs=[pl.BlockSpec(memory_spac...]
    unnamed x42 -> x23, local copies, waits for them, and re-layouts: 0.12 us -> 14.8 us
    all_to_all x0 -> x1, starting transfers between devices: none -> 7.1 us  [body(): slab = lax.all_to_all(mine, 'sub', 0, 0).reshape(subs * coarse, 256)]
    ppermute x6 -> x4, starting transfers between devices: 29.6 us -> 22.5 us  [shifted(): lax.ppermute(block, axis, [(i, i + step) for i in range(count) if 0 <= i...]
    transpose x3 -> x0, other arithmetic: 4.8 us -> none  [class_sum(): window_rows = jnp.transpose(window)]
  transfers between devices with their start and end apart: 6 -> 5, of which waited for: 0 -> 0; matrix products, arithmetic and copies ran while one was open for 23% -> 13% of each run, Pallas kernels for 0% -> 27%
where the time goes in v1:
time: 70.4 us; the launch traced here: 69.5 us
  starting transfers between devices  29.6 us (42%)
  Pallas kernels  23.6 us (34%)
  local copies, waits for them, and re-layouts  14.8 us (21%)
  other arithmetic  1.43 us (2%)
    pallas_call x3, Pallas kernels, call(): pl.pallas_call(kernel, out_shape=outs, in_specs=[pl.BlockSpec(memory_spac...  23.6 us
    ppermute x4, starting transfers between devices, shifted(): lax.ppermute(block, axis, [(i, i + step) for i in range(count) if 0 <= i...  22.5 us
    unnamed x23, local copies, waits for them, and re-layouts  14.8 us
    all_to_all x1, starting transfers between devices, body(): slab = lax.all_to_all(mine, 'sub', 0, 0).reshape(subs * coarse, 256)  7.1 us
  transfers between devices with their start and end apart: 5, of which 0 were waited for; matrix products, arithmetic and copies ran while one was open for 13% of the time, Pallas kernels for 27%

profile of v1, /device:TPU:6, one launch (start us, length us, event | category | flops | bytes accessed | tf_op | source)
XLA Modules:
  0.0 69.5 jit_solution(1692164356391830135)
XLA Ops:
  0.0 0.7 convert_element_type.4
  0.7 0.9 %copy.14.tiles_ref = bf16[4,128,32]{2,1,0:T(8,128)(2,1)S(1)} copy(bf16[4,128,32]{1,2,0:T(8,128)(2,1)} %param.13) | data formatting | bytes 65536 | tf_op args[2]
  1.6 1.2 %copy.17.m2m_ref = bf16[8,169,169]{2,1,0:T(8,128)(2,1)S(1)} copy(bf16[8,169,169]{2,0,1:T(8,128)(2,1)} %param.18) | data formatting | bytes 913952 | tf_op args[7]
  2.8 0.7 %pad_maximum_fusion.own_ref.payload_ref = bf16[40,384]{1,0:T(8,128)(2,1)S(1)} fusion(bf16[8,384]{1,0:T(8,128)(2,1)S(1)} %broadcast_in_dim.2, bf16[32,384]{1,0:T(8,128)(2,1)} %param.11), kind=kLoop, calls=%fused_computation | loop fusion | flops 61440 | bytes 61440 | tf_op jit(solution)/shard_map/concatenate | solution.py:180
  3.6 0.8 %copy-done.4 = bf16[169,128]{1,0:T(8,128)(2,1)S(1)} copy-done((bf16[169,128]{1,0:T(8,128)(2,1)S(1)}, bf16[169,128]{1,0:T(8,128)(2,1)}, u32[]{:S(2)}) %copy-start.4) | copy-done | bytes 43288
  4.4 1.4 %shard_map.110 = bf16[8,48,256]{2,1,0:T(8,128)(2,1)} custom-call(bf16[40,384]{1,0:T(8,128)(2,1)S(1)} %pad_maximum_fusion.own_ref.payload_ref, bf16[4,128,32]{2,1,0:T(8,128)(2,1)S(1)} %copy.14.tiles_ref, bf16[169,128]{1,0:T(8,128)(2,1)S(1)} %copy-done.4, bf16[8,169,169]{2,1,0:T(8,128)(2,1)S(1)} %copy.17.m2m_ref), custom_call_target="tpu_custom_call" | custom-call | flops 100000000 | bytes 1000000 | tf_op jit(solution)/shard_map/pallas_call | solution.py:153
  5.8 0.9 %copy-done = bf16[8,169,169]{2,1,0:T(8,128)(2,1)} copy-done((bf16[8,169,169]{2,1,0:T(8,128)(2,1)}, bf16[8,169,169]{2,1,0:T(8,128)(2,1)S(1)}, u32[]{:S(2)}) %copy-start) | copy-done | bytes 457000
  6.7 7.1 %all-to-all-start = ((bf16[8,48,256]{2,1,0:T(8,128)(2,1)}), bf16[8,48,256]{2,1,0:T(8,128)(2,1)S(1)}, u32[]{:S(2)}, u32[]{:S(2)}) async-start(bf16[8,48,256]{2,1,0:T(8,128)(2,1)} %shard_map.110), calls=%async_computation | async-start | bytes 393216 | tf_op jit(solution)/shard_map/all_to_all | solution.py:190
  13.8 3.9 %collective-permute-start = (bf16[40,384]{1,0:T(8,128)(2,1)S(1)}, bf16[40,384]{1,0:T(8,128)(2,1)S(1)}, u32[]{:S(2)}, u32[]{:S(2)}) collective-permute-start(bf16[40,384]{1,0:T(8,128)(2,1)S(1)} %pad_maximum_fusion.own_ref.payload_ref), channel_id=1, source_target_pairs={{0,1},{1,2},{2,3},{3,4},{4,5},{5,6},{6,7},{7,8},{8,9},{9,10},{10,1... | collective-permute-start | bytes 92168 | tf_op jit(solution)/shard_map/ppermute | solution.py:168
  17.7 10.8 %collective-permute-start.1 = (bf16[40,384]{1,0:T(8,128)(2,1)S(1)}, bf16[40,384]{1,0:T(8,128)(2,1)}, u32[]{:S(2)}, u32[]{:S(2)}) collective-permute-start(bf16[40,384]{1,0:T(8,128)(2,1)S(1)} %pad_maximum_fusion.own_ref.payload_ref), channel_id=1, source_target_pairs={{1,0},{2,1},{3,2},{4,3},{5,4},{6,5},{7,6},{8,7},{9,8},{10,9},{11,1... | collective-permute-start | bytes 92168 | tf_op jit(solution)/shard_map/ppermute | solution.py:168
  28.5 3.3 %copy.15.m2l_ref = bf16[32,169,169]{2,1,0:T(8,128)(2,1)S(1)} copy(bf16[32,169,169]{2,0,1:T(8,128)(2,1)} %param.19) | data formatting | bytes 3655808 | tf_op args[8]
  31.8 0.0 copy-start.7
  31.8 0.0 copy-start.5
  31.8 0.9 %copy.12.near_list_ref = s32[384,27]{1,0:T(8,128)S(1)} copy(s32[384,27]{0,1:T(8,128)} %param.14) | data formatting | bytes 82944 | tf_op args[3]
  32.8 1.6 %copy.13.leaf_list_ref = s32[384,32]{1,0:T(8,128)} copy(s32[384,32]{0,1:T(8,128)} %param.16) | data formatting | bytes 98304 | tf_op args[5]
  34.4 2.9 %copy.21.m2l_ref = bf16[16,169,169]{2,1,0:T(8,128)(2,1)} copy(bf16[16,169,169]{2,0,1:T(8,128)(2,1)} %param.21) | data formatting | bytes 1827904 | tf_op args[10]
  37.3 0.1 copy.18.list_ref
  37.4 0.0 all-to-all-done
  37.4 2.1 %collective-permute-start.2 = (bf16[384,256]{1,0:T(8,128)(2,1)S(1)}, bf16[384,256]{1,0:T(8,128)(2,1)S(1)}, u32[]{:S(2)}, u32[]{:S(2)}) collective-permute-start(bf16[384,256]{1,0:T(8,128)(2,1)S(1)} %bitcast.1), channel_id=1, source_target_pairs={{0,8},{8,16},{16,24},{24,32},{32,40},{40,48},{48,56},{56,64},{64,7... | collective-permute-start | bytes 589832 | tf_op jit(solution)/shard_map/ppermute | solution.py:168
  39.5 5.8 %collective-permute-start.3 = (bf16[384,256]{1,0:T(8,128)(2,1)S(1)}, bf16[384,256]{1,0:T(8,128)(2,1)S(1)}, u32[]{:S(2)}, u32[]{:S(2)}) collective-permute-start(bf16[384,256]{1,0:T(8,128)(2,1)S(1)} %bitcast.2), channel_id=1, source_target_pairs={{8,0},{16,8},{24,16},{32,24},{40,32},{48,40},{56,48},{64,56},{72,6... | collective-permute-start | bytes 589832 | tf_op jit(solution)/shard_map/ppermute | solution.py:168
  45.3 0.9 %copy-done.3 = s32[384,32]{1,0:T(8,128)S(1)} copy-done((s32[384,32]{1,0:T(8,128)S(1)}, s32[384,32]{1,0:T(8,128)}, u32[]{:S(2)}) %copy-start.3) | copy-done | bytes 49176
  46.2 1.2 %copy-done.6 = bf16[27,128,128]{2,1,0:T(8,128)(2,1)S(1)} copy-done((bf16[27,128,128]{2,1,0:T(8,128)(2,1)S(1)}, bf16[27,128,128]{2,1,0:T(8,128)(2,1)}, u32[]{:S(2)}) %copy-start.6) | copy-done | bytes 884760
  47.3 19.0 %shard_map.109 = (f32[384,128]{1,0:T(8,128)S(1)}, f32[384,176]{1,0:T(8,128)S(1)}) custom-call(bf16[40,384]{1,0:T(8,128)(2,1)S(1)} %pad_maximum_fusion.own_ref.payload_ref, bf16[40,384]{1,0:T(8,128)(2,1)S(1)} %collective-permute-done.low_ref, bf16[40,384]{1,0:T(8,128)(2,1)} %collective-permute-done.1.high_ref, s32[384,27]{1,0:T(8,128)S(1)} %copy.12.near_list_ref, ...), custom_call_target="tpu_custom_call" | custom-call | flops 10000000000 | bytes 5000000 | tf_op jit(solution)/shard_map/pallas_call | solution.py:153
  66.4 3.1 %shard_map.111 = bf16[32,384]{1,0:T(8,128)(2,1)} custom-call(f32[384,128]{1,0:T(8,128)S(1)} %get-tuple-element.7.near_part_ref, f32[384,176]{1,0:T(8,128)S(1)} %get-tuple-element.8.leaf_local_ref, bf16[384,256]{1,0:T(8,128)(2,1)S(1)} %bitcast.3, bf16[384,256]{1,0:T(8,128)(2,1)S(1)} %collective-permute-done.2.low_ref, ...), custom_call_target="tpu_custom_call" | custom-call | flops 1000000000 | bytes 3000000 | tf_op jit(solution)/shard_map/pallas_call | solution.py:153
  (15 shorter events, 0.0 us)
Async XLA Ops:
  3.6 0.8 %copy-start.4 = (bf16[169,128]{1,0:T(8,128)(2,1)S(1)}, bf16[169,128]{1,0:T(8,128)(2,1)}, u32[]{:S(2)}) copy-start(bf16[169,128]{1,0:T(8,128)(2,1)} %p2m_ref.5) | copy-start | bytes 129796
  5.8 0.9 %copy-start = (bf16[8,169,169]{2,1,0:T(8,128)(2,1)}, bf16[8,169,169]{2,1,0:T(8,128)(2,1)S(1)}, u32[]{:S(2)}) copy-start(bf16[8,169,169]{2,1,0:T(8,128)(2,1)S(1)} %copy.17.m2m_ref) | copy-start | bytes 1370932
  6.7 30.7 %all-to-all-start = ((bf16[8,48,256]{2,1,0:T(8,128)(2,1)}), bf16[8,48,256]{2,1,0:T(8,128)(2,1)S(1)}, u32[]{:S(2)}, u32[]{:S(2)}) async-start(bf16[8,48,256]{2,1,0:T(8,128)(2,1)} %shard_map.110), calls=%async_computation | async-start | bytes 393216 | tf_op jit(solution)/shard_map/all_to_all | solution.py:190
  13.8 31.4 %collective-permute-start = (bf16[40,384]{1,0:T(8,128)(2,1)S(1)}, bf16[40,384]{1,0:T(8,128)(2,1)S(1)}, u32[]{:S(2)}, u32[]{:S(2)}) collective-permute-start(bf16[40,384]{1,0:T(8,128)(2,1)S(1)} %pad_maximum_fusion.own_ref.payload_ref), channel_id=1, source_target_pairs={{0,1},{1,2},{2,3},{3,4},{4,5},{5,6},{6,7},{7,8},{8,9},{9,10},{10,1... | collective-permute-start | bytes 92168 | tf_op jit(solution)/shard_map/ppermute | solution.py:168
  17.7 27.5 %collective-permute-start.1 = (bf16[40,384]{1,0:T(8,128)(2,1)S(1)}, bf16[40,384]{1,0:T(8,128)(2,1)}, u32[]{:S(2)}, u32[]{:S(2)}) collective-permute-start(bf16[40,384]{1,0:T(8,128)(2,1)S(1)} %pad_maximum_fusion.own_ref.payload_ref), channel_id=1, source_target_pairs={{1,0},{2,1},{3,2},{4,3},{5,4},{6,5},{7,6},{8,7},{9,8},{10,9},{11,1... | collective-permute-start | bytes 92168 | tf_op jit(solution)/shard_map/ppermute | solution.py:168
  31.8 5.5 %copy-start.7 = (s32[48,16]{0,1:T(8,128)S(1)}, s32[48,16]{0,1:T(8,128)}, u32[]{:S(2)}) copy-start(s32[48,16]{0,1:T(8,128)} %param.20) | copy-start | bytes 9220
  31.8 13.4 %copy-start.5 = (bf16[169,128]{1,0:T(8,128)(2,1)S(1)}, bf16[169,128]{1,0:T(8,128)(2,1)}, u32[]{:S(2)}) copy-start(bf16[169,128]{1,0:T(8,128)(2,1)} %p2m_ref.5) | copy-start | bytes 129796
  37.4 29.0 %copy-start.1 = (bf16[8,169,169]{2,1,0:T(8,128)(2,1)S(1)}, bf16[8,169,169]{2,1,0:T(8,128)(2,1)}, u32[]{:S(2)}) copy-start(bf16[8,169,169]{2,1,0:T(8,128)(2,1)} %copy-done) | copy-start | bytes 1370932
  37.4 29.0 %copy-start.2 = (bf16[16,169,169]{2,1,0:T(8,128)(2,1)S(1)}, bf16[16,169,169]{2,1,0:T(8,128)(2,1)}, u32[]{:S(2)}) copy-start(bf16[16,169,169]{2,1,0:T(8,128)(2,1)} %copy.21.m2l_ref) | copy-start | bytes 2741860
  37.4 29.0 %collective-permute-start.2 = (bf16[384,256]{1,0:T(8,128)(2,1)S(1)}, bf16[384,256]{1,0:T(8,128)(2,1)S(1)}, u32[]{:S(2)}, u32[]{:S(2)}) collective-permute-start(bf16[384,256]{1,0:T(8,128)(2,1)S(1)} %bitcast.1), channel_id=1, source_target_pairs={{0,8},{8,16},{16,24},{24,32},{32,40},{40,48},{48,56},{56,64},{64,7... | collective-permute-start | bytes 589832 | tf_op jit(solution)/shard_map/ppermute | solution.py:168
  39.5 26.9 %collective-permute-start.3 = (bf16[384,256]{1,0:T(8,128)(2,1)S(1)}, bf16[384,256]{1,0:T(8,128)(2,1)S(1)}, u32[]{:S(2)}, u32[]{:S(2)}) collective-permute-start(bf16[384,256]{1,0:T(8,128)(2,1)S(1)} %bitcast.2), channel_id=1, source_target_pairs={{8,0},{16,8},{24,16},{32,24},{40,32},{48,40},{56,48},{64,56},{72,6... | collective-permute-start | bytes 589832 | tf_op jit(solution)/shard_map/ppermute | solution.py:168
  45.2 0.9 %copy-start.3 = (s32[384,32]{1,0:T(8,128)S(1)}, s32[384,32]{1,0:T(8,128)}, u32[]{:S(2)}) copy-start(s32[384,32]{1,0:T(8,128)} %copy.13.leaf_list_ref) | copy-start | bytes 147460
  46.2 1.2 %copy-start.6 = (bf16[27,128,128]{2,1,0:T(8,128)(2,1)S(1)}, bf16[27,128,128]{2,1,0:T(8,128)(2,1)}, u32[]{:S(2)}) copy-start(bf16[27,128,128]{2,1,0:T(8,128)(2,1)} %near_ref.1) | copy-start | bytes 2654212

commit v2 on v1

--- a/solution.py
+++ b/solution.py
@@ -18,45 +18,47 @@
 
 
 def refine_rows(payload, joined):
-    span = joined.shape[1] // 4
+    span = joined.shape[0] // 4
     values = payload[:span, :].astype(F32)
     kind = payload[span : span + 1, :].astype(F32)
     spread = jnp.concatenate([jnp.where(kind == k, values, 0.0) for k in range(4)], axis=0)
-    return dot(jnp.transpose(spread).astype(BF16), joined, NT).astype(BF16)
-
-
-def join_tiles(tiles_ref):
-    return jnp.concatenate([tiles_ref[k] for k in range(4)], axis=1)
-
-
-def upward_kernel(payload_ref, tiles_ref, p2m_ref, m2m_ref, out_ref, mult_ref):
+    return dot(jnp.transpose(spread).astype(BF16), joined).astype(BF16)
+
+
+def upward_kernel(
+    dual_ref, select_ref, joined_ref, p2m_ref, m2m_ref, payload_ref, out_ref, table_ref, product, refined
+):
     copies, coarse, _ = out_ref.shape
-    order = p2m_ref.shape[0]
-    refined = refine_rows(payload_ref[...], join_tiles(tiles_ref))
-    mult = dot(refined, p2m_ref[...], NT).astype(BF16).astype(F32)
-    mult_ref[0] = mult[:, :128]
-    mult_ref[1, :, : order - 128] = mult[:, 128:]
+    order, width = p2m_ref.shape
+    span = dual_ref.shape[0]
+    payload_ref[:span] = dual_ref[...]
+    payload_ref[span:] = jnp.broadcast_to(select_ref[...], (8, select_ref.shape[1])).astype(F32).astype(BF16)
+    product[...] = dot(m2m_ref[...], p2m_ref[...])
+    refined[...] = refine_rows(payload_ref[...], joined_ref[...]).astype(F32)
     total = jnp.zeros((coarse, order), F32)
-    for j in range(8):
-        rows = [mult_ref[half, pl.ds(j, coarse, stride=8), :] for half in range(2)]
-        rows = jnp.concatenate(rows, axis=1)[:, :order].astype(BF16)
-        total = total + dot(rows, m2m_ref[j], NT)
+    for j in range(0, 8, 2):
+        tables, rows = [], []
+        for i in (j, j + 1):
+            table = product[pl.ds(i, order, stride=8), :].astype(BF16)
+            table_ref[i, :order] = table
+            tables.append(table)
+            rows.append(refined[pl.ds(i, coarse, stride=8), :].astype(BF16))
+        total = total + dot(jnp.concatenate(rows, axis=1), jnp.concatenate(tables, axis=1), NT)
     out_ref[...] = jnp.zeros_like(out_ref)
     for d in range(copies):
         out_ref[d, :, :order] = total.astype(BF16)
 
 
 def near_leaf_kernel(
-    own_ref, low_ref, high_ref, near_list_ref, leaf_list_ref, tiles_ref, near_ref, m2l_ref, p2m_ref,
-    near_out, leaf_out, window, tail, lists, near_tab, leaf_tab, hot,
+    own_ref, low_ref, high_ref, near_list_ref, leaf_list_ref, joined_ref, near_ref, m2l_ref, p2m_ref,
+    near_out, leaf_out, window, tail, lists, near_tab, leaf_tab, hot, product,
 ):
     boxes = own_ref.shape[1]
     order, width = p2m_ref.shape
-    n_near, n_leaf = near_list_ref.shape[1], leaf_list_ref.shape[1]
+    n_near, n_leaf = near_list_ref.shape[0], leaf_list_ref.shape[0]
     near_groups, leaf_groups = -(-n_near // 4), -(-n_leaf // 4)
-    joined = join_tiles(tiles_ref)
     rows = jnp.concatenate(
-        [refine_rows(ref[...], joined) for ref in (low_ref, own_ref, high_ref)], axis=0
+        [refine_rows(ref[...], joined_ref[...]) for ref in (low_ref, own_ref, high_ref)], axis=0
     )
     for b in range(4):
         window[:, b * width : (b + 1) * width] = rows[b * 256 : (b + 1) * 256]
@@ -66,13 +68,16 @@
     near_tab[...] = jnp.zeros_like(near_tab)
     for k in range(n_near):
         near_tab[k // 4, :, (k % 4) * width : (k % 4 + 1) * width] = near_ref[k]
+    product[...] = dot(m2l_ref[...], p2m_ref[...])
     for c in range(n_leaf):
-        leaf_tab[c // 4, :order, (c % 4) * width : (c % 4 + 1) * width] = dot(
-            m2l_ref[c], p2m_ref[...]
-        ).astype(BF16)
-    lists[...] = jnp.full_like(lists, -1)
-    lists[0, :, :n_near] = near_list_ref[...]
-    lists[1, :, :n_leaf] = leaf_list_ref[...]
+        leaf_tab[c // 4, :order, (c % 4) * width : (c % 4 + 1) * width] = product[
+            pl.ds(c, order, stride=n_leaf), :
+        ].astype(BF16)
+    for at, ref in ((0, near_list_ref), (1, leaf_list_ref)):
+        padded = jnp.concatenate(
+            [ref[...], jnp.full((128 - ref.shape[0], boxes), -1, jnp.int32)], axis=0
+        )
+        lists[at] = jnp.transpose(padded)
     near_out[...] = jnp.zeros_like(near_out)
     leaf_out[...] = jnp.zeros_like(leaf_out)
     spot = lax.broadcasted_iota(jnp.int32, (boxes, 256), 1)
@@ -116,14 +121,23 @@
     lax.fori_loop(0, leaf_groups, leaf_step, 0)
 
 
+def table_kernel(m2l_ref, out_ref, wide):
+    classes, order, _ = out_ref.shape
+    wide[0] = m2l_ref[:, :128].astype(F32)
+    wide[1, :, : order - 128] = m2l_ref[:, 128:].astype(F32)
+    for c in range(classes):
+        rows = [wide[half, pl.ds(c, order, stride=classes), :] for half in range(2)]
+        out_ref[c] = jnp.concatenate(rows, axis=1)[:, :order].astype(BF16)
+
+
 def downward_kernel(
     near_part_ref, leaf_local_ref, slab_ref, low_ref, high_ref, list_ref, payload_ref,
-    tiles_ref, p2m_ref, m2m_ref, m2l_ref, out_ref, down,
+    joined_ref, p2m_ref, table_ref, m2l_ref, out_ref, down,
 ):
     order = p2m_ref.shape[0]
-    coarse, classes = list_ref.shape
+    classes, coarse = list_ref.shape
     span = out_ref.shape[0]
-    index = list_ref[...]
+    index = jnp.transpose(list_ref[...])
     window = jnp.concatenate([low_ref[...], slab_ref[...], high_ref[...]], axis=0)
     spot = lax.broadcasted_iota(jnp.int32, (coarse, window.shape[0]), 1)
     hot = jnp.concatenate(
@@ -135,13 +149,10 @@
         total = total + dot(picked[c * coarse : (c + 1) * coarse, :order], m2l_ref[c], NT)
     local = total.astype(BF16)
     for j in range(8):
-        part = dot(local, m2m_ref[j])
-        down[0, pl.ds(j, coarse, stride=8), :] = part[:, :128]
-        down[1, pl.ds(j, coarse, stride=8), : order - 128] = part[:, 128:]
-    expansion = jnp.concatenate([down[0], down[1]], axis=1)[:, :order]
-    expansion = (leaf_local_ref[:, :order] + expansion).astype(BF16)
-    field = (near_part_ref[...] + dot(expansion, p2m_ref[...])).astype(BF16)
-    by_kind = dot(join_tiles(tiles_ref), field, (((0,), (1,)), ((), ())))
+        down[pl.ds(j, coarse, stride=8), :] = dot(local, table_ref[j, :order])
+    leaf = leaf_local_ref[:, :order].astype(BF16)
+    field = (near_part_ref[...] + dot(leaf, p2m_ref[...]) + down[...]).astype(BF16)
+    by_kind = dot(joined_ref[...], field, NT)
     kind = payload_ref[span : span + 1, :].astype(F32)
     tested = jnp.zeros(out_ref.shape, F32)
     for k in range(4):
@@ -176,17 +187,23 @@
     order, width = p2m.shape
     coarse = boxes // 8
     subs = lax.axis_size("sub")
-    kinds = jnp.broadcast_to(refine_select[None, :], (8, boxes)).astype(BF16)
-    payload = jnp.concatenate([dual_coeffs, kinds], axis=0)
+    joined = jnp.transpose(refine_tiles, (0, 2, 1)).reshape(4 * span, width)
+    m2m_rows = jnp.transpose(m2m, (1, 0, 2)).reshape(-1, order)
+    leaf_rows = jnp.transpose(leaf_m2l, (1, 0, 2)).reshape(-1, order)
+    coarse_rows = jnp.transpose(coarse_m2l, (1, 0, 2)).reshape(-1, order)
+    payload, mine, table = call(
+        upward_kernel,
+        (
+            jax.ShapeDtypeStruct((span + 8, boxes), BF16),
+            jax.ShapeDtypeStruct((subs, coarse, 256), BF16),
+            jax.ShapeDtypeStruct((8, 176, width), BF16),
+        ),
+        [pltpu.VMEM((8 * order, width), F32), pltpu.VMEM((boxes, width), F32)],
+        (dual_coeffs, refine_select.reshape(1, boxes), joined, p2m, m2m_rows),
+        100_000_000, 1.0,
+    )
     low = shifted(payload, ("grp", "sub"), 1)
     high = shifted(payload, ("grp", "sub"), -1)
-    mine = call(
-        upward_kernel,
-        jax.ShapeDtypeStruct((subs, coarse, 256), BF16),
-        [pltpu.VMEM((2, boxes, 128), F32)],
-        (payload, refine_tiles, p2m, m2m),
-        100_000_000, 1.0,
-    )
     slab = lax.all_to_all(mine, "sub", 0, 0).reshape(subs * coarse, 256)
     near_part, leaf_local = call(
         near_leaf_kernel,
@@ -198,19 +215,27 @@
             pltpu.VMEM((7, width, 4 * width), BF16),
             pltpu.VMEM((8, 176, 4 * width), BF16),
             pltpu.VMEM((4 * boxes, 256), BF16),
+            pltpu.VMEM((32 * order, width), F32),
         ],
-        (payload, low, high, near_list, leaf_list, refine_tiles, near_tiles, leaf_m2l, p2m),
+        (payload, low, high, near_list.T, leaf_list.T, joined, near_tiles, leaf_rows, p2m),
         10_000_000_000, 5.0,
     )
     slab_low = shifted(slab, "grp", 1)
     slab_high = shifted(slab, "grp", -1)
+    coarse_table = call(
+        table_kernel,
+        jax.ShapeDtypeStruct(coarse_m2l.shape, BF16),
+        [pltpu.VMEM((2, 16 * order, 128), F32)],
+        (coarse_rows,),
+        100_000_000, 3.0,
+    )
     return call(
         downward_kernel,
         jax.ShapeDtypeStruct((span, boxes), BF16),
-        [pltpu.VMEM((2, boxes, 128), F32)],
+        [pltpu.VMEM((boxes, width), F32)],
         (
-            near_part, leaf_local, slab, slab_low, slab_high, coarse_list, payload, refine_tiles, p2m,
-            m2m, coarse_m2l,
+            near_part, leaf_local, slab, slab_low, slab_high, coarse_list.T, payload, joined, p2m,
+            table, coarse_table,
         ),
         1_000_000_000, 3.0,
     )

time: 70.4 us -> 62.5 us (0.89)
  the two profiles are of different devices: /device:TPU:6 before, /device:TPU:62 now
where the time goes in v2:
time: 62.5 us; the launch traced here: 61.9 us
  starting transfers between devices  28.8 us (46%)
  Pallas kernels  25.7 us (41%)
  local copies, waits for them, and re-layouts  7.2 us (12%)
    pallas_call x4, Pallas kernels, call(): pl.pallas_call(kernel, out_shape=outs, in_specs=[pl.BlockSpec(memory_spac...  25.7 us
    ppermute x4, starting transfers between devices, shifted(): lax.ppermute(block, axis, [(i, i + step) for i in range(count) if 0 <= i...  21.8 us
    all_to_all x1, starting transfers between devices, body(): slab = lax.all_to_all(mine, 'sub', 0, 0).reshape(subs * coarse, 256)  7.01 us
    unnamed x24, local copies, waits for them, and re-layouts  6.52 us
  transfers between devices with their start and end apart: 5, of which 0 were waited for; matrix products, arithmetic and copies ran while one was open for 0% of the time, Pallas kernels for 34%

profile of v2, /device:TPU:62, one launch (start us, length us, event | category | flops | bytes accessed | tf_op | source)
XLA Modules:
  0.0 61.9 jit_solution(11362840783462171902)
XLA Ops:
  0.0 0.7 %reshape.18.select_ref = s32[1,384]{1,0:T(1,128)S(1)} reshape(s32[384]{0:T(512)} %param.12) | data formatting | bytes 3072 | tf_op jit(solution)/shard_map/reshape | solution.py:202
  0.7 1.1 %copy-done.1 = bf16[8,169,169]{2,0,1:T(8,128)(2,1)S(1)} copy-done((bf16[8,169,169]{2,0,1:T(8,128)(2,1)S(1)}, bf16[8,169,169]{2,0,1:T(8,128)(2,1)}, u32[]{:S(2)}) %copy-start.1) | copy-done | bytes 457000
  1.8 0.8 %copy-done.2 = bf16[169,128]{1,0:T(8,128)(2,1)S(1)} copy-done((bf16[169,128]{1,0:T(8,128)(2,1)S(1)}, bf16[169,128]{1,0:T(8,128)(2,1)}, u32[]{:S(2)}) %copy-start.2) | copy-done | bytes 43288
  2.6 0.8 %copy-done.4 = bf16[4,128,32]{1,2,0:T(8,128)(2,1)S(1)} copy-done((bf16[4,128,32]{1,2,0:T(8,128)(2,1)S(1)}, bf16[4,128,32]{1,2,0:T(8,128)(2,1)}, u32[]{:S(2)}) %copy-start.4) | copy-done | bytes 32792
  3.3 0.7 %copy-done.6 = bf16[32,384]{1,0:T(8,128)(2,1)S(1)} copy-done((bf16[32,384]{1,0:T(8,128)(2,1)S(1)}, bf16[32,384]{1,0:T(8,128)(2,1)}, u32[]{:S(2)}) %copy-start.6) | copy-done | bytes 24600
  4.1 1.4 %shard_map.109 = (bf16[40,384]{1,0:T(8,128)(2,1)S(1)}, bf16[8,48,256]{2,1,0:T(8,128)(2,1)}, bf16[8,176,128]{2,1,0:T(8,128)(2,1)S(1)}) custom-call(bf16[32,384]{1,0:T(8,128)(2,1)S(1)} %copy-done.6, s32[1,384]{1,0:T(1,128)S(1)} %reshape.18.select_ref, bf16[128,128]{1,0:T(8,128)(2,1)S(1)} %bitcast.21, bf16[169,128]{1,0:T(8,128)(2,1)S(1)} %copy-done.2, ...), custom_call_target="tpu_custom_call" | custom-call | flops 100000000 | bytes 1000000 | tf_op jit(solution)/shard_map/pallas_call | solution.py:164
  5.5 7.0 %all-to-all-start = ((bf16[8,48,256]{2,1,0:T(8,128)(2,1)}), bf16[8,48,256]{2,1,0:T(8,128)(2,1)S(1)}, u32[]{:S(2)}, u32[]{:S(2)}) async-start(bf16[8,48,256]{2,1,0:T(8,128)(2,1)} %get-tuple-element.13), calls=%async_computation | async-start | bytes 393216 | tf_op jit(solution)/shard_map/all_to_all | solution.py:207
  12.5 3.4 %collective-permute-start.1 = (bf16[40,384]{1,0:T(8,128)(2,1)S(1)}, bf16[40,384]{1,0:T(8,128)(2,1)S(1)}, u32[]{:S(2)}, u32[]{:S(2)}) collective-permute-start(bf16[40,384]{1,0:T(8,128)(2,1)S(1)} %get-tuple-element.10.own_ref.payload_ref), channel_id=1, source_target_pairs={{1,0},{2,1},{3,2},{4,3},{5,4},{6,5},{7,6},{8,7},{9,8},{10,9},{11,1... | collective-permute-start | bytes 92168 | tf_op jit(solution)/shard_map/ppermute | solution.py:179
  15.9 3.4 %collective-permute-start = (bf16[40,384]{1,0:T(8,128)(2,1)S(1)}, bf16[40,384]{1,0:T(8,128)(2,1)S(1)}, u32[]{:S(2)}, u32[]{:S(2)}) collective-permute-start(bf16[40,384]{1,0:T(8,128)(2,1)S(1)} %get-tuple-element.10.own_ref.payload_ref), channel_id=1, source_target_pairs={{0,1},{1,2},{2,3},{3,4},{4,5},{5,6},{6,7},{7,8},{8,9},{9,10},{10,1... | collective-permute-start | bytes 92168 | tf_op jit(solution)/shard_map/ppermute | solution.py:179
  19.3 0.0 copy-start
  19.3 1.3 %copy-done = bf16[16,169,169]{2,0,1:T(8,128)(2,1)S(1)} copy-done((bf16[16,169,169]{2,0,1:T(8,128)(2,1)S(1)}, bf16[16,169,169]{2,0,1:T(8,128)(2,1)}, u32[]{:S(2)}) %copy-start) | copy-done | bytes 913976
  20.7 1.5 %shard_map.111.m2l_ref = bf16[16,169,169]{2,1,0:T(8,128)(2,1)S(1)} custom-call(bf16[2704,169]{1,0:T(8,128)(2,1)S(1)} %bitcast.16), custom_call_target="tpu_custom_call" | custom-call | flops 100000000 | bytes 3000000 | tf_op jit(solution)/shard_map/pallas_call | solution.py:164
  22.1 0.0 all-to-all-done
  22.1 13.1 %collective-permute-start.3 = (bf16[384,256]{1,0:T(8,128)(2,1)S(1)}, bf16[384,256]{1,0:T(8,128)(2,1)S(1)}, u32[]{:S(2)}, u32[]{:S(2)}) collective-permute-start(bf16[384,256]{1,0:T(8,128)(2,1)S(1)} %bitcast.18), channel_id=1, source_target_pairs={{8,0},{16,8},{24,16},{32,24},{40,32},{48,40},{56,48},{64,56},{72,6... | collective-permute-start | bytes 589832 | tf_op jit(solution)/shard_map/ppermute | solution.py:179
  35.2 1.9 %collective-permute-start.2 = (bf16[384,256]{1,0:T(8,128)(2,1)S(1)}, bf16[384,256]{1,0:T(8,128)(2,1)S(1)}, u32[]{:S(2)}, u32[]{:S(2)}) collective-permute-start(bf16[384,256]{1,0:T(8,128)(2,1)S(1)} %bitcast.19), channel_id=1, source_target_pairs={{0,8},{8,16},{16,24},{24,32},{32,40},{40,48},{48,56},{56,64},{64,7... | collective-permute-start | bytes 589832 | tf_op jit(solution)/shard_map/ppermute | solution.py:179
  37.2 0.0 collective-permute-done.1.high_ref
  37.2 0.0 collective-permute-done.low_ref
  37.2 0.0 copy-done.8
  37.2 0.0 copy-start.7
  37.3 1.8 %copy-done.7 = bf16[32,169,169]{2,0,1:T(8,128)(2,1)S(1)} copy-done((bf16[32,169,169]{2,0,1:T(8,128)(2,1)S(1)}, bf16[32,169,169]{2,0,1:T(8,128)(2,1)}, u32[]{:S(2)}) %copy-start.7) | copy-done | bytes 1827928
  39.0 19.7 %shard_map.110 = (f32[384,128]{1,0:T(8,128)S(1)}, f32[384,176]{1,0:T(8,128)S(1)}) custom-call(bf16[40,384]{1,0:T(8,128)(2,1)S(1)} %get-tuple-element.10.own_ref.payload_ref, bf16[40,384]{1,0:T(8,128)(2,1)S(1)} %collective-permute-done.low_ref, bf16[40,384]{1,0:T(8,128)(2,1)S(1)} %collective-permute-done.1.high_ref, s32[27,384]{1,0:T(8,128)S(1)} %bitcast.25, ...), custom_call_target="tpu_custom_call" | custom-call | flops 10000000000 | bytes 5000000 | tf_op jit(solution)/shard_map/pallas_call | solution.py:164
  58.8 0.0 collective-permute-done.3.high_ref
  58.8 0.0 collective-permute-done.2.low_ref
  58.8 3.0 %shard_map.112 = bf16[32,384]{1,0:T(8,128)(2,1)} custom-call(f32[384,128]{1,0:T(8,128)S(1)} %get-tuple-element.11.near_part_ref, f32[384,176]{1,0:T(8,128)S(1)} %get-tuple-element.12.leaf_local_ref, bf16[384,256]{1,0:T(8,128)(2,1)S(1)} %bitcast.20, bf16[384,256]{1,0:T(8,128)(2,1)S(1)} %collective-permute-done.2.low_ref, ...), custom_call_target="tpu_custom_call" | custom-call | flops 1000000000 | bytes 3000000 | tf_op jit(solution)/shard_map/pallas_call | solution.py:164
  (15 shorter events, 0.0 us)
Async XLA Ops:
  0.7 1.1 %copy-start.1 = (bf16[8,169,169]{2,0,1:T(8,128)(2,1)S(1)}, bf16[8,169,169]{2,0,1:T(8,128)(2,1)}, u32[]{:S(2)}) copy-start(bf16[8,169,169]{2,0,1:T(8,128)(2,1)} %param.18) | copy-start | bytes 1370932
  1.8 0.8 %copy-start.2 = (bf16[169,128]{1,0:T(8,128)(2,1)S(1)}, bf16[169,128]{1,0:T(8,128)(2,1)}, u32[]{:S(2)}) copy-start(bf16[169,128]{1,0:T(8,128)(2,1)} %p2m_ref.5) | copy-start | bytes 129796
  2.6 0.8 %copy-start.4 = (bf16[4,128,32]{1,2,0:T(8,128)(2,1)S(1)}, bf16[4,128,32]{1,2,0:T(8,128)(2,1)}, u32[]{:S(2)}) copy-start(bf16[4,128,32]{1,2,0:T(8,128)(2,1)} %param.13) | copy-start | bytes 98308
  3.3 0.7 %copy-start.6 = (bf16[32,384]{1,0:T(8,128)(2,1)S(1)}, bf16[32,384]{1,0:T(8,128)(2,1)}, u32[]{:S(2)}) copy-start(bf16[32,384]{1,0:T(8,128)(2,1)} %dual_ref.1) | copy-start | bytes 73732
  4.1 33.1 %copy-start.8 = (bf16[27,128,128]{2,1,0:T(8,128)(2,1)S(1)}, bf16[27,128,128]{2,1,0:T(8,128)(2,1)}, u32[]{:S(2)}) copy-start(bf16[27,128,128]{2,1,0:T(8,128)(2,1)} %near_ref.1) | copy-start | bytes 2654212
  5.5 31.7 %copy-start.3 = (bf16[169,128]{1,0:T(8,128)(2,1)S(1)}, bf16[169,128]{1,0:T(8,128)(2,1)}, u32[]{:S(2)}) copy-start(bf16[169,128]{1,0:T(8,128)(2,1)} %p2m_ref.5) | copy-start | bytes 129796
  5.5 31.7 %copy-start.5 = (bf16[4,128,32]{1,2,0:T(8,128)(2,1)S(1)}, bf16[4,128,32]{1,2,0:T(8,128)(2,1)}, u32[]{:S(2)}) copy-start(bf16[4,128,32]{1,2,0:T(8,128)(2,1)} %param.13) | copy-start | bytes 98308
  5.5 31.7 %copy-start.9 = (s32[384,27]{0,1:T(8,128)S(1)}, s32[384,27]{0,1:T(8,128)}, u32[]{:S(2)}) copy-start(s32[384,27]{0,1:T(8,128)} %param.14) | copy-start | bytes 124420
  5.5 31.7 %copy-start.10 = (s32[384,32]{0,1:T(8,128)S(1)}, s32[384,32]{0,1:T(8,128)}, u32[]{:S(2)}) copy-start(s32[384,32]{0,1:T(8,128)} %param.16) | copy-start | bytes 147460
  5.5 16.6 %all-to-all-start = ((bf16[8,48,256]{2,1,0:T(8,128)(2,1)}), bf16[8,48,256]{2,1,0:T(8,128)(2,1)S(1)}, u32[]{:S(2)}, u32[]{:S(2)}) async-start(bf16[8,48,256]{2,1,0:T(8,128)(2,1)} %get-tuple-element.13), calls=%async_computation | async-start | bytes 393216 | tf_op jit(solution)/shard_map/all_to_all | solution.py:207
  12.5 24.7 %collective-permute-start.1 = (bf16[40,384]{1,0:T(8,128)(2,1)S(1)}, bf16[40,384]{1,0:T(8,128)(2,1)S(1)}, u32[]{:S(2)}, u32[]{:S(2)}) collective-permute-start(bf16[40,384]{1,0:T(8,128)(2,1)S(1)} %get-tuple-element.10.own_ref.payload_ref), channel_id=1, source_target_pairs={{1,0},{2,1},{3,2},{4,3},{5,4},{6,5},{7,6},{8,7},{9,8},{10,9},{11,1... | collective-permute-start | bytes 92168 | tf_op jit(solution)/shard_map/ppermute | solution.py:179
  15.9 21.3 %collective-permute-start = (bf16[40,384]{1,0:T(8,128)(2,1)S(1)}, bf16[40,384]{1,0:T(8,128)(2,1)S(1)}, u32[]{:S(2)}, u32[]{:S(2)}) collective-permute-start(bf16[40,384]{1,0:T(8,128)(2,1)S(1)} %get-tuple-element.10.own_ref.payload_ref), channel_id=1, source_target_pairs={{0,1},{1,2},{2,3},{3,4},{4,5},{5,6},{6,7},{7,8},{8,9},{9,10},{10,1... | collective-permute-start | bytes 92168 | tf_op jit(solution)/shard_map/ppermute | solution.py:179
  19.3 1.3 %copy-start = (bf16[16,169,169]{2,0,1:T(8,128)(2,1)S(1)}, bf16[16,169,169]{2,0,1:T(8,128)(2,1)}, u32[]{:S(2)}) copy-start(bf16[16,169,169]{2,0,1:T(8,128)(2,1)} %param.21) | copy-start | bytes 2741860
  22.1 36.6 %collective-permute-start.3 = (bf16[384,256]{1,0:T(8,128)(2,1)S(1)}, bf16[384,256]{1,0:T(8,128)(2,1)S(1)}, u32[]{:S(2)}, u32[]{:S(2)}) collective-permute-start(bf16[384,256]{1,0:T(8,128)(2,1)S(1)} %bitcast.18), channel_id=1, source_target_pairs={{8,0},{16,8},{24,16},{32,24},{40,32},{48,40},{56,48},{64,56},{72,6... | collective-permute-start | bytes 589832 | tf_op jit(solution)/shard_map/ppermute | solution.py:179
  35.2 23.5 %collective-permute-start.2 = (bf16[384,256]{1,0:T(8,128)(2,1)S(1)}, bf16[384,256]{1,0:T(8,128)(2,1)S(1)}, u32[]{:S(2)}, u32[]{:S(2)}) collective-permute-start(bf16[384,256]{1,0:T(8,128)(2,1)S(1)} %bitcast.19), channel_id=1, source_target_pairs={{0,8},{8,16},{16,24},{24,32},{32,40},{40,48},{48,56},{56,64},{64,7... | collective-permute-start | bytes 589832 | tf_op jit(solution)/shard_map/ppermute | solution.py:179
  37.2 1.8 %copy-start.7 = (bf16[32,169,169]{2,0,1:T(8,128)(2,1)S(1)}, bf16[32,169,169]{2,0,1:T(8,128)(2,1)}, u32[]{:S(2)}) copy-start(bf16[32,169,169]{2,0,1:T(8,128)(2,1)} %param.19) | copy-start | bytes 5483716
  39.0 19.8 %copy-start.11 = (s32[48,16]{0,1:T(8,128)S(1)}, s32[48,16]{0,1:T(8,128)}, u32[]{:S(2)}) copy-start(s32[48,16]{0,1:T(8,128)} %param.20) | copy-start | bytes 9220

commit v3 on v2

v3 whole, which is shorter than its diff:
```python
import jax
import jax.numpy as jnp
from jax import lax
from jax.experimental import pallas as pl
from jax.experimental.pallas import tpu as pltpu
from jax.sharding import PartitionSpec as P

GROUP = 8
F32 = jnp.float32
BF16 = jnp.bfloat16
NT = (((1,), (1,)), ((), ()))
TN = (((0,), (0,)), ((), ()))


def dot(a, b, dims=(((1,), (0,)), ((), ()))):
    return lax.dot_general(a, b, dims, preferred_element_type=F32)


def refine_rows(payload, joined):
    span = joined.shape[0] // 4
    values = payload[:span, :].astype(F32)
    kind = payload[span : span + 1, :].astype(F32)
    spread = jnp.concatenate([jnp.where(kind == k, values, 0.0) for k in range(4)], axis=0)
    return dot(jnp.transpose(spread).astype(BF16), joined).astype(BF16)


def fetch(sources, targets, sems):
    copies = [
        pltpu.make_async_copy(source, target, sems.at[i])
        for i, (source, target) in enumerate(zip(sources, targets))
    ]
    for copy in copies:
        copy.start()
    return copies


def upward_kernel(
    dual_hbm, select_ref, joined_hbm, p2m_hbm, m2m_hbm, payload_ref, out_ref, table_ref,
    dual, joined, p2m, m2m, product, refined, sems,
):
    copies = fetch((dual_hbm, joined_hbm, p2m_hbm, m2m_hbm), (dual, joined, p2m, m2m), sems)
    subs, coarse, _ = out_ref.shape
    order, width = p2m.shape
    span, boxes = dual.shape
    payload_ref[span:] = jnp.broadcast_to(select_ref[...], (8, boxes)).astype(F32).astype(BF16)
    out_ref[...] = jnp.zeros_like(out_ref)
    for copy in copies:
        copy.wait()
    payload_ref[:span] = dual[...]
    product[...] = dot(m2m[...], p2m[...])
    refined[...] = refine_rows(payload_ref[...], joined[...]).astype(F32)
    total = jnp.zeros((coarse, order), F32)
    for j in range(0, 8, 2):
        tables, rows = [], []
        for i in (j, j + 1):
            table = product[pl.ds(i, order, stride=8), :].astype(BF16)
            table_ref[i, :order] = table
            tables.append(table)
            rows.append(refined[pl.ds(i, coarse, stride=8), :].astype(BF16))
        total = total + dot(jnp.concatenate(rows, axis=1), jnp.concatenate(tables, axis=1), NT)
    for d in range(subs):
        out_ref[d, :, :order] = total.astype(BF16)


def near_leaf_kernel(
    own_ref, low_ref, high_ref, near_list_ref, leaf_list_ref, joined_ref, near_ref, m2l_hbm, p2m_ref,
    field_ref, window, near_index, leaf_index, near_tab, leaf_tab, m2l, product, leaf_local, sems,
):
    copies = fetch((m2l_hbm,), (m2l,), sems)
    depth, boxes = own_ref.shape
    order, width = p2m_ref.shape
    span = depth - 8
    n_near, n_leaf = near_list_ref.shape[0], leaf_list_ref.shape[0]
    whole = jnp.concatenate(
        [low_ref[...], own_ref[...], high_ref[...], jnp.zeros((depth, 128), BF16)], axis=1
    ).astype(F32)
    blocks = whole.shape[1] // 256
    window[...] = jnp.concatenate(
        [whole[:, b * 256 : (b + 1) * 256] for b in range(blocks)], axis=0
    ).astype(BF16)
    spot = lax.broadcasted_iota(jnp.int32, (256, boxes), 0).astype(BF16)

    def hot_of(index):
        low = (index & 255).astype(F32).astype(BF16)
        return jnp.where(low == spot, jnp.array(1.0, BF16), jnp.array(0.0, BF16))

    def expand(index, got):
        block = index >> 8
        value = jnp.zeros((depth, boxes), F32)
        for b in range(blocks):
            value = jnp.where(block == b, got[b * depth : (b + 1) * depth], value)
        kind = value[span : span + 1]
        return [jnp.where(kind == k, value[:span], 0.0) for k in range(4)]

    def group(rows, table, out):
        index = [rows[c : c + 1, :] for c in range(GROUP)]
        got = dot(window[...], jnp.concatenate([hot_of(i) for i in index], axis=1))
        parts = []
        for c in range(GROUP):
            parts += expand(index[c], got[:, c * boxes : (c + 1) * boxes])
        out[...] += dot(table, jnp.concatenate(parts, axis=0).astype(BF16))

    joined = joined_ref[...]
    near_tab[...] = jnp.zeros_like(near_tab)
    near_index[...] = jnp.full_like(near_index, -1)
    for k in range(n_near):
        at = slice((k % GROUP) * width, (k % GROUP + 1) * width)
        near_tab[k // GROUP, :, at] = dot(near_ref[k], joined, NT).astype(BF16)
        near_index[k // GROUP, k % GROUP : k % GROUP + 1] = near_list_ref[k : k + 1]
    field_ref[...] = jnp.zeros_like(field_ref)
    for g in range(near_index.shape[0]):
        group(near_index[g], near_tab[g], field_ref)

    spread = dot(p2m_ref[...], joined, NT).astype(BF16)
    for copy in copies:
        copy.wait()
    product[...] = dot(m2l[...], spread)
    for c in range(n_leaf):
        at = slice((c % GROUP) * width, (c % GROUP + 1) * width)
        leaf_tab[c // GROUP, :order, at] = product[pl.ds(c, order, stride=n_leaf), :].astype(BF16)
        leaf_index[c // GROUP, c % GROUP : c % GROUP + 1] = leaf_list_ref[c : c + 1]
    leaf_local[...] = jnp.zeros_like(leaf_local)
    for g in range(leaf_index.shape[0]):
        group(leaf_index[g], leaf_tab[g], leaf_local)
    field_ref[...] += dot(p2m_ref[...], leaf_local[:order].astype(BF16), TN)


def table_kernel(m2l_ref, out_ref, wide):
    classes, order, _ = out_ref.shape
    wide[0] = m2l_ref[:, :128].astype(F32)
    wide[1, :, : order - 128] = m2l_ref[:, 128:].astype(F32)
    for c in range(classes):
        rows = [wide[half, pl.ds(c, order, stride=classes), :] for half in range(2)]
        out_ref[c] = jnp.concatenate(rows, axis=1)[:, :order].astype(BF16)


def downward_kernel(
    field_ref, slab_ref, low_ref, high_ref, list_ref, payload_ref, joined_ref, table_ref, m2l_ref,
    out_ref, down,
):
    order = m2l_ref.shape[1]
    classes, coarse = list_ref.shape
    span = out_ref.shape[0]
    index = jnp.transpose(list_ref[...])
    window = jnp.concatenate([low_ref[...], slab_ref[...], high_ref[...]], axis=0)
    spot = lax.broadcasted_iota(jnp.int32, (coarse, window.shape[0]), 1)
    hot = jnp.concatenate(
        [jnp.where(index[:, c : c + 1] == spot, 1.0, 0.0).astype(BF16) for c in range(classes)], axis=0
    )
    picked = dot(hot, window).astype(BF16)
    total = jnp.zeros((coarse, order), F32)
    for c in range(classes):
        total = total + dot(picked[c * coarse : (c + 1) * coarse, :order], m2l_ref[c], NT)
    local = total.astype(BF16)
    for j in range(8):
        down[pl.ds(j, coarse, stride=8), :] = dot(local, table_ref[j, :order])
    field = (field_ref[...] + jnp.transpose(down[...])).astype(BF16)
    by_kind = dot(joined_ref[...], field)
    kind = payload_ref[span : span + 1, :].astype(F32)
    tested = jnp.zeros(out_ref.shape, F32)
    for k in range(4):
        tested = jnp.where(kind == k, by_kind[k * span : (k + 1) * span], tested)
    out_ref[...] = tested.astype(BF16)


def call(kernel, outs, scratch, args, flops, megabytes, in_hbm=()):
    return pl.pallas_call(
        kernel,
        out_shape=outs,
        in_specs=[
            pl.BlockSpec(memory_space=pltpu.HBM if i in in_hbm else pltpu.VMEM)
            for i in range(len(args))
        ],
        out_specs=jax.tree.map(lambda _: pl.BlockSpec(memory_space=pltpu.VMEM), outs),
        scratch_shapes=scratch,
        compiler_params=pltpu.CompilerParams(vmem_limit_bytes=40 * 1024 * 1024),
        cost_estimate=pl.CostEstimate(
            flops=flops, bytes_accessed=int(megabytes * 1e6), transcendentals=0
        ),
    )(*args)


def shifted(block, axis, step):
    count = lax.axis_size(axis)
    return lax.ppermute(block, axis, [(i, i + step) for i in range(count) if 0 <= i + step < count])


def body(
    dual_coeffs, refine_select, refine_tiles, near_list, near_tiles, leaf_list, p2m, m2m, leaf_m2l,
    coarse_list, coarse_m2l,
):
    span, boxes = dual_coeffs.shape
    order, width = p2m.shape
    coarse = boxes // 8
    subs = lax.axis_size("sub")
    joined = jnp.transpose(refine_tiles, (0, 2, 1)).reshape(4 * span, width)
    m2m_rows = jnp.transpose(m2m, (1, 0, 2)).reshape(-1, order)
    leaf_rows = jnp.transpose(leaf_m2l, (1, 0, 2)).reshape(-1, order)
    coarse_rows = jnp.transpose(coarse_m2l, (1, 0, 2)).reshape(-1, order)
    payload, mine, table = call(
        upward_kernel,
        (
            jax.ShapeDtypeStruct((span + 8, boxes), BF16),
            jax.ShapeDtypeStruct((subs, coarse, 256), BF16),
            jax.ShapeDtypeStruct((8, 176, width), BF16),
        ),
        [pltpu.VMEM(a.shape, BF16) for a in (dual_coeffs, joined, p2m, m2m_rows)]
        + [
            pltpu.VMEM((8 * order, width), F32),
            pltpu.VMEM((boxes, width), F32),
            pltpu.SemaphoreType.DMA((4,)),
        ],
        (dual_coeffs, refine_select.reshape(1, boxes), joined, p2m, m2m_rows),
        100_000_000, 1.0, (0, 2, 3, 4),
    )
    low = shifted(payload, ("grp", "sub"), 1)
    high = shifted(payload, ("grp", "sub"), -1)
    slab = lax.all_to_all(mine, "sub", 0, 0).reshape(subs * coarse, 256)
    near_groups, leaf_groups = -(-near_tiles.shape[0] // GROUP), leaf_m2l.shape[0] // GROUP
    field = call(
        near_leaf_kernel,
        jax.ShapeDtypeStruct((width, boxes), F32),
        [
            pltpu.VMEM((5 * (span + 8), 256), BF16),
            pltpu.VMEM((near_groups, GROUP, boxes), jnp.int32),
            pltpu.VMEM((leaf_groups, GROUP, boxes), jnp.int32),
            pltpu.VMEM((near_groups, width, GROUP * width), BF16),
            pltpu.VMEM((leaf_groups, 176, GROUP * width), BF16),
            pltpu.VMEM(leaf_rows.shape, BF16),
            pltpu.VMEM((leaf_rows.shape[0], width), F32),
            pltpu.VMEM((176, boxes), F32),
            pltpu.SemaphoreType.DMA((1,)),
        ],
        (payload, low, high, near_list.T, leaf_list.T, joined, near_tiles, leaf_rows, p2m),
        5_000_000_000, 5.0, (7,),
    )
    slab_low = shifted(slab, "grp", 1)
    slab_high = shifted(slab, "grp", -1)
    coarse_table = call(
        table_kernel,
        jax.ShapeDtypeStruct(coarse_m2l.shape, BF16),
        [pltpu.VMEM((2, 16 * order, 128), F32)],
        (coarse_rows,),
        100_000_000, 3.0,
    )
    return call(
        downward_kernel,
        jax.ShapeDtypeStruct((span, boxes), BF16),
        [pltpu.VMEM((boxes, width), F32)],
        (
            field, slab, slab_low, slab_high, coarse_list.T, payload, joined, table, coarse_table,
        ),
        1_000_000_000, 3.0,
    )


def solution(mesh):
    placed = (
        P(None, ("grp", "sub")),
        P(("grp", "sub")),
        P(),
        P(("grp", "sub"), None),
        P(),
        P(("grp", "sub"), None),
        P(),
        P(),
        P(),
        P(("grp", "sub"), None),
        P(),
    )
    return jax.shard_map(
        body, mesh=mesh, in_specs=placed, out_specs=P(None, ("grp", "sub")), check_vma=False
    )
```

time: 62.5 us -> 51.8 us (0.83)
  Pallas kernels: 25.7 us -> 15 us
    pallas_call x4, Pallas kernels: 25.7 us -> 15 us  [call(): pl.pallas_call(kernel, out_shape=outs, in_specs=[pl.BlockSpec(memory_spac...]
  transfers between devices with their start and end apart: 5 -> 5, of which waited for: 0 -> 0; matrix products, arithmetic and copies ran while one was open for 0% -> 0% of each run, Pallas kernels for 34% -> 20%
where the time goes in v3:
time: 51.8 us; the launch traced here: 51.2 us
  starting transfers between devices  28.8 us (56%)
  Pallas kernels  15 us (29%)
  local copies, waits for them, and re-layouts  7.21 us (14%)
    ppermute x4, starting transfers between devices, shifted(): lax.ppermute(block, axis, [(i, i + step) for i in range(count) if 0 <= i...  21.8 us
    pallas_call x4, Pallas kernels, call(): pl.pallas_call(kernel, out_shape=outs, in_specs=[pl.BlockSpec(memory_spac...  15 us
    all_to_all x1, starting transfers between devices, body(): slab = lax.all_to_all(mine, 'sub', 0, 0).reshape(subs * coarse, 256)  7.01 us
    unnamed x24, local copies, waits for them, and re-layouts  6.53 us
  transfers between devices with their start and end apart: 5, of which 0 were waited for; matrix products, arithmetic and copies ran while one was open for 0% of the time, Pallas kernels for 20%

profile of v3, /device:TPU:62, one launch (start us, length us, event | category | flops | bytes accessed | tf_op | source)
XLA Modules:
  0.0 51.2 jit_solution(10699038229046656094)
XLA Ops:
  0.0 0.7 %reshape.18.select_ref = s32[1,384]{1,0:T(1,128)S(1)} reshape(s32[384]{0:T(512)} %param.12) | data formatting | bytes 3072 | tf_op jit(solution)/shard_map/reshape | solution.py:213
  0.7 1.1 %copy-done.1 = bf16[8,169,169]{2,0,1:T(8,128)(2,1)S(1)} copy-done((bf16[8,169,169]{2,0,1:T(8,128)(2,1)S(1)}, bf16[8,169,169]{2,0,1:T(8,128)(2,1)}, u32[]{:S(2)}) %copy-start.1) | copy-done | bytes 457000
  1.8 0.8 %copy-done.2 = bf16[169,128]{1,0:T(8,128)(2,1)S(1)} copy-done((bf16[169,128]{1,0:T(8,128)(2,1)S(1)}, bf16[169,128]{1,0:T(8,128)(2,1)}, u32[]{:S(2)}) %copy-start.2) | copy-done | bytes 43288
  2.6 0.8 %copy-done.4 = bf16[4,128,32]{1,2,0:T(8,128)(2,1)S(1)} copy-done((bf16[4,128,32]{1,2,0:T(8,128)(2,1)S(1)}, bf16[4,128,32]{1,2,0:T(8,128)(2,1)}, u32[]{:S(2)}) %copy-start.4) | copy-done | bytes 32792
  3.3 0.7 %copy-done.6 = bf16[32,384]{1,0:T(8,128)(2,1)S(1)} copy-done((bf16[32,384]{1,0:T(8,128)(2,1)S(1)}, bf16[32,384]{1,0:T(8,128)(2,1)}, u32[]{:S(2)}) %copy-start.6) | copy-done | bytes 24600
  4.1 1.9 %shard_map.109 = (bf16[40,384]{1,0:T(8,128)(2,1)S(1)}, bf16[8,48,256]{2,1,0:T(8,128)(2,1)}, bf16[8,176,128]{2,1,0:T(8,128)(2,1)S(1)}) custom-call(bf16[32,384]{1,0:T(8,128)(2,1)S(1)} %copy-done.6, s32[1,384]{1,0:T(1,128)S(1)} %reshape.18.select_ref, bf16[128,128]{1,0:T(8,128)(2,1)S(1)} %bitcast.21, bf16[169,128]{1,0:T(8,128)(2,1)S(1)} %copy-done.2, ...), custom_call_target="tpu_custom_call" | custom-call | flops 100000000 | bytes 1000000 | tf_op jit(solution)/shard_map/pallas_call | solution.py:167
  6.0 0.0 copy-start.3
  6.0 0.0 copy-start.5
  6.0 0.0 copy-start.9
  6.0 0.0 copy-start.10
  6.0 7.0 %all-to-all-start = ((bf16[8,48,256]{2,1,0:T(8,128)(2,1)}), bf16[8,48,256]{2,1,0:T(8,128)(2,1)S(1)}, u32[]{:S(2)}, u32[]{:S(2)}) async-start(bf16[8,48,256]{2,1,0:T(8,128)(2,1)} %get-tuple-element.9), calls=%async_computation | async-start | bytes 393216 | tf_op jit(solution)/shard_map/all_to_all | solution.py:218
  13.0 3.4 %collective-permute-start.1 = (bf16[40,384]{1,0:T(8,128)(2,1)S(1)}, bf16[40,384]{1,0:T(8,128)(2,1)S(1)}, u32[]{:S(2)}, u32[]{:S(2)}) collective-permute-start(bf16[40,384]{1,0:T(8,128)(2,1)S(1)} %get-tuple-element.8.own_ref.payload_ref), channel_id=1, source_target_pairs={{1,0},{2,1},{3,2},{4,3},{5,4},{6,5},{7,6},{8,7},{9,8},{10,9},{11,1... | collective-permute-start | bytes 92168 | tf_op jit(solution)/shard_map/ppermute | solution.py:185
  16.4 3.4 %collective-permute-start = (bf16[40,384]{1,0:T(8,128)(2,1)S(1)}, bf16[40,384]{1,0:T(8,128)(2,1)S(1)}, u32[]{:S(2)}, u32[]{:S(2)}) collective-permute-start(bf16[40,384]{1,0:T(8,128)(2,1)S(1)} %get-tuple-element.8.own_ref.payload_ref), channel_id=1, source_target_pairs={{0,1},{1,2},{2,3},{3,4},{4,5},{5,6},{6,7},{7,8},{8,9},{9,10},{10,1... | collective-permute-start | bytes 92168 | tf_op jit(solution)/shard_map/ppermute | solution.py:185
  19.8 0.0 copy-start
  19.8 1.3 %copy-done = bf16[16,169,169]{2,0,1:T(8,128)(2,1)S(1)} copy-done((bf16[16,169,169]{2,0,1:T(8,128)(2,1)S(1)}, bf16[16,169,169]{2,0,1:T(8,128)(2,1)}, u32[]{:S(2)}) %copy-start) | copy-done | bytes 913976
  21.1 1.5 %shard_map.111.m2l_ref = bf16[16,169,169]{2,1,0:T(8,128)(2,1)S(1)} custom-call(bf16[2704,169]{1,0:T(8,128)(2,1)S(1)} %bitcast.16), custom_call_target="tpu_custom_call" | custom-call | flops 100000000 | bytes 3000000 | tf_op jit(solution)/shard_map/pallas_call | solution.py:167
  22.6 13.1 %collective-permute-start.3 = (bf16[384,256]{1,0:T(8,128)(2,1)S(1)}, bf16[384,256]{1,0:T(8,128)(2,1)S(1)}, u32[]{:S(2)}, u32[]{:S(2)}) collective-permute-start(bf16[384,256]{1,0:T(8,128)(2,1)S(1)} %bitcast.18), channel_id=1, source_target_pairs={{8,0},{16,8},{24,16},{32,24},{40,32},{48,40},{56,48},{64,56},{72,6... | collective-permute-start | bytes 589832 | tf_op jit(solution)/shard_map/ppermute | solution.py:185
  35.7 1.9 %collective-permute-start.2 = (bf16[384,256]{1,0:T(8,128)(2,1)S(1)}, bf16[384,256]{1,0:T(8,128)(2,1)S(1)}, u32[]{:S(2)}, u32[]{:S(2)}) collective-permute-start(bf16[384,256]{1,0:T(8,128)(2,1)S(1)} %bitcast.19), channel_id=1, source_target_pairs={{0,8},{8,16},{16,24},{24,32},{32,40},{40,48},{48,56},{56,64},{64,7... | collective-permute-start | bytes 589832 | tf_op jit(solution)/shard_map/ppermute | solution.py:185
  37.6 0.0 collective-permute-done.1.high_ref
  37.7 0.0 copy-start.7
  37.7 1.8 %copy-done.7 = bf16[32,169,169]{2,0,1:T(8,128)(2,1)S(1)} copy-done((bf16[32,169,169]{2,0,1:T(8,128)(2,1)S(1)}, bf16[32,169,169]{2,0,1:T(8,128)(2,1)}, u32[]{:S(2)}) %copy-start.7) | copy-done | bytes 1827928
  39.5 8.6 %shard_map.110.field_ref = f32[128,384]{1,0:T(8,128)S(1)} custom-call(bf16[40,384]{1,0:T(8,128)(2,1)S(1)} %get-tuple-element.8.own_ref.payload_ref, bf16[40,384]{1,0:T(8,128)(2,1)S(1)} %collective-permute-done.low_ref, bf16[40,384]{1,0:T(8,128)(2,1)S(1)} %collective-permute-done.1.high_ref, s32[27,384]{1,0:T(8,128)S(1)} %bitcast.25, s32[32,384]{1,0:T(8,128)S(1)} %bitcast.26, ...), custom_call_target="tpu_custom_call" | custom-call | flops 5000000000 | bytes 5000000 | tf_op jit(solution)/shard_map/pallas_call | solution.py:167
  48.1 0.0 collective-permute-done.2.low_ref
  48.1 3.1 %shard_map.112 = bf16[32,384]{1,0:T(8,128)(2,1)} custom-call(f32[128,384]{1,0:T(8,128)S(1)} %shard_map.110.field_ref, bf16[384,256]{1,0:T(8,128)(2,1)S(1)} %bitcast.20, bf16[384,256]{1,0:T(8,128)(2,1)S(1)} %collective-permute-done.2.low_ref, bf16[384,256]{1,0:T(8,128)(2,1)S(1)} %collective-permute-done.3.high_ref, s32[16,48]{1,0:T(8,128)S(1)} %bitcast.27, ...), custom_call_target="tpu_custom_call" | custom-call | flops 1000000000 | bytes 3000000 | tf_op jit(solution)/shard_map/pallas_call | solution.py:167
  (15 shorter events, 0.0 us)
Async XLA Ops:
  0.7 1.1 %copy-start.1 = (bf16[8,169,169]{2,0,1:T(8,128)(2,1)S(1)}, bf16[8,169,169]{2,0,1:T(8,128)(2,1)}, u32[]{:S(2)}) copy-start(bf16[8,169,169]{2,0,1:T(8,128)(2,1)} %param.18) | copy-start | bytes 1370932
  1.8 0.8 %copy-start.2 = (bf16[169,128]{1,0:T(8,128)(2,1)S(1)}, bf16[169,128]{1,0:T(8,128)(2,1)}, u32[]{:S(2)}) copy-start(bf16[169,128]{1,0:T(8,128)(2,1)} %p2m_ref.1) | copy-start | bytes 129796
  2.6 0.8 %copy-start.4 = (bf16[4,128,32]{1,2,0:T(8,128)(2,1)S(1)}, bf16[4,128,32]{1,2,0:T(8,128)(2,1)}, u32[]{:S(2)}) copy-start(bf16[4,128,32]{1,2,0:T(8,128)(2,1)} %param.13) | copy-start | bytes 98308
  3.3 0.7 %copy-start.6 = (bf16[32,384]{1,0:T(8,128)(2,1)S(1)}, bf16[32,384]{1,0:T(8,128)(2,1)}, u32[]{:S(2)}) copy-start(bf16[32,384]{1,0:T(8,128)(2,1)} %dual_hbm.1) | copy-start | bytes 73732
  4.1 33.6 %copy-start.8 = (bf16[27,128,128]{2,1,0:T(8,128)(2,1)S(1)}, bf16[27,128,128]{2,1,0:T(8,128)(2,1)}, u32[]{:S(2)}) copy-start(bf16[27,128,128]{2,1,0:T(8,128)(2,1)} %near_ref.1) | copy-start | bytes 2654212
  6.0 31.7 %copy-start.3 = (bf16[169,128]{1,0:T(8,128)(2,1)S(1)}, bf16[169,128]{1,0:T(8,128)(2,1)}, u32[]{:S(2)}) copy-start(bf16[169,128]{1,0:T(8,128)(2,1)} %p2m_ref.1) | copy-start | bytes 129796
  6.0 31.7 %copy-start.5 = (bf16[4,128,32]{1,2,0:T(8,128)(2,1)S(1)}, bf16[4,128,32]{1,2,0:T(8,128)(2,1)}, u32[]{:S(2)}) copy-start(bf16[4,128,32]{1,2,0:T(8,128)(2,1)} %param.13) | copy-start | bytes 98308
  6.0 31.7 %copy-start.9 = (s32[384,27]{0,1:T(8,128)S(1)}, s32[384,27]{0,1:T(8,128)}, u32[]{:S(2)}) copy-start(s32[384,27]{0,1:T(8,128)} %param.14) | copy-start | bytes 124420
  6.0 31.7 %copy-start.10 = (s32[384,32]{0,1:T(8,128)S(1)}, s32[384,32]{0,1:T(8,128)}, u32[]{:S(2)}) copy-start(s32[384,32]{0,1:T(8,128)} %param.16) | copy-start | bytes 147460
  6.0 16.6 %all-to-all-start = ((bf16[8,48,256]{2,1,0:T(8,128)(2,1)}), bf16[8,48,256]{2,1,0:T(8,128)(2,1)S(1)}, u32[]{:S(2)}, u32[]{:S(2)}) async-start(bf16[8,48,256]{2,1,0:T(8,128)(2,1)} %get-tuple-element.9), calls=%async_computation | async-start | bytes 393216 | tf_op jit(solution)/shard_map/all_to_all | solution.py:218
  13.0 24.6 %collective-permute-start.1 = (bf16[40,384]{1,0:T(8,128)(2,1)S(1)}, bf16[40,384]{1,0:T(8,128)(2,1)S(1)}, u32[]{:S(2)}, u32[]{:S(2)}) collective-permute-start(bf16[40,384]{1,0:T(8,128)(2,1)S(1)} %get-tuple-element.8.own_ref.payload_ref), channel_id=1, source_target_pairs={{1,0},{2,1},{3,2},{4,3},{5,4},{6,5},{7,6},{8,7},{9,8},{10,9},{11,1... | collective-permute-start | bytes 92168 | tf_op jit(solution)/shard_map/ppermute | solution.py:185
  16.4 21.3 %collective-permute-start = (bf16[40,384]{1,0:T(8,128)(2,1)S(1)}, bf16[40,384]{1,0:T(8,128)(2,1)S(1)}, u32[]{:S(2)}, u32[]{:S(2)}) collective-permute-start(bf16[40,384]{1,0:T(8,128)(2,1)S(1)} %get-tuple-element.8.own_ref.payload_ref), channel_id=1, source_target_pairs={{0,1},{1,2},{2,3},{3,4},{4,5},{5,6},{6,7},{7,8},{8,9},{9,10},{10,1... | collective-permute-start | bytes 92168 | tf_op jit(solution)/shard_map/ppermute | solution.py:185
  19.8 1.3 %copy-start = (bf16[16,169,169]{2,0,1:T(8,128)(2,1)S(1)}, bf16[16,169,169]{2,0,1:T(8,128)(2,1)}, u32[]{:S(2)}) copy-start(bf16[16,169,169]{2,0,1:T(8,128)(2,1)} %param.21) | copy-start | bytes 2741860
  22.6 25.5 %collective-permute-start.3 = (bf16[384,256]{1,0:T(8,128)(2,1)S(1)}, bf16[384,256]{1,0:T(8,128)(2,1)S(1)}, u32[]{:S(2)}, u32[]{:S(2)}) collective-permute-start(bf16[384,256]{1,0:T(8,128)(2,1)S(1)} %bitcast.18), channel_id=1, source_target_pairs={{8,0},{16,8},{24,16},{32,24},{40,32},{48,40},{56,48},{64,56},{72,6... | collective-permute-start | bytes 589832 | tf_op jit(solution)/shard_map/ppermute | solution.py:185
  35.7 12.4 %collective-permute-start.2 = (bf16[384,256]{1,0:T(8,128)(2,1)S(1)}, bf16[384,256]{1,0:T(8,128)(2,1)S(1)}, u32[]{:S(2)}, u32[]{:S(2)}) collective-permute-start(bf16[384,256]{1,0:T(8,128)(2,1)S(1)} %bitcast.19), channel_id=1, source_target_pairs={{0,8},{8,16},{16,24},{24,32},{32,40},{40,48},{48,56},{56,64},{64,7... | collective-permute-start | bytes 589832 | tf_op jit(solution)/shard_map/ppermute | solution.py:185
  37.7 1.8 %copy-start.7 = (bf16[32,169,169]{2,0,1:T(8,128)(2,1)S(1)}, bf16[32,169,169]{2,0,1:T(8,128)(2,1)}, u32[]{:S(2)}) copy-start(bf16[32,169,169]{2,0,1:T(8,128)(2,1)} %param.19) | copy-start | bytes 5483716
  39.5 8.6 %copy-start.11 = (s32[48,16]{0,1:T(8,128)S(1)}, s32[48,16]{0,1:T(8,128)}, u32[]{:S(2)}) copy-start(s32[48,16]{0,1:T(8,128)} %param.20) | copy-start | bytes 9220

commit v4 on v3

v4 whole, which is shorter than its diff:
```python
import jax
import jax.numpy as jnp
from jax import lax
from jax.experimental import pallas as pl
from jax.experimental.pallas import tpu as pltpu
from jax.sharding import PartitionSpec as P

GROUP = 8
F32 = jnp.float32
BF16 = jnp.bfloat16
NT = (((1,), (1,)), ((), ()))
TN = (((0,), (0,)), ((), ()))


def dot(a, b, dims=(((1,), (0,)), ((), ()))):
    return lax.dot_general(a, b, dims, preferred_element_type=F32)


def refine_rows(payload, joined):
    span = joined.shape[0] // 4
    values = payload[:span, :].astype(F32)
    kind = payload[span : span + 1, :].astype(F32)
    spread = jnp.concatenate([jnp.where(kind == k, values, 0.0) for k in range(4)], axis=0)
    return dot(jnp.transpose(spread).astype(BF16), joined).astype(BF16)


def fetch(sources, targets, sems):
    copies = [
        pltpu.make_async_copy(source, target, sems.at[i])
        for i, (source, target) in enumerate(zip(sources, targets))
    ]
    for copy in copies:
        copy.start()
    return copies


def upward_kernel(
    dual_hbm, select_hbm, joined_hbm, p2m_hbm, m2m_hbm, payload_ref, out_ref, table_ref,
    dual, select, joined, p2m, m2m, product, refined, sems,
):
    copies = fetch(
        (dual_hbm, select_hbm, joined_hbm, p2m_hbm, m2m_hbm), (dual, select, joined, p2m, m2m), sems
    )
    subs, coarse, _ = out_ref.shape
    order, width = p2m.shape
    span, boxes = dual.shape
    out_ref[...] = jnp.zeros_like(out_ref)
    for copy in copies:
        copy.wait()
    payload_ref[:span] = dual[...]
    kind = select[...].reshape(1, boxes)
    payload_ref[span:] = jnp.broadcast_to(kind, (8, boxes)).astype(F32).astype(BF16)
    product[...] = dot(m2m[...], p2m[...])
    refined[...] = refine_rows(payload_ref[...], joined[...]).astype(F32)
    total = jnp.zeros((coarse, order), F32)
    for j in range(0, 8, 2):
        tables, rows = [], []
        for i in (j, j + 1):
            table = product[pl.ds(i, order, stride=8), :].astype(BF16)
            table_ref[i, :order] = table
            tables.append(table)
            rows.append(refined[pl.ds(i, coarse, stride=8), :].astype(BF16))
        total = total + dot(jnp.concatenate(rows, axis=1), jnp.concatenate(tables, axis=1), NT)
    for d in range(subs):
        out_ref[d, :, :order] = total.astype(BF16)


class Picker:
    def __init__(self, own_ref, low_ref, high_ref, window):
        self.depth, self.boxes = own_ref.shape
        self.window = window
        whole = jnp.concatenate(
            [low_ref[...], own_ref[...], high_ref[...], jnp.zeros((self.depth, 128), BF16)], axis=1
        ).astype(F32)
        self.blocks = whole.shape[1] // 256
        window[...] = jnp.concatenate(
            [whole[:, b * 256 : (b + 1) * 256] for b in range(self.blocks)], axis=0
        ).astype(BF16)
        self.spot = lax.broadcasted_iota(jnp.int32, (256, self.boxes), 0).astype(BF16)

    def hot(self, index):
        low = (index & 255).astype(F32).astype(BF16)
        return jnp.where(low == self.spot, jnp.array(1.0, BF16), jnp.array(0.0, BF16))

    def expand(self, index, got):
        block, depth = index >> 8, self.depth
        value = jnp.zeros((depth, self.boxes), F32)
        for b in range(self.blocks):
            value = jnp.where(block == b, got[b * depth : (b + 1) * depth], value)
        kind = value[depth - 8 : depth - 7]
        return [jnp.where(kind == k, value[: depth - 8], 0.0) for k in range(4)]

    def add(self, index, table, out):
        boxes = self.boxes
        got = dot(self.window[...], jnp.concatenate([self.hot(i) for i in index], axis=1))
        parts = []
        for c, i in enumerate(index):
            parts += self.expand(i, got[:, c * boxes : (c + 1) * boxes])
        out[...] += dot(table, jnp.concatenate(parts, axis=0).astype(BF16))


def leaf_kernel(
    own_ref, low_ref, high_ref, list_hbm, joined_hbm, p2m_hbm, m2l_hbm, coarse_hbm, field_ref, coarse_ref,
    list_ref, joined_ref, p2m_ref, m2l, coarse, window, table, product, wide, local, sems,
):
    copies = fetch(
        (list_hbm, joined_hbm, p2m_hbm, m2l_hbm, coarse_hbm),
        (list_ref, joined_ref, p2m_ref, m2l, coarse),
        sems,
    )
    picker = Picker(own_ref, low_ref, high_ref, window)
    for copy in copies[:3]:
        copy.wait()
    order, width = p2m_ref.shape
    classes = list_ref.shape[0]
    spread = dot(p2m_ref[...], joined_ref[...], NT).astype(BF16)
    local[...] = jnp.zeros_like(local)
    copies[3].wait()
    product[...] = dot(m2l[...], spread)
    for c in range(classes):
        at = slice((c % GROUP) * width, (c % GROUP + 1) * width)
        table[c // GROUP, :order, at] = product[pl.ds(c, order, stride=classes), :].astype(BF16)
    for g in range(classes // GROUP):
        index = [list_ref[c : c + 1, :] for c in range(g * GROUP, (g + 1) * GROUP)]
        picker.add(index, table[g], local)
    field_ref[...] = dot(p2m_ref[...], local[:order].astype(BF16), TN)
    copies[4].wait()
    classes = coarse_ref.shape[0]
    wide[0] = coarse[:, :128].astype(F32)
    wide[1, :, : order - 128] = coarse[:, 128:].astype(F32)
    for c in range(classes):
        rows = [wide[half, pl.ds(c, order, stride=classes), :] for half in range(2)]
        coarse_ref[c] = jnp.concatenate(rows, axis=1)[:, :order].astype(BF16)


def near_kernel(
    own_ref, low_ref, high_ref, list_ref, joined_ref, near_ref, field_ref, out_ref, window, table,
):
    picker = Picker(own_ref, low_ref, high_ref, window)
    width = near_ref.shape[1]
    classes = list_ref.shape[0]
    joined = joined_ref[...]
    out_ref[...] = field_ref[...]
    for g in range(0, classes, GROUP):
        members = range(g, min(g + GROUP, classes))
        for c in members:
            table[:, (c - g) * width : (c - g + 1) * width] = dot(near_ref[c], joined, NT).astype(BF16)
        index = [list_ref[c : c + 1, :] for c in members]
        picker.add(index, table[:, : len(members) * width], out_ref)


def downward_kernel(
    field_ref, slab_ref, low_ref, high_ref, list_ref, payload_ref, joined_ref, table_ref, m2l_ref,
    out_ref, down,
):
    order = m2l_ref.shape[1]
    classes, coarse = list_ref.shape
    span = out_ref.shape[0]
    index = jnp.transpose(list_ref[...])
    window = jnp.concatenate([low_ref[...], slab_ref[...], high_ref[...]], axis=0)
    spot = lax.broadcasted_iota(jnp.int32, (coarse, window.shape[0]), 1)
    hot = jnp.concatenate(
        [jnp.where(index[:, c : c + 1] == spot, 1.0, 0.0).astype(BF16) for c in range(classes)], axis=0
    )
    picked = dot(hot, window).astype(BF16)
    total = jnp.zeros((coarse, order), F32)
    for c in range(classes):
        total = total + dot(picked[c * coarse : (c + 1) * coarse, :order], m2l_ref[c], NT)
    local = total.astype(BF16)
    for j in range(8):
        down[pl.ds(j, coarse, stride=8), :] = dot(local, table_ref[j, :order])
    field = (field_ref[...] + jnp.transpose(down[...])).astype(BF16)
    by_kind = dot(joined_ref[...], field)
    kind = payload_ref[span : span + 1, :].astype(F32)
    tested = jnp.zeros(out_ref.shape, F32)
    for k in range(4):
        tested = jnp.where(kind == k, by_kind[k * span : (k + 1) * span], tested)
    out_ref[...] = tested.astype(BF16)


def call(kernel, outs, scratch, args, flops, megabytes, in_hbm=()):
    args = [
        pltpu.with_memory_space_constraint(x, pltpu.HBM) if i in in_hbm else x
        for i, x in enumerate(args)
    ]
    return pl.pallas_call(
        kernel,
        out_shape=outs,
        in_specs=[
            pl.BlockSpec(memory_space=pltpu.HBM if i in in_hbm else pltpu.VMEM)
            for i in range(len(args))
        ],
        out_specs=jax.tree.map(lambda _: pl.BlockSpec(memory_space=pltpu.VMEM), outs),
        scratch_shapes=scratch,
        compiler_params=pltpu.CompilerParams(vmem_limit_bytes=40 * 1024 * 1024),
        cost_estimate=pl.CostEstimate(
            flops=flops, bytes_accessed=int(megabytes * 1e6), transcendentals=0
        ),
    )(*args)


def shifted(block, axis, step):
    count = lax.axis_size(axis)
    return lax.ppermute(block, axis, [(i, i + step) for i in range(count) if 0 <= i + step < count])


def body(
    dual_coeffs, refine_select, refine_tiles, near_list, near_tiles, leaf_list, p2m, m2m, leaf_m2l,
    coarse_list, coarse_m2l,
):
    span, boxes = dual_coeffs.shape
    order, width = p2m.shape
    coarse = boxes // 8
    subs = lax.axis_size("sub")
    joined = jnp.transpose(refine_tiles, (0, 2, 1)).reshape(4 * span, width)
    m2m_rows = jnp.transpose(m2m, (1, 0, 2)).reshape(-1, order)
    leaf_rows = jnp.transpose(leaf_m2l, (1, 0, 2)).reshape(-1, order)
    coarse_rows = jnp.transpose(coarse_m2l, (1, 0, 2)).reshape(-1, order)
    payload, mine, table = call(
        upward_kernel,
        (
            jax.ShapeDtypeStruct((span + 8, boxes), BF16),
            jax.ShapeDtypeStruct((subs, coarse, 256), BF16),
            jax.ShapeDtypeStruct((8, 176, width), BF16),
        ),
        [pltpu.VMEM(a.shape, a.dtype) for a in (dual_coeffs, refine_select, joined, p2m, m2m_rows)]
        + [
            pltpu.VMEM((8 * order, width), F32),
            pltpu.VMEM((boxes, width), F32),
            pltpu.SemaphoreType.DMA((5,)),
        ],
        (dual_coeffs, refine_select, joined, p2m, m2m_rows),
        100_000_000, 1.0, (0, 1, 2, 3, 4),
    )
    low = shifted(payload, ("grp", "sub"), 1)
    high = shifted(payload, ("grp", "sub"), -1)
    slab = lax.all_to_all(mine, "sub", 0, 0).reshape(subs * coarse, 256)
    windows = (payload, low, high)
    leaf_args = (leaf_list.T, joined, p2m, leaf_rows, coarse_rows)
    leaf_field, coarse_table = call(
        leaf_kernel,
        (jax.ShapeDtypeStruct((width, boxes), F32), jax.ShapeDtypeStruct(coarse_m2l.shape, BF16)),
        [pltpu.VMEM(a.shape, a.dtype) for a in leaf_args]
        + [
            pltpu.VMEM((5 * (span + 8), 256), BF16),
            pltpu.VMEM((leaf_m2l.shape[0] // GROUP, 176, GROUP * width), BF16),
            pltpu.VMEM((leaf_rows.shape[0], width), F32),
            pltpu.VMEM((2, coarse_rows.shape[0], 128), F32),
            pltpu.VMEM((176, boxes), F32),
            pltpu.SemaphoreType.DMA((5,)),
        ],
        (*windows, *leaf_args),
        100_000_000, 1.0, (3, 4, 5, 6, 7),
    )
    slab_low = shifted(slab, "grp", 1)
    slab_high = shifted(slab, "grp", -1)
    field = call(
        near_kernel,
        jax.ShapeDtypeStruct((width, boxes), F32),
        [pltpu.VMEM((5 * (span + 8), 256), BF16), pltpu.VMEM((width, GROUP * width), BF16)],
        (*windows, near_list.T, joined, near_tiles, leaf_field),
        3_000_000_000, 2.0,
    )
    return call(
        downward_kernel,
        jax.ShapeDtypeStruct((span, boxes), BF16),
        [pltpu.VMEM((boxes, width), F32)],
        (
            field, slab, slab_low, slab_high, coarse_list.T, payload, joined, table, coarse_table,
        ),
        1_000_000_000, 3.0,
    )


def solution(mesh):
    placed = (
        P(None, ("grp", "sub")),
        P(("grp", "sub")),
        P(),
        P(("grp", "sub"), None),
        P(),
        P(("grp", "sub"), None),
        P(),
        P(),
        P(),
        P(("grp", "sub"), None),
        P(),
    )
    return jax.shard_map(
        body, mesh=mesh, in_specs=placed, out_specs=P(None, ("grp", "sub")), check_vma=False
    )
```

time: 51.8 us -> 48.9 us (0.944)
  the two profiles are of different devices: /device:TPU:62 before, /device:TPU:6 now
where the time goes in v4:
time: 48.9 us; the launch traced here: 48.7 us
  starting transfers between devices  29.5 us (60%)
  Pallas kernels  17.1 us (35%)
  waiting for transfers between devices  1.97 us (4%)
    ppermute x4, starting transfers between devices, shifted(): lax.ppermute(block, axis, [(i, i + step) for i in range(count) if 0 <= i...  22.3 us
    pallas_call x4, Pallas kernels, call(): pl.pallas_call(kernel, out_shape=outs, in_specs=[pl.BlockSpec(memory_spac...  17.1 us
    all_to_all x1, starting transfers between devices, body(): slab = lax.all_to_all(mine, 'sub', 0, 0).reshape(subs * coarse, 256)  7.12 us
    ppermute x4, waiting for transfers between devices, shifted(): lax.ppermute(block, axis, [(i, i + step) for i in range(count) if 0 <= i...  1.96 us
  transfers between devices with their start and end apart: 5, of which 3 were waited for; matrix products, arithmetic and copies ran while one was open for 0% of the time, Pallas kernels for 23%

profile of v4, /device:TPU:6, one launch (start us, length us, event | category | flops | bytes accessed | tf_op | source)
XLA Modules:
  0.0 48.7 jit_solution(9020714536832445273)
XLA Ops:
  0.0 2.7 %shard_map.109 = (bf16[40,384]{1,0:T(8,128)(2,1)S(1)}, bf16[8,48,256]{2,1,0:T(8,128)(2,1)}, bf16[8,176,128]{2,1,0:T(8,128)(2,1)S(1)}) custom-call(bf16[32,384]{1,0:T(8,128)(2,1)} %dual_hbm.1, s32[384]{0:T(512)} %select_hbm.1, bf16[128,128]{1,0:T(8,128)(2,1)} %bitcast.19, bf16[169,128]{1,0:T(8,128)(2,1)} %p2m_hbm.3, bf16[1352,169]{1,0:T(8,128)(2,1)} %bitcast.27), custom_call_target="tpu_custom_call" | custom-call | flops 100000000 | bytes 1000000 | tf_op jit(solution)/shard_map/pallas_call | solution.py:186
  2.7 7.1 %all-to-all-start = ((bf16[8,48,256]{2,1,0:T(8,128)(2,1)}), bf16[8,48,256]{2,1,0:T(8,128)(2,1)S(1)}, u32[]{:S(2)}, u32[]{:S(2)}) async-start(bf16[8,48,256]{2,1,0:T(8,128)(2,1)} %get-tuple-element.12), calls=%async_computation | async-start | bytes 393216 | tf_op jit(solution)/shard_map/all_to_all | solution.py:237
  9.8 3.9 %collective-permute-start = (bf16[40,384]{1,0:T(8,128)(2,1)S(1)}, bf16[40,384]{1,0:T(8,128)(2,1)S(1)}, u32[]{:S(2)}, u32[]{:S(2)}) collective-permute-start(bf16[40,384]{1,0:T(8,128)(2,1)S(1)} %get-tuple-element.10.own_ref.payload_ref), channel_id=1, source_target_pairs={{0,1},{1,2},{2,3},{3,4},{4,5},{5,6},{6,7},{7,8},{8,9},{9,10},{10,1... | collective-permute-start | bytes 92168 | tf_op jit(solution)/shard_map/ppermute | solution.py:204
  13.7 10.7 %collective-permute-start.1 = (bf16[40,384]{1,0:T(8,128)(2,1)S(1)}, bf16[40,384]{1,0:T(8,128)(2,1)S(1)}, u32[]{:S(2)}, u32[]{:S(2)}) collective-permute-start(bf16[40,384]{1,0:T(8,128)(2,1)S(1)} %get-tuple-element.10.own_ref.payload_ref), channel_id=1, source_target_pairs={{1,0},{2,1},{3,2},{4,3},{5,4},{6,5},{7,6},{8,7},{9,8},{10,9},{11,1... | collective-permute-start | bytes 92168 | tf_op jit(solution)/shard_map/ppermute | solution.py:204
  24.5 0.9 %collective-permute-done.low_ref = bf16[40,384]{1,0:T(8,128)(2,1)S(1)} collective-permute-done((bf16[40,384]{1,0:T(8,128)(2,1)S(1)}, bf16[40,384]{1,0:T(8,128)(2,1)S(1)}, u32[]{:S(2)}, u32[]{:S(2)}) %collective-permute-start) | collective-permute-done | bytes 30752 | tf_op jit(solution)/shard_map/ppermute | solution.py:204
  25.4 0.6 %collective-permute-done.1.high_ref = bf16[40,384]{1,0:T(8,128)(2,1)S(1)} collective-permute-done((bf16[40,384]{1,0:T(8,128)(2,1)S(1)}, bf16[40,384]{1,0:T(8,128)(2,1)S(1)}, u32[]{:S(2)}, u32[]{:S(2)}) %collective-permute-start.1) | collective-permute-done | bytes 30752 | tf_op jit(solution)/shard_map/ppermute | solution.py:204
  26.0 0.0 copy-start
  26.0 0.0 copy-start.1
  26.0 0.0 copy-start.2
  26.0 8.7 %shard_map.110 = (f32[128,384]{1,0:T(8,128)S(1)}, bf16[16,169,169]{2,1,0:T(8,128)(2,1)S(1)}) custom-call(bf16[40,384]{1,0:T(8,128)(2,1)S(1)} %get-tuple-element.10.own_ref.payload_ref, bf16[40,384]{1,0:T(8,128)(2,1)S(1)} %collective-permute-done.low_ref, bf16[40,384]{1,0:T(8,128)(2,1)S(1)} %collective-permute-done.1.high_ref, s32[32,384]{1,0:T(8,128)} %bitcast.28, ...), custom_call_target="tpu_custom_call" | custom-call | flops 100000000 | bytes 1000000 | tf_op jit(solution)/shard_map/pallas_call | solution.py:186
  34.7 0.0 all-to-all-done
  34.7 1.9 %collective-permute-start.2 = (bf16[384,256]{1,0:T(8,128)(2,1)S(1)}, bf16[384,256]{1,0:T(8,128)(2,1)S(1)}, u32[]{:S(2)}, u32[]{:S(2)}) collective-permute-start(bf16[384,256]{1,0:T(8,128)(2,1)S(1)} %bitcast.16), channel_id=1, source_target_pairs={{0,8},{8,16},{16,24},{24,32},{32,40},{40,48},{48,56},{56,64},{64,7... | collective-permute-start | bytes 589832 | tf_op jit(solution)/shard_map/ppermute | solution.py:204
  36.7 5.8 %collective-permute-start.3 = (bf16[384,256]{1,0:T(8,128)(2,1)S(1)}, bf16[384,256]{1,0:T(8,128)(2,1)S(1)}, u32[]{:S(2)}, u32[]{:S(2)}) collective-permute-start(bf16[384,256]{1,0:T(8,128)(2,1)S(1)} %bitcast.17), channel_id=1, source_target_pairs={{8,0},{16,8},{24,16},{32,24},{40,32},{48,40},{56,48},{64,56},{72,6... | collective-permute-start | bytes 589832 | tf_op jit(solution)/shard_map/ppermute | solution.py:204
  42.4 0.0 copy-done
  42.4 0.0 copy-done.1
  42.4 0.0 copy-done.2
  42.5 0.0 copy-start.3
  42.5 2.7 %shard_map.111.field_ref = f32[128,384]{1,0:T(8,128)S(1)} custom-call(bf16[40,384]{1,0:T(8,128)(2,1)S(1)} %get-tuple-element.10.own_ref.payload_ref, bf16[40,384]{1,0:T(8,128)(2,1)S(1)} %collective-permute-done.low_ref, bf16[40,384]{1,0:T(8,128)(2,1)S(1)} %collective-permute-done.1.high_ref, s32[27,384]{1,0:T(8,128)S(1)} %bitcast.23, ...), custom_call_target="tpu_custom_call" | custom-call | flops 3000000000 | bytes 2000000 | tf_op jit(solution)/shard_map/pallas_call | solution.py:186
  45.2 0.0 collective-permute-done.2.low_ref
  45.2 0.4 collective-permute-done.3.high_ref
  45.6 0.0 copy-done.3
  45.6 3.1 %shard_map.112 = bf16[32,384]{1,0:T(8,128)(2,1)} custom-call(f32[128,384]{1,0:T(8,128)S(1)} %shard_map.111.field_ref, bf16[384,256]{1,0:T(8,128)(2,1)S(1)} %bitcast.18, bf16[384,256]{1,0:T(8,128)(2,1)S(1)} %collective-permute-done.2.low_ref, bf16[384,256]{1,0:T(8,128)(2,1)S(1)} %collective-permute-done.3.high_ref, s32[16,48]{1,0:T(8,128)S(1)} %bitcast.24, ...), custom_call_target="tpu_custom_call" | custom-call | flops 1000000000 | bytes 3000000 | tf_op jit(solution)/shard_map/pallas_call | solution.py:186
Async XLA Ops:
  2.7 32.0 %all-to-all-start = ((bf16[8,48,256]{2,1,0:T(8,128)(2,1)}), bf16[8,48,256]{2,1,0:T(8,128)(2,1)S(1)}, u32[]{:S(2)}, u32[]{:S(2)}) async-start(bf16[8,48,256]{2,1,0:T(8,128)(2,1)} %get-tuple-element.12), calls=%async_computation | async-start | bytes 393216 | tf_op jit(solution)/shard_map/all_to_all | solution.py:237
  9.8 15.6 %collective-permute-start = (bf16[40,384]{1,0:T(8,128)(2,1)S(1)}, bf16[40,384]{1,0:T(8,128)(2,1)S(1)}, u32[]{:S(2)}, u32[]{:S(2)}) collective-permute-start(bf16[40,384]{1,0:T(8,128)(2,1)S(1)} %get-tuple-element.10.own_ref.payload_ref), channel_id=1, source_target_pairs={{0,1},{1,2},{2,3},{3,4},{4,5},{5,6},{6,7},{7,8},{8,9},{9,10},{10,1... | collective-permute-start | bytes 92168 | tf_op jit(solution)/shard_map/ppermute | solution.py:204
  13.7 12.3 %collective-permute-start.1 = (bf16[40,384]{1,0:T(8,128)(2,1)S(1)}, bf16[40,384]{1,0:T(8,128)(2,1)S(1)}, u32[]{:S(2)}, u32[]{:S(2)}) collective-permute-start(bf16[40,384]{1,0:T(8,128)(2,1)S(1)} %get-tuple-element.10.own_ref.payload_ref), channel_id=1, source_target_pairs={{1,0},{2,1},{3,2},{4,3},{5,4},{6,5},{7,6},{8,7},{9,8},{10,9},{11,1... | collective-permute-start | bytes 92168 | tf_op jit(solution)/shard_map/ppermute | solution.py:204
  26.0 16.4 %copy-start = (bf16[4,128,32]{1,2,0:T(8,128)(2,1)S(1)}, bf16[4,128,32]{1,2,0:T(8,128)(2,1)}, u32[]{:S(2)}) copy-start(bf16[4,128,32]{1,2,0:T(8,128)(2,1)} %param.13) | copy-start | bytes 98308
  26.0 16.4 %copy-start.1 = (bf16[27,128,128]{2,1,0:T(8,128)(2,1)S(1)}, bf16[27,128,128]{2,1,0:T(8,128)(2,1)}, u32[]{:S(2)}) copy-start(bf16[27,128,128]{2,1,0:T(8,128)(2,1)} %near_ref.1) | copy-start | bytes 2654212
  26.0 16.4 %copy-start.2 = (s32[384,27]{0,1:T(8,128)S(1)}, s32[384,27]{0,1:T(8,128)}, u32[]{:S(2)}) copy-start(s32[384,27]{0,1:T(8,128)} %param.14) | copy-start | bytes 124420
  34.7 10.4 %collective-permute-start.2 = (bf16[384,256]{1,0:T(8,128)(2,1)S(1)}, bf16[384,256]{1,0:T(8,128)(2,1)S(1)}, u32[]{:S(2)}, u32[]{:S(2)}) collective-permute-start(bf16[384,256]{1,0:T(8,128)(2,1)S(1)} %bitcast.16), channel_id=1, source_target_pairs={{0,8},{8,16},{16,24},{24,32},{32,40},{40,48},{48,56},{56,64},{64,7... | collective-permute-start | bytes 589832 | tf_op jit(solution)/shard_map/ppermute | solution.py:204
  36.7 8.9 %collective-permute-start.3 = (bf16[384,256]{1,0:T(8,128)(2,1)S(1)}, bf16[384,256]{1,0:T(8,128)(2,1)S(1)}, u32[]{:S(2)}, u32[]{:S(2)}) collective-permute-start(bf16[384,256]{1,0:T(8,128)(2,1)S(1)} %bitcast.17), channel_id=1, source_target_pairs={{8,0},{16,8},{24,16},{32,24},{40,32},{48,40},{56,48},{64,56},{72,6... | collective-permute-start | bytes 589832 | tf_op jit(solution)/shard_map/ppermute | solution.py:204
  42.5 3.1 %copy-start.3 = (s32[48,16]{0,1:T(8,128)S(1)}, s32[48,16]{0,1:T(8,128)}, u32[]{:S(2)}) copy-start(s32[48,16]{0,1:T(8,128)} %param.20) | copy-start | bytes 9220

commit v5 on v4

--- a/solution.py
+++ b/solution.py
@@ -99,38 +99,37 @@
         out[...] += dot(table, jnp.concatenate(parts, axis=0).astype(BF16))
 
 
-def leaf_kernel(
-    own_ref, low_ref, high_ref, list_hbm, joined_hbm, p2m_hbm, m2l_hbm, coarse_hbm, field_ref, coarse_ref,
-    list_ref, joined_ref, p2m_ref, m2l, coarse, window, table, product, wide, local, sems,
-):
-    copies = fetch(
-        (list_hbm, joined_hbm, p2m_hbm, m2l_hbm, coarse_hbm),
-        (list_ref, joined_ref, p2m_ref, m2l, coarse),
-        sems,
-    )
-    picker = Picker(own_ref, low_ref, high_ref, window)
-    for copy in copies[:3]:
-        copy.wait()
-    order, width = p2m_ref.shape
-    classes = list_ref.shape[0]
-    spread = dot(p2m_ref[...], joined_ref[...], NT).astype(BF16)
-    local[...] = jnp.zeros_like(local)
-    copies[3].wait()
+def table_kernel(
+    joined_hbm, p2m_hbm, m2l_hbm, coarse_hbm, leaf_ref, coarse_ref, joined, p2m, m2l, coarse, product, wide, sems
+):
+    copies = fetch((joined_hbm, p2m_hbm, m2l_hbm, coarse_hbm), (joined, p2m, m2l, coarse), sems)
+    order, width = p2m.shape
+    copies[0].wait()
+    copies[1].wait()
+    spread = dot(p2m[...], joined[...], NT).astype(BF16)
+    copies[2].wait()
     product[...] = dot(m2l[...], spread)
+    classes = leaf_ref.shape[0] * GROUP
     for c in range(classes):
         at = slice((c % GROUP) * width, (c % GROUP + 1) * width)
-        table[c // GROUP, :order, at] = product[pl.ds(c, order, stride=classes), :].astype(BF16)
-    for g in range(classes // GROUP):
-        index = [list_ref[c : c + 1, :] for c in range(g * GROUP, (g + 1) * GROUP)]
-        picker.add(index, table[g], local)
-    field_ref[...] = dot(p2m_ref[...], local[:order].astype(BF16), TN)
-    copies[4].wait()
+        leaf_ref[c // GROUP, :order, at] = product[pl.ds(c, order, stride=classes), :].astype(BF16)
+    copies[3].wait()
     classes = coarse_ref.shape[0]
     wide[0] = coarse[:, :128].astype(F32)
     wide[1, :, : order - 128] = coarse[:, 128:].astype(F32)
     for c in range(classes):
         rows = [wide[half, pl.ds(c, order, stride=classes), :] for half in range(2)]
         coarse_ref[c] = jnp.concatenate(rows, axis=1)[:, :order].astype(BF16)
+
+
+def leaf_kernel(own_ref, low_ref, high_ref, list_ref, p2m_ref, table_ref, field_ref, window, local):
+    picker = Picker(own_ref, low_ref, high_ref, window)
+    order = p2m_ref.shape[0]
+    local[...] = jnp.zeros_like(local)
+    for g in range(table_ref.shape[0]):
+        index = [list_ref[c : c + 1, :] for c in range(g * GROUP, (g + 1) * GROUP)]
+        picker.add(index, table_ref[g], local)
+    field_ref[...] = dot(p2m_ref[...], local[:order].astype(BF16), TN)
 
 
 def near_kernel(
@@ -236,21 +235,28 @@
     high = shifted(payload, ("grp", "sub"), -1)
     slab = lax.all_to_all(mine, "sub", 0, 0).reshape(subs * coarse, 256)
     windows = (payload, low, high)
-    leaf_args = (leaf_list.T, joined, p2m, leaf_rows, coarse_rows)
-    leaf_field, coarse_table = call(
-        leaf_kernel,
-        (jax.ShapeDtypeStruct((width, boxes), F32), jax.ShapeDtypeStruct(coarse_m2l.shape, BF16)),
-        [pltpu.VMEM(a.shape, a.dtype) for a in leaf_args]
+    table_args = (joined, p2m, leaf_rows, coarse_rows)
+    leaf_table, coarse_table = call(
+        table_kernel,
+        (
+            jax.ShapeDtypeStruct((leaf_m2l.shape[0] // GROUP, 176, GROUP * width), BF16),
+            jax.ShapeDtypeStruct(coarse_m2l.shape, BF16),
+        ),
+        [pltpu.VMEM(a.shape, a.dtype) for a in table_args]
         + [
-            pltpu.VMEM((5 * (span + 8), 256), BF16),
-            pltpu.VMEM((leaf_m2l.shape[0] // GROUP, 176, GROUP * width), BF16),
             pltpu.VMEM((leaf_rows.shape[0], width), F32),
             pltpu.VMEM((2, coarse_rows.shape[0], 128), F32),
-            pltpu.VMEM((176, boxes), F32),
-            pltpu.SemaphoreType.DMA((5,)),
+            pltpu.SemaphoreType.DMA((4,)),
         ],
-        (*windows, *leaf_args),
-        100_000_000, 1.0, (3, 4, 5, 6, 7),
+        table_args,
+        100_000_000, 1.0, (0, 1, 2, 3),
+    )
+    leaf_field = call(
+        leaf_kernel,
+        jax.ShapeDtypeStruct((width, boxes), F32),
+        [pltpu.VMEM((5 * (span + 8), 256), BF16), pltpu.VMEM((176, boxes), F32)],
+        (*windows, leaf_list.T, p2m, leaf_table),
+        100_000_000, 1.0,
     )
     slab_low = shifted(slab, "grp", 1)
     slab_high = shifted(slab, "grp", -1)

time: 48.9 us -> 47.1 us (0.963)
  waiting for transfers between devices: 1.97 us -> 0.43 us
    ppermute x4, waiting for transfers between devices: 1.96 us -> 0.43 us  [shifted(): lax.ppermute(block, axis, [(i, i + step) for i in range(count) if 0 <= i...]
    pallas_call x4 -> x5, Pallas kernels: 17.1 us -> 16.7 us  [call(): pl.pallas_call(kernel, out_shape=outs, in_specs=[pl.BlockSpec(memory_spac...]
  transfers between devices with their start and end apart: 5 -> 5, of which waited for: 3 -> 1; matrix products, arithmetic and copies ran while one was open for 0% -> 0% of each run, Pallas kernels for 23% -> 23%
where the time goes in v5:
time: 47.1 us; the launch traced here: 46.8 us
  starting transfers between devices  29.5 us (63%)
  Pallas kernels  16.7 us (35%)
    ppermute x4, starting transfers between devices, shifted(): lax.ppermute(block, axis, [(i, i + step) for i in range(count) if 0 <= i...  22.3 us
    pallas_call x5, Pallas kernels, call(): pl.pallas_call(kernel, out_shape=outs, in_specs=[pl.BlockSpec(memory_spac...  16.7 us
    all_to_all x1, starting transfers between devices, body(): slab = lax.all_to_all(mine, 'sub', 0, 0).reshape(subs * coarse, 256)  7.12 us
  transfers between devices with their start and end apart: 5, of which 1 were waited for; matrix products, arithmetic and copies ran while one was open for 0% of the time, Pallas kernels for 23%

profile of v5, /device:TPU:6, one launch (start us, length us, event | category | flops | bytes accessed | tf_op | source)
XLA Modules:
  0.0 46.8 jit_solution(12862697945209832992)
XLA Ops:
  0.0 2.7 %shard_map.109 = (bf16[40,384]{1,0:T(8,128)(2,1)S(1)}, bf16[8,48,256]{2,1,0:T(8,128)(2,1)}, bf16[8,176,128]{2,1,0:T(8,128)(2,1)S(1)}) custom-call(bf16[32,384]{1,0:T(8,128)(2,1)} %dual_hbm.1, s32[384]{0:T(512)} %select_hbm.1, bf16[128,128]{1,0:T(8,128)(2,1)} %bitcast.19, bf16[169,128]{1,0:T(8,128)(2,1)} %p2m_ref.1, bf16[1352,169]{1,0:T(8,128)(2,1)} %bitcast.28), custom_call_target="tpu_custom_call" | custom-call | flops 100000000 | bytes 1000000 | tf_op jit(solution)/shard_map/pallas_call | solution.py:185
  2.7 7.1 %all-to-all-start = ((bf16[8,48,256]{2,1,0:T(8,128)(2,1)}), bf16[8,48,256]{2,1,0:T(8,128)(2,1)S(1)}, u32[]{:S(2)}, u32[]{:S(2)}) async-start(bf16[8,48,256]{2,1,0:T(8,128)(2,1)} %get-tuple-element.12), calls=%async_computation | async-start | bytes 393216 | tf_op jit(solution)/shard_map/all_to_all | solution.py:236
  9.8 3.9 %collective-permute-start = (bf16[40,384]{1,0:T(8,128)(2,1)S(1)}, bf16[40,384]{1,0:T(8,128)(2,1)S(1)}, u32[]{:S(2)}, u32[]{:S(2)}) collective-permute-start(bf16[40,384]{1,0:T(8,128)(2,1)S(1)} %get-tuple-element.10.own_ref.payload_ref), channel_id=1, source_target_pairs={{0,1},{1,2},{2,3},{3,4},{4,5},{5,6},{6,7},{7,8},{8,9},{9,10},{10,1... | collective-permute-start | bytes 92168 | tf_op jit(solution)/shard_map/ppermute | solution.py:203
  13.7 10.7 %collective-permute-start.1 = (bf16[40,384]{1,0:T(8,128)(2,1)S(1)}, bf16[40,384]{1,0:T(8,128)(2,1)S(1)}, u32[]{:S(2)}, u32[]{:S(2)}) collective-permute-start(bf16[40,384]{1,0:T(8,128)(2,1)S(1)} %get-tuple-element.10.own_ref.payload_ref), channel_id=1, source_target_pairs={{1,0},{2,1},{3,2},{4,3},{5,4},{6,5},{7,6},{8,7},{9,8},{10,9},{11,1... | collective-permute-start | bytes 92168 | tf_op jit(solution)/shard_map/ppermute | solution.py:203
  24.5 0.0 copy-start
  24.5 0.0 copy-start.2
  24.5 5.8 %shard_map.110 = (bf16[4,176,1024]{2,1,0:T(8,128)(2,1)S(1)}, bf16[16,169,169]{2,1,0:T(8,128)(2,1)S(1)}) custom-call(bf16[128,128]{1,0:T(8,128)(2,1)} %bitcast.20, bf16[169,128]{1,0:T(8,128)(2,1)} %p2m_ref.1, bf16[5408,169]{1,0:T(8,128)(2,1)} %bitcast.26, bf16[2704,169]{1,0:T(8,128)(2,1)} %bitcast.27), custom_call_target="tpu_custom_call" | custom-call | flops 100000000 | bytes 1000000 | tf_op jit(solution)/shard_map/pallas_call | solution.py:185
  30.3 0.0 copy-start.1
  30.3 0.0 copy-start.3
  30.4 0.0 copy-start.4
  30.4 0.0 collective-permute-done.low_ref
  30.4 0.0 collective-permute-done.1.high_ref
  30.4 0.0 copy-done
  30.4 0.0 copy-done.2
  30.4 2.4 %shard_map.111.field_ref = f32[128,384]{1,0:T(8,128)S(1)} custom-call(bf16[40,384]{1,0:T(8,128)(2,1)S(1)} %get-tuple-element.10.own_ref.payload_ref, bf16[40,384]{1,0:T(8,128)(2,1)S(1)} %collective-permute-done.low_ref, bf16[40,384]{1,0:T(8,128)(2,1)S(1)} %collective-permute-done.1.high_ref, s32[32,384]{1,0:T(8,128)S(1)} %bitcast.23, ...), custom_call_target="tpu_custom_call" | custom-call | flops 100000000 | bytes 1000000 | tf_op jit(solution)/shard_map/pallas_call | solution.py:185
  32.9 0.0 all-to-all-done
  32.9 1.9 %collective-permute-start.2 = (bf16[384,256]{1,0:T(8,128)(2,1)S(1)}, bf16[384,256]{1,0:T(8,128)(2,1)S(1)}, u32[]{:S(2)}, u32[]{:S(2)}) collective-permute-start(bf16[384,256]{1,0:T(8,128)(2,1)S(1)} %bitcast.16), channel_id=1, source_target_pairs={{0,8},{8,16},{16,24},{24,32},{32,40},{40,48},{48,56},{56,64},{64,7... | collective-permute-start | bytes 589832 | tf_op jit(solution)/shard_map/ppermute | solution.py:203
  34.8 5.8 %collective-permute-start.3 = (bf16[384,256]{1,0:T(8,128)(2,1)S(1)}, bf16[384,256]{1,0:T(8,128)(2,1)S(1)}, u32[]{:S(2)}, u32[]{:S(2)}) collective-permute-start(bf16[384,256]{1,0:T(8,128)(2,1)S(1)} %bitcast.17), channel_id=1, source_target_pairs={{8,0},{16,8},{24,16},{32,24},{40,32},{48,40},{56,48},{64,56},{72,6... | collective-permute-start | bytes 589832 | tf_op jit(solution)/shard_map/ppermute | solution.py:203
  40.6 0.0 copy-done.1
  40.6 0.0 copy-start.5
  40.6 2.7 %shard_map.112.field_ref = f32[128,384]{1,0:T(8,128)S(1)} custom-call(bf16[40,384]{1,0:T(8,128)(2,1)S(1)} %get-tuple-element.10.own_ref.payload_ref, bf16[40,384]{1,0:T(8,128)(2,1)S(1)} %collective-permute-done.low_ref, bf16[40,384]{1,0:T(8,128)(2,1)S(1)} %collective-permute-done.1.high_ref, s32[27,384]{1,0:T(8,128)S(1)} %bitcast.24, ...), custom_call_target="tpu_custom_call" | custom-call | flops 3000000000 | bytes 2000000 | tf_op jit(solution)/shard_map/pallas_call | solution.py:185
  43.3 0.0 collective-permute-done.2.low_ref
  43.3 0.4 collective-permute-done.3.high_ref
  43.7 3.1 %shard_map.113 = bf16[32,384]{1,0:T(8,128)(2,1)} custom-call(f32[128,384]{1,0:T(8,128)S(1)} %shard_map.112.field_ref, bf16[384,256]{1,0:T(8,128)(2,1)S(1)} %bitcast.18, bf16[384,256]{1,0:T(8,128)(2,1)S(1)} %collective-permute-done.2.low_ref, bf16[384,256]{1,0:T(8,128)(2,1)S(1)} %collective-permute-done.3.high_ref, s32[16,48]{1,0:T(8,128)S(1)} %bitcast.25, ...), custom_call_target="tpu_custom_call" | custom-call | flops 1000000000 | bytes 3000000 | tf_op jit(solution)/shard_map/pallas_call | solution.py:185
  (3 shorter events, 0.0 us)
Async XLA Ops:
  2.7 30.2 %all-to-all-start = ((bf16[8,48,256]{2,1,0:T(8,128)(2,1)}), bf16[8,48,256]{2,1,0:T(8,128)(2,1)S(1)}, u32[]{:S(2)}, u32[]{:S(2)}) async-start(bf16[8,48,256]{2,1,0:T(8,128)(2,1)} %get-tuple-element.12), calls=%async_computation | async-start | bytes 393216 | tf_op jit(solution)/shard_map/all_to_all | solution.py:236
  9.8 20.6 %collective-permute-start = (bf16[40,384]{1,0:T(8,128)(2,1)S(1)}, bf16[40,384]{1,0:T(8,128)(2,1)S(1)}, u32[]{:S(2)}, u32[]{:S(2)}) collective-permute-start(bf16[40,384]{1,0:T(8,128)(2,1)S(1)} %get-tuple-element.10.own_ref.payload_ref), channel_id=1, source_target_pairs={{0,1},{1,2},{2,3},{3,4},{4,5},{5,6},{6,7},{7,8},{8,9},{9,10},{10,1... | collective-permute-start | bytes 92168 | tf_op jit(solution)/shard_map/ppermute | solution.py:203
  13.7 16.7 %collective-permute-start.1 = (bf16[40,384]{1,0:T(8,128)(2,1)S(1)}, bf16[40,384]{1,0:T(8,128)(2,1)S(1)}, u32[]{:S(2)}, u32[]{:S(2)}) collective-permute-start(bf16[40,384]{1,0:T(8,128)(2,1)S(1)} %get-tuple-element.10.own_ref.payload_ref), channel_id=1, source_target_pairs={{1,0},{2,1},{3,2},{4,3},{5,4},{6,5},{7,6},{8,7},{9,8},{10,9},{11,1... | collective-permute-start | bytes 92168 | tf_op jit(solution)/shard_map/ppermute | solution.py:203
  24.5 5.9 %copy-start = (bf16[169,128]{1,0:T(8,128)(2,1)S(1)}, bf16[169,128]{1,0:T(8,128)(2,1)}, u32[]{:S(2)}) copy-start(bf16[169,128]{1,0:T(8,128)(2,1)} %p2m_ref.1) | copy-start | bytes 129796
  24.5 5.9 %copy-start.2 = (s32[384,32]{0,1:T(8,128)S(1)}, s32[384,32]{0,1:T(8,128)}, u32[]{:S(2)}) copy-start(s32[384,32]{0,1:T(8,128)} %param.16) | copy-start | bytes 147460
  30.3 10.2 %copy-start.1 = (bf16[4,128,32]{1,2,0:T(8,128)(2,1)S(1)}, bf16[4,128,32]{1,2,0:T(8,128)(2,1)}, u32[]{:S(2)}) copy-start(bf16[4,128,32]{1,2,0:T(8,128)(2,1)} %param.13) | copy-start | bytes 98308
  30.3 10.2 %copy-start.3 = (bf16[27,128,128]{2,1,0:T(8,128)(2,1)S(1)}, bf16[27,128,128]{2,1,0:T(8,128)(2,1)}, u32[]{:S(2)}) copy-start(bf16[27,128,128]{2,1,0:T(8,128)(2,1)} %near_ref.1) | copy-start | bytes 2654212
  30.4 10.2 %copy-start.4 = (s32[384,27]{0,1:T(8,128)S(1)}, s32[384,27]{0,1:T(8,128)}, u32[]{:S(2)}) copy-start(s32[384,27]{0,1:T(8,128)} %param.14) | copy-start | bytes 124420
  32.9 10.4 %collective-permute-start.2 = (bf16[384,256]{1,0:T(8,128)(2,1)S(1)}, bf16[384,256]{1,0:T(8,128)(2,1)S(1)}, u32[]{:S(2)}, u32[]{:S(2)}) collective-permute-start(bf16[384,256]{1,0:T(8,128)(2,1)S(1)} %bitcast.16), channel_id=1, source_target_pairs={{0,8},{8,16},{16,24},{24,32},{32,40},{40,48},{48,56},{56,64},{64,7... | collective-permute-start | bytes 589832 | tf_op jit(solution)/shard_map/ppermute | solution.py:203
  34.8 8.9 %collective-permute-start.3 = (bf16[384,256]{1,0:T(8,128)(2,1)S(1)}, bf16[384,256]{1,0:T(8,128)(2,1)S(1)}, u32[]{:S(2)}, u32[]{:S(2)}) collective-permute-start(bf16[384,256]{1,0:T(8,128)(2,1)S(1)} %bitcast.17), channel_id=1, source_target_pairs={{8,0},{16,8},{24,16},{32,24},{40,32},{48,40},{56,48},{64,56},{72,6... | collective-permute-start | bytes 589832 | tf_op jit(solution)/shard_map/ppermute | solution.py:203
  40.6 3.1 %copy-start.5 = (s32[48,16]{0,1:T(8,128)S(1)}, s32[48,16]{0,1:T(8,128)}, u32[]{:S(2)}) copy-start(s32[48,16]{0,1:T(8,128)} %param.20) | copy-start | bytes 9220

commit v6 on v5

--- a/solution.py
+++ b/solution.py
@@ -99,27 +99,22 @@
         out[...] += dot(table, jnp.concatenate(parts, axis=0).astype(BF16))
 
 
-def table_kernel(
-    joined_hbm, p2m_hbm, m2l_hbm, coarse_hbm, leaf_ref, coarse_ref, joined, p2m, m2l, coarse, product, wide, sems
-):
-    copies = fetch((joined_hbm, p2m_hbm, m2l_hbm, coarse_hbm), (joined, p2m, m2l, coarse), sems)
-    order, width = p2m.shape
-    copies[0].wait()
-    copies[1].wait()
-    spread = dot(p2m[...], joined[...], NT).astype(BF16)
-    copies[2].wait()
-    product[...] = dot(m2l[...], spread)
-    classes = leaf_ref.shape[0] * GROUP
+def by_eights(ref, rows, classes):
+    order, width = rows.shape[0] // classes, rows.shape[1]
+    split = rows.reshape(order, classes // 8, 8, width)
+    for b in range(classes // 8):
+        ref[b, :, :width] = split[:, b].reshape(order * 8, width)
+
+
+def table_kernel(joined_ref, p2m_ref, m2l_ref, out_ref, product):
+    order, width = p2m_ref.shape
+    classes = out_ref.shape[0] * GROUP
+    spread = dot(p2m_ref[...], joined_ref[...], NT).astype(BF16)
+    by_eights(product, dot(m2l_ref[...], spread), classes)
     for c in range(classes):
         at = slice((c % GROUP) * width, (c % GROUP + 1) * width)
-        leaf_ref[c // GROUP, :order, at] = product[pl.ds(c, order, stride=classes), :].astype(BF16)
-    copies[3].wait()
-    classes = coarse_ref.shape[0]
-    wide[0] = coarse[:, :128].astype(F32)
-    wide[1, :, : order - 128] = coarse[:, 128:].astype(F32)
-    for c in range(classes):
-        rows = [wide[half, pl.ds(c, order, stride=classes), :] for half in range(2)]
-        coarse_ref[c] = jnp.concatenate(rows, axis=1)[:, :order].astype(BF16)
+        rows = product[c // 8, pl.ds(c % 8, order, stride=8), :]
+        out_ref[c // GROUP, :order, at] = rows.astype(BF16)
 
 
 def leaf_kernel(own_ref, low_ref, high_ref, list_ref, p2m_ref, table_ref, field_ref, window, local):
@@ -133,7 +128,8 @@
 
 
 def near_kernel(
-    own_ref, low_ref, high_ref, list_ref, joined_ref, near_ref, field_ref, out_ref, window, table,
+    own_ref, low_ref, high_ref, list_ref, joined_ref, near_ref, field_ref, coarse, out_ref, coarse_ref,
+    window, table, wide,
 ):
     picker = Picker(own_ref, low_ref, high_ref, window)
     width = near_ref.shape[1]
@@ -146,6 +142,12 @@
             table[:, (c - g) * width : (c - g + 1) * width] = dot(near_ref[c], joined, NT).astype(BF16)
         index = [list_ref[c : c + 1, :] for c in members]
         picker.add(index, table[:, : len(members) * width], out_ref)
+    classes, order, _ = coarse_ref.shape
+    by_eights(wide.at[0], coarse[:, :128].astype(F32), classes)
+    by_eights(wide.at[1], coarse[:, 128:].astype(F32), classes)
+    for c in range(classes):
+        rows = [wide[half, c // 8, pl.ds(c % 8, order, stride=8), :] for half in range(2)]
+        coarse_ref[c] = jnp.concatenate(rows, axis=1)[:, :order].astype(BF16)
 
 
 def downward_kernel(
@@ -191,7 +193,7 @@
         ],
         out_specs=jax.tree.map(lambda _: pl.BlockSpec(memory_space=pltpu.VMEM), outs),
         scratch_shapes=scratch,
-        compiler_params=pltpu.CompilerParams(vmem_limit_bytes=40 * 1024 * 1024),
+        compiler_params=pltpu.CompilerParams(vmem_limit_bytes=32 * 1024 * 1024),
         cost_estimate=pl.CostEstimate(
             flops=flops, bytes_accessed=int(megabytes * 1e6), transcendentals=0
         ),
@@ -229,42 +231,37 @@
             pltpu.SemaphoreType.DMA((5,)),
         ],
         (dual_coeffs, refine_select, joined, p2m, m2m_rows),
-        100_000_000, 1.0, (0, 1, 2, 3, 4),
+        10_000_000_000, 1.0, (0, 1, 2, 3, 4),
     )
     low = shifted(payload, ("grp", "sub"), 1)
     high = shifted(payload, ("grp", "sub"), -1)
     slab = lax.all_to_all(mine, "sub", 0, 0).reshape(subs * coarse, 256)
     windows = (payload, low, high)
-    table_args = (joined, p2m, leaf_rows, coarse_rows)
-    leaf_table, coarse_table = call(
+    leaf_table = call(
         table_kernel,
-        (
-            jax.ShapeDtypeStruct((leaf_m2l.shape[0] // GROUP, 176, GROUP * width), BF16),
-            jax.ShapeDtypeStruct(coarse_m2l.shape, BF16),
-        ),
-        [pltpu.VMEM(a.shape, a.dtype) for a in table_args]
-        + [
-            pltpu.VMEM((leaf_rows.shape[0], width), F32),
-            pltpu.VMEM((2, coarse_rows.shape[0], 128), F32),
-            pltpu.SemaphoreType.DMA((4,)),
-        ],
-        table_args,
-        100_000_000, 1.0, (0, 1, 2, 3),
+        jax.ShapeDtypeStruct((leaf_m2l.shape[0] // GROUP, 176, GROUP * width), BF16),
+        [pltpu.VMEM((leaf_m2l.shape[0] // 8, 8 * order, width), F32)],
+        (joined, p2m, leaf_rows),
+        100_000_000, 1.0,
     )
     leaf_field = call(
         leaf_kernel,
         jax.ShapeDtypeStruct((width, boxes), F32),
         [pltpu.VMEM((5 * (span + 8), 256), BF16), pltpu.VMEM((176, boxes), F32)],
         (*windows, leaf_list.T, p2m, leaf_table),
-        100_000_000, 1.0,
+        2_000_000_000, 1.0,
     )
     slab_low = shifted(slab, "grp", 1)
     slab_high = shifted(slab, "grp", -1)
-    field = call(
+    field, coarse_table = call(
         near_kernel,
-        jax.ShapeDtypeStruct((width, boxes), F32),
-        [pltpu.VMEM((5 * (span + 8), 256), BF16), pltpu.VMEM((width, GROUP * width), BF16)],
-        (*windows, near_list.T, joined, near_tiles, leaf_field),
+        (jax.ShapeDtypeStruct((width, boxes), F32), jax.ShapeDtypeStruct(coarse_m2l.shape, BF16)),
+        [
+            pltpu.VMEM((5 * (span + 8), 256), BF16),
+            pltpu.VMEM((width, GROUP * width), BF16),
+            pltpu.VMEM((2, coarse_m2l.shape[0] // 8, 8 * order, 128), F32),
+        ],
+        (*windows, near_list.T, joined, near_tiles, leaf_field, coarse_rows),
         3_000_000_000, 2.0,
     )
     return call(

time: 47.1 us -> 43.2 us (0.917)
  Pallas kernels: 16.7 us -> 13 us
    pallas_call x5, Pallas kernels: 16.7 us -> 13 us  [call(): pl.pallas_call(kernel, out_shape=outs, in_specs=[pl.BlockSpec(memory_spac...]
  transfers between devices with their start and end apart: 5 -> 5, of which waited for: 1 -> 1; matrix products, arithmetic and copies ran while one was open for 0% -> 0% of each run, Pallas kernels for 23% -> 17%
where the time goes in v6:
time: 43.2 us; the launch traced here: 42.9 us
  starting transfers between devices  29.5 us (68%)
  Pallas kernels  13 us (30%)
    ppermute x4, starting transfers between devices, shifted(): lax.ppermute(block, axis, [(i, i + step) for i in range(count) if 0 <= i...  22.3 us
    pallas_call x5, Pallas kernels, call(): pl.pallas_call(kernel, out_shape=outs, in_specs=[pl.BlockSpec(memory_spac...  13 us
    all_to_all x1, starting transfers between devices, body(): slab = lax.all_to_all(mine, 'sub', 0, 0).reshape(subs * coarse, 256)  7.12 us
  transfers between devices with their start and end apart: 5, of which 1 were waited for; matrix products, arithmetic and copies ran while one was open for 0% of the time, Pallas kernels for 17%

profile of v6, /device:TPU:6, one launch (start us, length us, event | category | flops | bytes accessed | tf_op | source)
XLA Modules:
  0.0 42.9 jit_solution(11277606285406855112)
XLA Ops:
  0.0 2.8 %shard_map.109 = (bf16[40,384]{1,0:T(8,128)(2,1)S(1)}, bf16[8,48,256]{2,1,0:T(8,128)(2,1)}, bf16[8,176,128]{2,1,0:T(8,128)(2,1)S(1)}) custom-call(bf16[32,384]{1,0:T(8,128)(2,1)} %dual_hbm.1, s32[384]{0:T(512)} %select_hbm.1, bf16[128,128]{1,0:T(8,128)(2,1)} %bitcast.20, bf16[169,128]{1,0:T(8,128)(2,1)} %p2m_ref.3, bf16[1352,169]{1,0:T(8,128)(2,1)} %bitcast.28), custom_call_target="tpu_custom_call" | custom-call | flops 10000000000 | bytes 1000000 | tf_op jit(solution)/shard_map/pallas_call | solution.py:187
  2.8 7.1 %all-to-all-start = ((bf16[8,48,256]{2,1,0:T(8,128)(2,1)}), bf16[8,48,256]{2,1,0:T(8,128)(2,1)S(1)}, u32[]{:S(2)}, u32[]{:S(2)}) async-start(bf16[8,48,256]{2,1,0:T(8,128)(2,1)} %get-tuple-element.12), calls=%async_computation | async-start | bytes 393216 | tf_op jit(solution)/shard_map/all_to_all | solution.py:238
  10.0 3.9 %collective-permute-start = (bf16[40,384]{1,0:T(8,128)(2,1)S(1)}, bf16[40,384]{1,0:T(8,128)(2,1)S(1)}, u32[]{:S(2)}, u32[]{:S(2)}) collective-permute-start(bf16[40,384]{1,0:T(8,128)(2,1)S(1)} %get-tuple-element.10.own_ref.payload_ref), channel_id=1, source_target_pairs={{0,1},{1,2},{2,3},{3,4},{4,5},{5,6},{6,7},{7,8},{8,9},{9,10},{10,1... | collective-permute-start | bytes 92168 | tf_op jit(solution)/shard_map/ppermute | solution.py:205
  13.9 10.7 %collective-permute-start.1 = (bf16[40,384]{1,0:T(8,128)(2,1)S(1)}, bf16[40,384]{1,0:T(8,128)(2,1)S(1)}, u32[]{:S(2)}, u32[]{:S(2)}) collective-permute-start(bf16[40,384]{1,0:T(8,128)(2,1)S(1)} %get-tuple-element.10.own_ref.payload_ref), channel_id=1, source_target_pairs={{1,0},{2,1},{3,2},{4,3},{5,4},{6,5},{7,6},{8,7},{9,8},{10,9},{11,1... | collective-permute-start | bytes 92168 | tf_op jit(solution)/shard_map/ppermute | solution.py:205
  24.6 0.0 copy-done
  24.6 0.0 copy-done.1
  24.7 0.0 copy-done.2
  24.7 0.0 copy-start.5
  24.7 1.3 %shard_map.110.table_ref = bf16[4,176,1024]{2,1,0:T(8,128)(2,1)S(1)} custom-call(bf16[128,128]{1,0:T(8,128)(2,1)S(1)} %bitcast.21, bf16[169,128]{1,0:T(8,128)(2,1)S(1)} %copy-done.1, bf16[5408,169]{1,0:T(8,128)(2,1)S(1)} %bitcast.16), custom_call_target="tpu_custom_call" | custom-call | flops 100000000 | bytes 1000000 | tf_op jit(solution)/shard_map/pallas_call | solution.py:187
  26.0 0.0 collective-permute-done.low_ref
  26.0 0.2 collective-permute-done.1.high_ref
  26.2 0.0 copy-done.5
  26.2 2.5 %shard_map.111.field_ref = f32[128,384]{1,0:T(8,128)S(1)} custom-call(bf16[40,384]{1,0:T(8,128)(2,1)S(1)} %get-tuple-element.10.own_ref.payload_ref, bf16[40,384]{1,0:T(8,128)(2,1)S(1)} %collective-permute-done.low_ref, bf16[40,384]{1,0:T(8,128)(2,1)S(1)} %collective-permute-done.1.high_ref, s32[32,384]{1,0:T(8,128)S(1)} %bitcast.25, ...), custom_call_target="tpu_custom_call" | custom-call | flops 2000000000 | bytes 1000000 | tf_op jit(solution)/shard_map/pallas_call | solution.py:187
  28.7 0.0 all-to-all-done
  28.7 1.9 %collective-permute-start.2 = (bf16[384,256]{1,0:T(8,128)(2,1)S(1)}, bf16[384,256]{1,0:T(8,128)(2,1)S(1)}, u32[]{:S(2)}, u32[]{:S(2)}) collective-permute-start(bf16[384,256]{1,0:T(8,128)(2,1)S(1)} %bitcast.17), channel_id=1, source_target_pairs={{0,8},{8,16},{16,24},{24,32},{32,40},{40,48},{48,56},{56,64},{64,7... | collective-permute-start | bytes 589832 | tf_op jit(solution)/shard_map/ppermute | solution.py:205
  30.6 5.8 %collective-permute-start.3 = (bf16[384,256]{1,0:T(8,128)(2,1)S(1)}, bf16[384,256]{1,0:T(8,128)(2,1)S(1)}, u32[]{:S(2)}, u32[]{:S(2)}) collective-permute-start(bf16[384,256]{1,0:T(8,128)(2,1)S(1)} %bitcast.18), channel_id=1, source_target_pairs={{8,0},{16,8},{24,16},{32,24},{40,32},{48,40},{56,48},{64,56},{72,6... | collective-permute-start | bytes 589832 | tf_op jit(solution)/shard_map/ppermute | solution.py:205
  36.4 0.0 copy-done.3
  36.4 0.0 copy-done.4
  36.4 0.0 copy-done.6
  36.4 0.0 copy-start.7
  36.4 3.4 %shard_map.112 = (f32[128,384]{1,0:T(8,128)S(1)}, bf16[16,169,169]{2,1,0:T(8,128)(2,1)S(1)}) custom-call(bf16[40,384]{1,0:T(8,128)(2,1)S(1)} %get-tuple-element.10.own_ref.payload_ref, bf16[40,384]{1,0:T(8,128)(2,1)S(1)} %collective-permute-done.low_ref, bf16[40,384]{1,0:T(8,128)(2,1)S(1)} %collective-permute-done.1.high_ref, s32[27,384]{1,0:T(8,128)S(1)} %bitcast.26, ...), custom_call_target="tpu_custom_call" | custom-call | flops 3000000000 | bytes 2000000 | tf_op jit(solution)/shard_map/pallas_call | solution.py:187
  39.8 0.0 collective-permute-done.2.low_ref
  39.8 0.0 collective-permute-done.3.high_ref
  39.8 3.1 %shard_map.113 = bf16[32,384]{1,0:T(8,128)(2,1)} custom-call(f32[128,384]{1,0:T(8,128)S(1)} %get-tuple-element.11.field_ref, bf16[384,256]{1,0:T(8,128)(2,1)S(1)} %bitcast.19, bf16[384,256]{1,0:T(8,128)(2,1)S(1)} %collective-permute-done.2.low_ref, bf16[384,256]{1,0:T(8,128)(2,1)S(1)} %collective-permute-done.3.high_ref, s32[16,48]{1,0:T(8,128)S(1)} %bitcast.27, ...), custom_call_target="tpu_custom_call" | custom-call | flops 1000000000 | bytes 3000000 | tf_op jit(solution)/shard_map/pallas_call | solution.py:187
  (7 shorter events, 0.0 us)
Async XLA Ops:
  0.0 24.6 %copy-start = (bf16[32,169,169]{2,0,1:T(8,128)(2,1)S(1)}, bf16[32,169,169]{2,0,1:T(8,128)(2,1)}, u32[]{:S(2)}) copy-start(bf16[32,169,169]{2,0,1:T(8,128)(2,1)} %param.19) | copy-start | bytes 5483716
  0.0 24.6 %copy-start.1 = (bf16[169,128]{1,0:T(8,128)(2,1)S(1)}, bf16[169,128]{1,0:T(8,128)(2,1)}, u32[]{:S(2)}) copy-start(bf16[169,128]{1,0:T(8,128)(2,1)} %p2m_ref.3) | copy-start | bytes 129796
  0.0 24.7 %copy-start.2 = (bf16[4,128,32]{1,2,0:T(8,128)(2,1)S(1)}, bf16[4,128,32]{1,2,0:T(8,128)(2,1)}, u32[]{:S(2)}) copy-start(bf16[4,128,32]{1,2,0:T(8,128)(2,1)} %param.13) | copy-start | bytes 98308
  2.8 25.8 %all-to-all-start = ((bf16[8,48,256]{2,1,0:T(8,128)(2,1)}), bf16[8,48,256]{2,1,0:T(8,128)(2,1)S(1)}, u32[]{:S(2)}, u32[]{:S(2)}) async-start(bf16[8,48,256]{2,1,0:T(8,128)(2,1)} %get-tuple-element.12), calls=%async_computation | async-start | bytes 393216 | tf_op jit(solution)/shard_map/all_to_all | solution.py:238
  10.0 16.0 %collective-permute-start = (bf16[40,384]{1,0:T(8,128)(2,1)S(1)}, bf16[40,384]{1,0:T(8,128)(2,1)S(1)}, u32[]{:S(2)}, u32[]{:S(2)}) collective-permute-start(bf16[40,384]{1,0:T(8,128)(2,1)S(1)} %get-tuple-element.10.own_ref.payload_ref), channel_id=1, source_target_pairs={{0,1},{1,2},{2,3},{3,4},{4,5},{5,6},{6,7},{7,8},{8,9},{9,10},{10,1... | collective-permute-start | bytes 92168 | tf_op jit(solution)/shard_map/ppermute | solution.py:205
  13.9 12.3 %collective-permute-start.1 = (bf16[40,384]{1,0:T(8,128)(2,1)S(1)}, bf16[40,384]{1,0:T(8,128)(2,1)S(1)}, u32[]{:S(2)}, u32[]{:S(2)}) collective-permute-start(bf16[40,384]{1,0:T(8,128)(2,1)S(1)} %get-tuple-element.10.own_ref.payload_ref), channel_id=1, source_target_pairs={{1,0},{2,1},{3,2},{4,3},{5,4},{6,5},{7,6},{8,7},{9,8},{10,9},{11,1... | collective-permute-start | bytes 92168 | tf_op jit(solution)/shard_map/ppermute | solution.py:205
  24.7 1.5 %copy-start.5 = (s32[384,32]{0,1:T(8,128)S(1)}, s32[384,32]{0,1:T(8,128)}, u32[]{:S(2)}) copy-start(s32[384,32]{0,1:T(8,128)} %param.16) | copy-start | bytes 147460
  26.2 10.2 %copy-start.3 = (bf16[16,169,169]{2,0,1:T(8,128)(2,1)S(1)}, bf16[16,169,169]{2,0,1:T(8,128)(2,1)}, u32[]{:S(2)}) copy-start(bf16[16,169,169]{2,0,1:T(8,128)(2,1)} %param.21) | copy-start | bytes 2741860
  26.2 10.2 %copy-start.4 = (bf16[27,128,128]{2,1,0:T(8,128)(2,1)S(1)}, bf16[27,128,128]{2,1,0:T(8,128)(2,1)}, u32[]{:S(2)}) copy-start(bf16[27,128,128]{2,1,0:T(8,128)(2,1)} %near_ref.1) | copy-start | bytes 2654212
  26.2 10.2 %copy-start.6 = (s32[384,27]{0,1:T(8,128)S(1)}, s32[384,27]{0,1:T(8,128)}, u32[]{:S(2)}) copy-start(s32[384,27]{0,1:T(8,128)} %param.14) | copy-start | bytes 124420
  28.7 11.1 %collective-permute-start.2 = (bf16[384,256]{1,0:T(8,128)(2,1)S(1)}, bf16[384,256]{1,0:T(8,128)(2,1)S(1)}, u32[]{:S(2)}, u32[]{:S(2)}) collective-permute-start(bf16[384,256]{1,0:T(8,128)(2,1)S(1)} %bitcast.17), channel_id=1, source_target_pairs={{0,8},{8,16},{16,24},{24,32},{32,40},{40,48},{48,56},{56,64},{64,7... | collective-permute-start | bytes 589832 | tf_op jit(solution)/shard_map/ppermute | solution.py:205
  30.6 9.2 %collective-permute-start.3 = (bf16[384,256]{1,0:T(8,128)(2,1)S(1)}, bf16[384,256]{1,0:T(8,128)(2,1)S(1)}, u32[]{:S(2)}, u32[]{:S(2)}) collective-permute-start(bf16[384,256]{1,0:T(8,128)(2,1)S(1)} %bitcast.18), channel_id=1, source_target_pairs={{8,0},{16,8},{24,16},{32,24},{40,32},{48,40},{56,48},{64,56},{72,6... | collective-permute-start | bytes 589832 | tf_op jit(solution)/shard_map/ppermute | solution.py:205
  36.4 3.4 %copy-start.7 = (s32[48,16]{0,1:T(8,128)S(1)}, s32[48,16]{0,1:T(8,128)}, u32[]{:S(2)}) copy-start(s32[48,16]{0,1:T(8,128)} %param.20) | copy-start | bytes 9220

commit v7 on v6

--- a/solution.py
+++ b/solution.py
@@ -5,7 +5,8 @@
 from jax.experimental.pallas import tpu as pltpu
 from jax.sharding import PartitionSpec as P
 
-GROUP = 8
+LEAF_GROUP = 8
+NEAR_GROUP = 14
 F32 = jnp.float32
 BF16 = jnp.bfloat16
 NT = (((1,), (1,)), ((), ()))
@@ -57,7 +58,7 @@
         tables, rows = [], []
         for i in (j, j + 1):
             table = product[pl.ds(i, order, stride=8), :].astype(BF16)
-            table_ref[i, :order] = table
+            table_ref[:order, i * width : (i + 1) * width] = table
             tables.append(table)
             rows.append(refined[pl.ds(i, coarse, stride=8), :].astype(BF16))
         total = total + dot(jnp.concatenate(rows, axis=1), jnp.concatenate(tables, axis=1), NT)
@@ -108,13 +109,13 @@
 
 def table_kernel(joined_ref, p2m_ref, m2l_ref, out_ref, product):
     order, width = p2m_ref.shape
-    classes = out_ref.shape[0] * GROUP
+    classes = out_ref.shape[0] * LEAF_GROUP
     spread = dot(p2m_ref[...], joined_ref[...], NT).astype(BF16)
     by_eights(product, dot(m2l_ref[...], spread), classes)
     for c in range(classes):
-        at = slice((c % GROUP) * width, (c % GROUP + 1) * width)
+        at = slice((c % LEAF_GROUP) * width, (c % LEAF_GROUP + 1) * width)
         rows = product[c // 8, pl.ds(c % 8, order, stride=8), :]
-        out_ref[c // GROUP, :order, at] = rows.astype(BF16)
+        out_ref[c // LEAF_GROUP, :order, at] = rows.astype(BF16)
 
 
 def leaf_kernel(own_ref, low_ref, high_ref, list_ref, p2m_ref, table_ref, field_ref, window, local):
@@ -122,7 +123,7 @@
     order = p2m_ref.shape[0]
     local[...] = jnp.zeros_like(local)
     for g in range(table_ref.shape[0]):
-        index = [list_ref[c : c + 1, :] for c in range(g * GROUP, (g + 1) * GROUP)]
+        index = [list_ref[c : c + 1, :] for c in range(g * LEAF_GROUP, (g + 1) * LEAF_GROUP)]
         picker.add(index, table_ref[g], local)
     field_ref[...] = dot(p2m_ref[...], local[:order].astype(BF16), TN)
 
@@ -136,10 +137,11 @@
     classes = list_ref.shape[0]
     joined = joined_ref[...]
     out_ref[...] = field_ref[...]
-    for g in range(0, classes, GROUP):
-        members = range(g, min(g + GROUP, classes))
+    for g in range(0, classes, NEAR_GROUP):
+        members = range(g, min(g + NEAR_GROUP, classes))
         for c in members:
-            table[:, (c - g) * width : (c - g + 1) * width] = dot(near_ref[c], joined, NT).astype(BF16)
+            at = (c - g) * width
+            table[:, at : at + width] = dot(near_ref[c], joined, NT).astype(BF16)
         index = [list_ref[c : c + 1, :] for c in members]
         picker.add(index, table[:, : len(members) * width], out_ref)
     classes, order, _ = coarse_ref.shape
@@ -163,13 +165,17 @@
     hot = jnp.concatenate(
         [jnp.where(index[:, c : c + 1] == spot, 1.0, 0.0).astype(BF16) for c in range(classes)], axis=0
     )
-    picked = dot(hot, window).astype(BF16)
+    count = hot.shape[0] // 4
+    picked = jnp.concatenate(
+        [dot(hot[i * count : (i + 1) * count], window).astype(BF16) for i in range(4)], axis=0
+    )
     total = jnp.zeros((coarse, order), F32)
     for c in range(classes):
         total = total + dot(picked[c * coarse : (c + 1) * coarse, :order], m2l_ref[c], NT)
     local = total.astype(BF16)
+    parts = dot(local, table_ref[:order])
     for j in range(8):
-        down[pl.ds(j, coarse, stride=8), :] = dot(local, table_ref[j, :order])
+        down[pl.ds(j, coarse, stride=8), :] = parts[:, j * 128 : (j + 1) * 128]
     field = (field_ref[...] + jnp.transpose(down[...])).astype(BF16)
     by_kind = dot(joined_ref[...], field)
     kind = payload_ref[span : span + 1, :].astype(F32)
@@ -222,7 +228,7 @@
         (
             jax.ShapeDtypeStruct((span + 8, boxes), BF16),
             jax.ShapeDtypeStruct((subs, coarse, 256), BF16),
-            jax.ShapeDtypeStruct((8, 176, width), BF16),
+            jax.ShapeDtypeStruct((176, 8 * width), BF16),
         ),
         [pltpu.VMEM(a.shape, a.dtype) for a in (dual_coeffs, refine_select, joined, p2m, m2m_rows)]
         + [
@@ -239,7 +245,7 @@
     windows = (payload, low, high)
     leaf_table = call(
         table_kernel,
-        jax.ShapeDtypeStruct((leaf_m2l.shape[0] // GROUP, 176, GROUP * width), BF16),
+        jax.ShapeDtypeStruct((leaf_m2l.shape[0] // LEAF_GROUP, 176, LEAF_GROUP * width), BF16),
         [pltpu.VMEM((leaf_m2l.shape[0] // 8, 8 * order, width), F32)],
         (joined, p2m, leaf_rows),
         100_000_000, 1.0,
@@ -258,7 +264,7 @@
         (jax.ShapeDtypeStruct((width, boxes), F32), jax.ShapeDtypeStruct(coarse_m2l.shape, BF16)),
         [
             pltpu.VMEM((5 * (span + 8), 256), BF16),
-            pltpu.VMEM((width, GROUP * width), BF16),
+            pltpu.VMEM((width, NEAR_GROUP * width), BF16),
             pltpu.VMEM((2, coarse_m2l.shape[0] // 8, 8 * order, 128), F32),
         ],
         (*windows, near_list.T, joined, near_tiles, leaf_field, coarse_rows),

time: 43.2 us -> 42.3 us (0.979)
  Pallas kernels: 13 us -> 12.1 us
    pallas_call x5, Pallas kernels: 13 us -> 12.1 us  [call(): pl.pallas_call(kernel, out_shape=outs, in_specs=[pl.BlockSpec(memory_spac...]
  transfers between devices with their start and end apart: 5 -> 5, of which waited for: 1 -> 1; matrix products, arithmetic and copies ran while one was open for 0% -> 0% of each run, Pallas kernels for 17% -> 16%
where the time goes in v7:
time: 42.3 us; the launch traced here: 42 us
  starting transfers between devices  29.5 us (70%)
  Pallas kernels  12.1 us (29%)
    ppermute x4, starting transfers between devices, shifted(): lax.ppermute(block, axis, [(i, i + step) for i in range(count) if 0 <= i...  22.3 us
    pallas_call x5, Pallas kernels, call(): pl.pallas_call(kernel, out_shape=outs, in_specs=[pl.BlockSpec(memory_spac...  12.1 us
    all_to_all x1, starting transfers between devices, body(): slab = lax.all_to_all(mine, 'sub', 0, 0).reshape(subs * coarse, 256)  7.12 us
  transfers between devices with their start and end apart: 5, of which 1 were waited for; matrix products, arithmetic and copies ran while one was open for 0% of the time, Pallas kernels for 16%

profile of v7, /device:TPU:6, one launch (start us, length us, event | category | flops | bytes accessed | tf_op | source)
XLA Modules:
  0.0 42.0 jit_solution(1596313834699321998)
XLA Ops:
  0.0 2.8 %shard_map.109 = (bf16[40,384]{1,0:T(8,128)(2,1)S(1)}, bf16[8,48,256]{2,1,0:T(8,128)(2,1)}, bf16[176,1024]{1,0:T(8,128)(2,1)S(1)}) custom-call(bf16[32,384]{1,0:T(8,128)(2,1)} %dual_hbm.1, s32[384]{0:T(512)} %select_hbm.1, bf16[128,128]{1,0:T(8,128)(2,1)} %bitcast.20, bf16[169,128]{1,0:T(8,128)(2,1)} %p2m_ref.3, bf16[1352,169]{1,0:T(8,128)(2,1)} %bitcast.28), custom_call_target="tpu_custom_call" | custom-call | flops 10000000000 | bytes 1000000 | tf_op jit(solution)/shard_map/pallas_call | solution.py:193
  2.8 7.1 %all-to-all-start = ((bf16[8,48,256]{2,1,0:T(8,128)(2,1)}), bf16[8,48,256]{2,1,0:T(8,128)(2,1)S(1)}, u32[]{:S(2)}, u32[]{:S(2)}) async-start(bf16[8,48,256]{2,1,0:T(8,128)(2,1)} %get-tuple-element.12), calls=%async_computation | async-start | bytes 393216 | tf_op jit(solution)/shard_map/all_to_all | solution.py:244
  10.0 3.9 %collective-permute-start = (bf16[40,384]{1,0:T(8,128)(2,1)S(1)}, bf16[40,384]{1,0:T(8,128)(2,1)S(1)}, u32[]{:S(2)}, u32[]{:S(2)}) collective-permute-start(bf16[40,384]{1,0:T(8,128)(2,1)S(1)} %get-tuple-element.10.own_ref.payload_ref), channel_id=1, source_target_pairs={{0,1},{1,2},{2,3},{3,4},{4,5},{5,6},{6,7},{7,8},{8,9},{9,10},{10,1... | collective-permute-start | bytes 92168 | tf_op jit(solution)/shard_map/ppermute | solution.py:211
  13.9 10.8 %collective-permute-start.1 = (bf16[40,384]{1,0:T(8,128)(2,1)S(1)}, bf16[40,384]{1,0:T(8,128)(2,1)S(1)}, u32[]{:S(2)}, u32[]{:S(2)}) collective-permute-start(bf16[40,384]{1,0:T(8,128)(2,1)S(1)} %get-tuple-element.10.own_ref.payload_ref), channel_id=1, source_target_pairs={{1,0},{2,1},{3,2},{4,3},{5,4},{6,5},{7,6},{8,7},{9,8},{10,9},{11,1... | collective-permute-start | bytes 92168 | tf_op jit(solution)/shard_map/ppermute | solution.py:211
  24.6 0.0 copy-done
  24.6 0.0 copy-done.1
  24.7 0.0 copy-done.2
  24.7 0.0 copy-start.5
  24.7 1.3 %shard_map.110.table_ref = bf16[4,176,1024]{2,1,0:T(8,128)(2,1)S(1)} custom-call(bf16[128,128]{1,0:T(8,128)(2,1)S(1)} %bitcast.21, bf16[169,128]{1,0:T(8,128)(2,1)S(1)} %copy-done.1, bf16[5408,169]{1,0:T(8,128)(2,1)S(1)} %bitcast.16), custom_call_target="tpu_custom_call" | custom-call | flops 100000000 | bytes 1000000 | tf_op jit(solution)/shard_map/pallas_call | solution.py:193
  26.0 0.0 collective-permute-done.low_ref
  26.0 0.2 collective-permute-done.1.high_ref
  26.2 0.0 copy-done.5
  26.2 2.5 %shard_map.111.field_ref = f32[128,384]{1,0:T(8,128)S(1)} custom-call(bf16[40,384]{1,0:T(8,128)(2,1)S(1)} %get-tuple-element.10.own_ref.payload_ref, bf16[40,384]{1,0:T(8,128)(2,1)S(1)} %collective-permute-done.low_ref, bf16[40,384]{1,0:T(8,128)(2,1)S(1)} %collective-permute-done.1.high_ref, s32[32,384]{1,0:T(8,128)S(1)} %bitcast.25, ...), custom_call_target="tpu_custom_call" | custom-call | flops 2000000000 | bytes 1000000 | tf_op jit(solution)/shard_map/pallas_call | solution.py:193
  28.7 0.0 all-to-all-done
  28.7 1.9 %collective-permute-start.2 = (bf16[384,256]{1,0:T(8,128)(2,1)S(1)}, bf16[384,256]{1,0:T(8,128)(2,1)S(1)}, u32[]{:S(2)}, u32[]{:S(2)}) collective-permute-start(bf16[384,256]{1,0:T(8,128)(2,1)S(1)} %bitcast.17), channel_id=1, source_target_pairs={{0,8},{8,16},{16,24},{24,32},{32,40},{40,48},{48,56},{56,64},{64,7... | collective-permute-start | bytes 589832 | tf_op jit(solution)/shard_map/ppermute | solution.py:211
  30.6 5.8 %collective-permute-start.3 = (bf16[384,256]{1,0:T(8,128)(2,1)S(1)}, bf16[384,256]{1,0:T(8,128)(2,1)S(1)}, u32[]{:S(2)}, u32[]{:S(2)}) collective-permute-start(bf16[384,256]{1,0:T(8,128)(2,1)S(1)} %bitcast.18), channel_id=1, source_target_pairs={{8,0},{16,8},{24,16},{32,24},{40,32},{48,40},{56,48},{64,56},{72,6... | collective-permute-start | bytes 589832 | tf_op jit(solution)/shard_map/ppermute | solution.py:211
  36.4 0.0 copy-done.3
  36.4 0.0 copy-done.4
  36.4 0.0 copy-done.6
  36.4 0.0 copy-start.7
  36.4 3.1 %shard_map.112 = (f32[128,384]{1,0:T(8,128)S(1)}, bf16[16,169,169]{2,1,0:T(8,128)(2,1)S(1)}) custom-call(bf16[40,384]{1,0:T(8,128)(2,1)S(1)} %get-tuple-element.10.own_ref.payload_ref, bf16[40,384]{1,0:T(8,128)(2,1)S(1)} %collective-permute-done.low_ref, bf16[40,384]{1,0:T(8,128)(2,1)S(1)} %collective-permute-done.1.high_ref, s32[27,384]{1,0:T(8,128)S(1)} %bitcast.26, ...), custom_call_target="tpu_custom_call" | custom-call | flops 3000000000 | bytes 2000000 | tf_op jit(solution)/shard_map/pallas_call | solution.py:193
  39.5 0.0 collective-permute-done.2.low_ref
  39.5 0.1 collective-permute-done.3.high_ref
  39.5 2.5 %shard_map.113 = bf16[32,384]{1,0:T(8,128)(2,1)} custom-call(f32[128,384]{1,0:T(8,128)S(1)} %get-tuple-element.11.field_ref, bf16[384,256]{1,0:T(8,128)(2,1)S(1)} %bitcast.19, bf16[384,256]{1,0:T(8,128)(2,1)S(1)} %collective-permute-done.2.low_ref, bf16[384,256]{1,0:T(8,128)(2,1)S(1)} %collective-permute-done.3.high_ref, s32[16,48]{1,0:T(8,128)S(1)} %bitcast.27, ...), custom_call_target="tpu_custom_call" | custom-call | flops 1000000000 | bytes 3000000 | tf_op jit(solution)/shard_map/pallas_call | solution.py:193
  (7 shorter events, 0.0 us)
Async XLA Ops:
  0.0 24.6 %copy-start = (bf16[32,169,169]{2,0,1:T(8,128)(2,1)S(1)}, bf16[32,169,169]{2,0,1:T(8,128)(2,1)}, u32[]{:S(2)}) copy-start(bf16[32,169,169]{2,0,1:T(8,128)(2,1)} %param.19) | copy-start | bytes 5483716
  0.0 24.6 %copy-start.1 = (bf16[169,128]{1,0:T(8,128)(2,1)S(1)}, bf16[169,128]{1,0:T(8,128)(2,1)}, u32[]{:S(2)}) copy-start(bf16[169,128]{1,0:T(8,128)(2,1)} %p2m_ref.3) | copy-start | bytes 129796
  0.0 24.7 %copy-start.2 = (bf16[4,128,32]{1,2,0:T(8,128)(2,1)S(1)}, bf16[4,128,32]{1,2,0:T(8,128)(2,1)}, u32[]{:S(2)}) copy-start(bf16[4,128,32]{1,2,0:T(8,128)(2,1)} %param.13) | copy-start | bytes 98308
  2.8 25.8 %all-to-all-start = ((bf16[8,48,256]{2,1,0:T(8,128)(2,1)}), bf16[8,48,256]{2,1,0:T(8,128)(2,1)S(1)}, u32[]{:S(2)}, u32[]{:S(2)}) async-start(bf16[8,48,256]{2,1,0:T(8,128)(2,1)} %get-tuple-element.12), calls=%async_computation | async-start | bytes 393216 | tf_op jit(solution)/shard_map/all_to_all | solution.py:244
  10.0 16.0 %collective-permute-start = (bf16[40,384]{1,0:T(8,128)(2,1)S(1)}, bf16[40,384]{1,0:T(8,128)(2,1)S(1)}, u32[]{:S(2)}, u32[]{:S(2)}) collective-permute-start(bf16[40,384]{1,0:T(8,128)(2,1)S(1)} %get-tuple-element.10.own_ref.payload_ref), channel_id=1, source_target_pairs={{0,1},{1,2},{2,3},{3,4},{4,5},{5,6},{6,7},{7,8},{8,9},{9,10},{10,1... | collective-permute-start | bytes 92168 | tf_op jit(solution)/shard_map/ppermute | solution.py:211
  13.9 12.3 %collective-permute-start.1 = (bf16[40,384]{1,0:T(8,128)(2,1)S(1)}, bf16[40,384]{1,0:T(8,128)(2,1)S(1)}, u32[]{:S(2)}, u32[]{:S(2)}) collective-permute-start(bf16[40,384]{1,0:T(8,128)(2,1)S(1)} %get-tuple-element.10.own_ref.payload_ref), channel_id=1, source_target_pairs={{1,0},{2,1},{3,2},{4,3},{5,4},{6,5},{7,6},{8,7},{9,8},{10,9},{11,1... | collective-permute-start | bytes 92168 | tf_op jit(solution)/shard_map/ppermute | solution.py:211
  24.7 1.5 %copy-start.5 = (s32[384,32]{0,1:T(8,128)S(1)}, s32[384,32]{0,1:T(8,128)}, u32[]{:S(2)}) copy-start(s32[384,32]{0,1:T(8,128)} %param.16) | copy-start | bytes 147460
  26.2 10.2 %copy-start.3 = (bf16[16,169,169]{2,0,1:T(8,128)(2,1)S(1)}, bf16[16,169,169]{2,0,1:T(8,128)(2,1)}, u32[]{:S(2)}) copy-start(bf16[16,169,169]{2,0,1:T(8,128)(2,1)} %param.21) | copy-start | bytes 2741860
  26.2 10.2 %copy-start.4 = (bf16[27,128,128]{2,1,0:T(8,128)(2,1)S(1)}, bf16[27,128,128]{2,1,0:T(8,128)(2,1)}, u32[]{:S(2)}) copy-start(bf16[27,128,128]{2,1,0:T(8,128)(2,1)} %near_ref.1) | copy-start | bytes 2654212
  26.2 10.2 %copy-start.6 = (s32[384,27]{0,1:T(8,128)S(1)}, s32[384,27]{0,1:T(8,128)}, u32[]{:S(2)}) copy-start(s32[384,27]{0,1:T(8,128)} %param.14) | copy-start | bytes 124420
  28.7 10.8 %collective-permute-start.2 = (bf16[384,256]{1,0:T(8,128)(2,1)S(1)}, bf16[384,256]{1,0:T(8,128)(2,1)S(1)}, u32[]{:S(2)}, u32[]{:S(2)}) collective-permute-start(bf16[384,256]{1,0:T(8,128)(2,1)S(1)} %bitcast.17), channel_id=1, source_target_pairs={{0,8},{8,16},{16,24},{24,32},{32,40},{40,48},{48,56},{56,64},{64,7... | collective-permute-start | bytes 589832 | tf_op jit(solution)/shard_map/ppermute | solution.py:211
  30.6 8.9 %collective-permute-start.3 = (bf16[384,256]{1,0:T(8,128)(2,1)S(1)}, bf16[384,256]{1,0:T(8,128)(2,1)S(1)}, u32[]{:S(2)}, u32[]{:S(2)}) collective-permute-start(bf16[384,256]{1,0:T(8,128)(2,1)S(1)} %bitcast.18), channel_id=1, source_target_pairs={{8,0},{16,8},{24,16},{32,24},{40,32},{48,40},{56,48},{64,56},{72,6... | collective-permute-start | bytes 589832 | tf_op jit(solution)/shard_map/ppermute | solution.py:211
  36.4 3.1 %copy-start.7 = (s32[48,16]{0,1:T(8,128)S(1)}, s32[48,16]{0,1:T(8,128)}, u32[]{:S(2)}) copy-start(s32[48,16]{0,1:T(8,128)} %param.20) | copy-start | bytes 9220

commit v8 on v7

--- a/solution.py
+++ b/solution.py
@@ -68,15 +68,17 @@
 
 class Picker:
     def __init__(self, own_ref, low_ref, high_ref, window):
-        self.depth, self.boxes = own_ref.shape
+        depth, self.boxes = own_ref.shape
+        self.span = depth - 8
         self.window = window
         whole = jnp.concatenate(
-            [low_ref[...], own_ref[...], high_ref[...], jnp.zeros((self.depth, 128), BF16)], axis=1
+            [low_ref[...], own_ref[...], high_ref[...], jnp.zeros((depth, 128), BF16)], axis=1
         ).astype(F32)
         self.blocks = whole.shape[1] // 256
-        window[...] = jnp.concatenate(
-            [whole[:, b * 256 : (b + 1) * 256] for b in range(self.blocks)], axis=0
-        ).astype(BF16)
+        pieces = [whole[:, b * 256 : (b + 1) * 256] for b in range(self.blocks)]
+        kinds = [piece[self.span : self.span + 1] for piece in pieces]
+        kinds.append(jnp.zeros((8 - self.blocks, 256), F32))
+        window[...] = jnp.concatenate([piece[: self.span] for piece in pieces] + kinds, axis=0).astype(BF16)
         self.spot = lax.broadcasted_iota(jnp.int32, (256, self.boxes), 0).astype(BF16)
 
     def hot(self, index):
@@ -84,12 +86,13 @@
         return jnp.where(low == self.spot, jnp.array(1.0, BF16), jnp.array(0.0, BF16))
 
     def expand(self, index, got):
-        block, depth = index >> 8, self.depth
-        value = jnp.zeros((depth, self.boxes), F32)
+        block, span = index >> 8, self.span
+        value = jnp.zeros((span, self.boxes), F32)
+        kind = jnp.zeros((1, self.boxes), F32)
         for b in range(self.blocks):
-            value = jnp.where(block == b, got[b * depth : (b + 1) * depth], value)
-        kind = value[depth - 8 : depth - 7]
-        return [jnp.where(kind == k, value[: depth - 8], 0.0) for k in range(4)]
+            value = jnp.where(block == b, got[b * span : (b + 1) * span], value)
+            kind = jnp.where(block == b, got[self.blocks * span + b : self.blocks * span + b + 1], kind)
+        return [jnp.where(kind == k, value, 0.0) for k in range(4)]
 
     def add(self, index, table, out):
         boxes = self.boxes
@@ -107,57 +110,50 @@
         ref[b, :, :width] = split[:, b].reshape(order * 8, width)
 
 
-def table_kernel(joined_ref, p2m_ref, m2l_ref, out_ref, product):
+def field_kernel(
+    own_ref, high_ref, low_ref, leaf_list_ref, near_list_ref, p2m_ref, m2l_ref, joined_ref, near_hbm, _,
+    out_ref, near_ref, window, local, leaf_table, near_table, product, sems,
+):
+    copies = fetch((near_hbm,), (near_ref,), sems)
+    picker = Picker(own_ref, low_ref, high_ref, window)
     order, width = p2m_ref.shape
-    classes = out_ref.shape[0] * LEAF_GROUP
-    spread = dot(p2m_ref[...], joined_ref[...], NT).astype(BF16)
+    joined = joined_ref[...]
+    classes = leaf_list_ref.shape[0]
+    spread = dot(p2m_ref[...], joined, NT).astype(BF16)
     by_eights(product, dot(m2l_ref[...], spread), classes)
     for c in range(classes):
-        at = slice((c % LEAF_GROUP) * width, (c % LEAF_GROUP + 1) * width)
+        group, at = c // LEAF_GROUP, c % LEAF_GROUP * width
         rows = product[c // 8, pl.ds(c % 8, order, stride=8), :]
-        out_ref[c // LEAF_GROUP, :order, at] = rows.astype(BF16)
-
-
-def leaf_kernel(own_ref, low_ref, high_ref, list_ref, p2m_ref, table_ref, field_ref, window, local):
-    picker = Picker(own_ref, low_ref, high_ref, window)
-    order = p2m_ref.shape[0]
+        leaf_table[group, :order, at : at + width] = rows.astype(BF16)
     local[...] = jnp.zeros_like(local)
-    for g in range(table_ref.shape[0]):
-        index = [list_ref[c : c + 1, :] for c in range(g * LEAF_GROUP, (g + 1) * LEAF_GROUP)]
-        picker.add(index, table_ref[g], local)
-    field_ref[...] = dot(p2m_ref[...], local[:order].astype(BF16), TN)
-
-
-def near_kernel(
-    own_ref, low_ref, high_ref, list_ref, joined_ref, near_ref, field_ref, coarse, out_ref, coarse_ref,
-    window, table, wide,
-):
-    picker = Picker(own_ref, low_ref, high_ref, window)
-    width = near_ref.shape[1]
-    classes = list_ref.shape[0]
-    joined = joined_ref[...]
-    out_ref[...] = field_ref[...]
-    for g in range(0, classes, NEAR_GROUP):
-        members = range(g, min(g + NEAR_GROUP, classes))
-        for c in members:
-            at = (c - g) * width
-            table[:, at : at + width] = dot(near_ref[c], joined, NT).astype(BF16)
-        index = [list_ref[c : c + 1, :] for c in members]
-        picker.add(index, table[:, : len(members) * width], out_ref)
-    classes, order, _ = coarse_ref.shape
-    by_eights(wide.at[0], coarse[:, :128].astype(F32), classes)
-    by_eights(wide.at[1], coarse[:, 128:].astype(F32), classes)
+    for g in range(leaf_table.shape[0]):
+        index = [leaf_list_ref[c : c + 1, :] for c in range(g * LEAF_GROUP, (g + 1) * LEAF_GROUP)]
+        picker.add(index, leaf_table[g], local)
+    out_ref[...] = dot(p2m_ref[...], local[:order].astype(BF16), TN)
+    copies[0].wait()
+    classes = near_ref.shape[0]
     for c in range(classes):
+        group, at = c // NEAR_GROUP, c % NEAR_GROUP * width
+        near_table[group, :, at : at + width] = dot(near_ref[c], joined, NT).astype(BF16)
+    for g in range(near_table.shape[0]):
+        members = range(g * NEAR_GROUP, min((g + 1) * NEAR_GROUP, classes))
+        index = [near_list_ref[c : c + 1, :] for c in members]
+        picker.add(index, near_table[g, :, : len(members) * width], out_ref)
+
+
+def downward_kernel(
+    field_ref, slab_ref, low_ref, high_ref, list_ref, payload_ref, joined_ref, table_ref, m2l_rows,
+    out_ref, down, wide,
+):
+    order = m2l_rows.shape[1]
+    classes, coarse = list_ref.shape
+    by_eights(wide.at[0], m2l_rows[:, :128].astype(F32), classes)
+    by_eights(wide.at[1], m2l_rows[:, 128:].astype(F32), classes)
+
+    def class_table(c):
         rows = [wide[half, c // 8, pl.ds(c % 8, order, stride=8), :] for half in range(2)]
-        coarse_ref[c] = jnp.concatenate(rows, axis=1)[:, :order].astype(BF16)
-
-
-def downward_kernel(
-    field_ref, slab_ref, low_ref, high_ref, list_ref, payload_ref, joined_ref, table_ref, m2l_ref,
-    out_ref, down,
-):
-    order = m2l_ref.shape[1]
-    classes, coarse = list_ref.shape
+        return jnp.concatenate(rows, axis=1)[:, :order].astype(BF16)
+
     span = out_ref.shape[0]
     index = jnp.transpose(list_ref[...])
     window = jnp.concatenate([low_ref[...], slab_ref[...], high_ref[...]], axis=0)
@@ -171,7 +167,7 @@
     )
     total = jnp.zeros((coarse, order), F32)
     for c in range(classes):
-        total = total + dot(picked[c * coarse : (c + 1) * coarse, :order], m2l_ref[c], NT)
+        total = total + dot(picked[c * coarse : (c + 1) * coarse, :order], class_table(c), NT)
     local = total.astype(BF16)
     parts = dot(local, table_ref[:order])
     for j in range(8):
@@ -185,7 +181,7 @@
     out_ref[...] = tested.astype(BF16)
 
 
-def call(kernel, outs, scratch, args, flops, megabytes, in_hbm=()):
+def call(kernel, outs, scratch, args, flops, megabytes, in_hbm=(), anywhere=()):
     args = [
         pltpu.with_memory_space_constraint(x, pltpu.HBM) if i in in_hbm else x
         for i, x in enumerate(args)
@@ -194,7 +190,7 @@
         kernel,
         out_shape=outs,
         in_specs=[
-            pl.BlockSpec(memory_space=pltpu.HBM if i in in_hbm else pltpu.VMEM)
+            pl.BlockSpec(memory_space=pltpu.HBM if i in in_hbm else pl.ANY if i in anywhere else pltpu.VMEM)
             for i in range(len(args))
         ],
         out_specs=jax.tree.map(lambda _: pl.BlockSpec(memory_space=pltpu.VMEM), outs),
@@ -228,7 +224,7 @@
         (
             jax.ShapeDtypeStruct((span + 8, boxes), BF16),
             jax.ShapeDtypeStruct((subs, coarse, 256), BF16),
-            jax.ShapeDtypeStruct((176, 8 * width), BF16),
+            pltpu.HBM((176, 8 * width), BF16),
         ),
         [pltpu.VMEM(a.shape, a.dtype) for a in (dual_coeffs, refine_select, joined, p2m, m2m_rows)]
         + [
@@ -242,40 +238,33 @@
     low = shifted(payload, ("grp", "sub"), 1)
     high = shifted(payload, ("grp", "sub"), -1)
     slab = lax.all_to_all(mine, "sub", 0, 0).reshape(subs * coarse, 256)
-    windows = (payload, low, high)
-    leaf_table = call(
-        table_kernel,
-        jax.ShapeDtypeStruct((leaf_m2l.shape[0] // LEAF_GROUP, 176, LEAF_GROUP * width), BF16),
-        [pltpu.VMEM((leaf_m2l.shape[0] // 8, 8 * order, width), F32)],
-        (joined, p2m, leaf_rows),
-        100_000_000, 1.0,
-    )
-    leaf_field = call(
-        leaf_kernel,
-        jax.ShapeDtypeStruct((width, boxes), F32),
-        [pltpu.VMEM((5 * (span + 8), 256), BF16), pltpu.VMEM((176, boxes), F32)],
-        (*windows, leaf_list.T, p2m, leaf_table),
-        2_000_000_000, 1.0,
-    )
+    windows = (payload, high, low)
     slab_low = shifted(slab, "grp", 1)
     slab_high = shifted(slab, "grp", -1)
-    field, coarse_table = call(
-        near_kernel,
-        (jax.ShapeDtypeStruct((width, boxes), F32), jax.ShapeDtypeStruct(coarse_m2l.shape, BF16)),
+    field = call(
+        field_kernel,
+        jax.ShapeDtypeStruct((width, boxes), F32),
         [
-            pltpu.VMEM((5 * (span + 8), 256), BF16),
-            pltpu.VMEM((width, NEAR_GROUP * width), BF16),
-            pltpu.VMEM((2, coarse_m2l.shape[0] // 8, 8 * order, 128), F32),
-        ],
-        (*windows, near_list.T, joined, near_tiles, leaf_field, coarse_rows),
-        3_000_000_000, 2.0,
+            pltpu.VMEM(near_tiles.shape, BF16),
+            pltpu.VMEM((5 * span + 8, 256), BF16),
+            pltpu.VMEM((176, boxes), F32),
+            pltpu.VMEM((leaf_m2l.shape[0] // LEAF_GROUP, 176, LEAF_GROUP * width), BF16),
+            pltpu.VMEM((-(-near_tiles.shape[0] // NEAR_GROUP), width, NEAR_GROUP * width), BF16),
+            pltpu.VMEM((leaf_m2l.shape[0] // 8, 8 * order, width), F32),
+            pltpu.SemaphoreType.DMA((1,)),
+        ],
+        (*windows, leaf_list.T, near_list.T, p2m, leaf_rows, joined, near_tiles, slab),
+        2_000_000_000, 3.0, (8,), (9,),
     )
     return call(
         downward_kernel,
         jax.ShapeDtypeStruct((span, boxes), BF16),
-        [pltpu.VMEM((boxes, width), F32)],
+        [
+            pltpu.VMEM((boxes, width), F32),
+            pltpu.VMEM((2, coarse_m2l.shape[0] // 8, 8 * order, 128), F32),
+        ],
         (
-            field, slab, slab_low, slab_high, coarse_list.T, payload, joined, table, coarse_table,
+            field, slab, slab_low, slab_high, coarse_list.T, payload, joined, table, coarse_rows,
         ),
         1_000_000_000, 3.0,
     )

time: 42.3 us -> 41.7 us (0.986)
  starting transfers between devices: 29.5 us -> 28.2 us
  Pallas kernels: 12.1 us -> 13 us
    ppermute x4, starting transfers between devices: 22.3 us -> 21.1 us  [shifted(): lax.ppermute(block, axis, [(i, i + step) for i in range(count) if 0 <= i...]
    pallas_call x5 -> x3, Pallas kernels: 12.1 us -> 13 us  [call(): pl.pallas_call(kernel, out_shape=outs, in_specs=[pl.BlockSpec(memory_spac...]
  transfers between devices with their start and end apart: 5 -> 5, of which waited for: 1 -> 0; matrix products, arithmetic and copies ran while one was open for 0% -> 0% of each run, Pallas kernels for 16% -> 18%
where the time goes in v8:
time: 41.7 us; the launch traced here: 41.4 us
  starting transfers between devices  28.2 us (68%)
  Pallas kernels  13 us (31%)
    ppermute x4, starting transfers between devices, shifted(): lax.ppermute(block, axis, [(i, i + step) for i in range(count) if 0 <= i...  21.1 us
    pallas_call x3, Pallas kernels, call(): pl.pallas_call(kernel, out_shape=outs, in_specs=[pl.BlockSpec(memory_spac...  13 us
    all_to_all x1, starting transfers between devices, body(): slab = lax.all_to_all(mine, 'sub', 0, 0).reshape(subs * coarse, 256)  7.1 us
  transfers between devices with their start and end apart: 5, of which 0 were waited for; matrix products, arithmetic and copies ran while one was open for 0% of the time, Pallas kernels for 18%

profile of v8, /device:TPU:6, one launch (start us, length us, event | category | flops | bytes accessed | tf_op | source)
XLA Modules:
  0.0 41.4 jit_solution(17137035797038460079)
XLA Ops:
  0.0 0.0 copy-start.4
  0.0 0.0 copy-start.5
  0.0 2.8 %shard_map.109 = (bf16[40,384]{1,0:T(8,128)(2,1)S(1)}, bf16[8,48,256]{2,1,0:T(8,128)(2,1)}, bf16[176,1024]{1,0:T(8,128)(2,1)}) custom-call(bf16[32,384]{1,0:T(8,128)(2,1)} %dual_hbm.1, s32[384]{0:T(512)} %select_hbm.1, bf16[128,128]{1,0:T(8,128)(2,1)} %bitcast.24, bf16[169,128]{1,0:T(8,128)(2,1)} %p2m_ref.1, bf16[1352,169]{1,0:T(8,128)(2,1)} %bitcast.28), custom_call_target="tpu_custom_call" | custom-call | flops 10000000000 | bytes 1000000 | tf_op jit(solution)/shard_map/pallas_call | solution.py:189
  2.9 7.1 %all-to-all-start = ((bf16[8,48,256]{2,1,0:T(8,128)(2,1)}), bf16[8,48,256]{2,1,0:T(8,128)(2,1)S(1)}, u32[]{:S(2)}, u32[]{:S(2)}) async-start(bf16[8,48,256]{2,1,0:T(8,128)(2,1)} %get-tuple-element.9), calls=%async_computation | async-start | bytes 393216 | tf_op jit(solution)/shard_map/all_to_all | solution.py:240
  10.0 3.9 %collective-permute-start.1 = (bf16[40,384]{1,0:T(8,128)(2,1)S(1)}, bf16[40,384]{1,0:T(8,128)(2,1)S(1)}, u32[]{:S(2)}, u32[]{:S(2)}) collective-permute-start(bf16[40,384]{1,0:T(8,128)(2,1)S(1)} %get-tuple-element.8.own_ref.payload_ref), channel_id=1, source_target_pairs={{0,1},{1,2},{2,3},{3,4},{4,5},{5,6},{6,7},{7,8},{8,9},{9,10},{10,1... | collective-permute-start | bytes 92168 | tf_op jit(solution)/shard_map/ppermute | solution.py:207
  13.9 10.8 %collective-permute-start = (bf16[40,384]{1,0:T(8,128)(2,1)S(1)}, bf16[40,384]{1,0:T(8,128)(2,1)S(1)}, u32[]{:S(2)}, u32[]{:S(2)}) collective-permute-start(bf16[40,384]{1,0:T(8,128)(2,1)S(1)} %get-tuple-element.8.own_ref.payload_ref), channel_id=1, source_target_pairs={{1,0},{2,1},{3,2},{4,3},{5,4},{6,5},{7,6},{8,7},{9,8},{10,9},{11,1... | collective-permute-start | bytes 92168 | tf_op jit(solution)/shard_map/ppermute | solution.py:207
  24.7 0.0 all-to-all-done
  24.7 4.5 %collective-permute-start.3 = (bf16[384,256]{1,0:T(8,128)(2,1)S(1)}, bf16[384,256]{1,0:T(8,128)(2,1)S(1)}, u32[]{:S(2)}, u32[]{:S(2)}) collective-permute-start(bf16[384,256]{1,0:T(8,128)(2,1)S(1)} %bitcast.16), channel_id=1, source_target_pairs={{8,0},{16,8},{24,16},{32,24},{40,32},{48,40},{56,48},{64,56},{72,6... | collective-permute-start | bytes 589832 | tf_op jit(solution)/shard_map/ppermute | solution.py:207
  29.2 1.9 %collective-permute-start.2 = (bf16[384,256]{1,0:T(8,128)(2,1)S(1)}, bf16[384,256]{1,0:T(8,128)(2,1)S(1)}, u32[]{:S(2)}, u32[]{:S(2)}) collective-permute-start(bf16[384,256]{1,0:T(8,128)(2,1)S(1)} %bitcast.17), channel_id=1, source_target_pairs={{0,8},{8,16},{16,24},{24,32},{32,40},{40,48},{48,56},{56,64},{64,7... | collective-permute-start | bytes 589832 | tf_op jit(solution)/shard_map/ppermute | solution.py:207
  31.1 0.0 collective-permute-done.1.low_ref
  31.1 0.0 collective-permute-done.high_ref
  31.1 0.0 copy-done
  31.1 0.0 copy-done.2
  31.1 0.0 copy-done.3
  31.2 0.0 copy-done.4
  31.2 0.0 copy-done.5
  31.2 0.0 copy-start.1
  31.2 0.0 copy-start.6
  31.2 0.0 copy-start.7
  31.2 7.4 %shard_map.110.field_ref = f32[128,384]{1,0:T(8,128)S(1)} custom-call(bf16[40,384]{1,0:T(8,128)(2,1)S(1)} %get-tuple-element.8.own_ref.payload_ref, bf16[40,384]{1,0:T(8,128)(2,1)S(1)} %collective-permute-done.high_ref, bf16[40,384]{1,0:T(8,128)(2,1)S(1)} %collective-permute-done.1.low_ref, s32[32,384]{1,0:T(8,128)S(1)} %bitcast.22, s32[27,384]{1,0:T(8,128)S(1)} %bitcast.23, ...), custom_call_target="tpu_custom_call" | custom-call | flops 2000000000 | bytes 3000000 | tf_op jit(solution)/shard_map/pallas_call | solution.py:189
  38.6 0.0 collective-permute-done.3.high_ref
  38.6 0.0 collective-permute-done.2.low_ref
  38.6 0.0 copy-done.1
  38.6 2.8 %shard_map.111 = bf16[32,384]{1,0:T(8,128)(2,1)} custom-call(f32[128,384]{1,0:T(8,128)S(1)} %shard_map.110.field_ref, bf16[384,256]{1,0:T(8,128)(2,1)S(1)} %bitcast.19, bf16[384,256]{1,0:T(8,128)(2,1)S(1)} %collective-permute-done.2.low_ref, bf16[384,256]{1,0:T(8,128)(2,1)S(1)} %collective-permute-done.3.high_ref, s32[16,48]{1,0:T(8,128)S(1)} %bitcast.27, ...), custom_call_target="tpu_custom_call" | custom-call | flops 1000000000 | bytes 3000000 | tf_op jit(solution)/shard_map/pallas_call | solution.py:189
  (5 shorter events, 0.0 us)
Async XLA Ops:
  0.0 31.1 %copy-start = (bf16[32,169,169]{2,0,1:T(8,128)(2,1)S(1)}, bf16[32,169,169]{2,0,1:T(8,128)(2,1)}, u32[]{:S(2)}) copy-start(bf16[32,169,169]{2,0,1:T(8,128)(2,1)} %param.19) | copy-start | bytes 5483716
  0.0 31.1 %copy-start.2 = (s32[384,32]{0,1:T(8,128)S(1)}, s32[384,32]{0,1:T(8,128)}, u32[]{:S(2)}) copy-start(s32[384,32]{0,1:T(8,128)} %param.16) | copy-start | bytes 147460
  0.0 31.1 %copy-start.3 = (s32[384,27]{0,1:T(8,128)S(1)}, s32[384,27]{0,1:T(8,128)}, u32[]{:S(2)}) copy-start(s32[384,27]{0,1:T(8,128)} %param.14) | copy-start | bytes 124420
  0.0 31.1 %copy-start.4 = (bf16[169,128]{1,0:T(8,128)(2,1)S(1)}, bf16[169,128]{1,0:T(8,128)(2,1)}, u32[]{:S(2)}) copy-start(bf16[169,128]{1,0:T(8,128)(2,1)} %p2m_ref.1) | copy-start | bytes 129796
  0.0 31.1 %copy-start.5 = (bf16[4,128,32]{1,2,0:T(8,128)(2,1)S(1)}, bf16[4,128,32]{1,2,0:T(8,128)(2,1)}, u32[]{:S(2)}) copy-start(bf16[4,128,32]{1,2,0:T(8,128)(2,1)} %param.13) | copy-start | bytes 98308
  2.9 21.8 %all-to-all-start = ((bf16[8,48,256]{2,1,0:T(8,128)(2,1)}), bf16[8,48,256]{2,1,0:T(8,128)(2,1)S(1)}, u32[]{:S(2)}, u32[]{:S(2)}) async-start(bf16[8,48,256]{2,1,0:T(8,128)(2,1)} %get-tuple-element.9), calls=%async_computation | async-start | bytes 393216 | tf_op jit(solution)/shard_map/all_to_all | solution.py:240
  10.0 21.2 %collective-permute-start.1 = (bf16[40,384]{1,0:T(8,128)(2,1)S(1)}, bf16[40,384]{1,0:T(8,128)(2,1)S(1)}, u32[]{:S(2)}, u32[]{:S(2)}) collective-permute-start(bf16[40,384]{1,0:T(8,128)(2,1)S(1)} %get-tuple-element.8.own_ref.payload_ref), channel_id=1, source_target_pairs={{0,1},{1,2},{2,3},{3,4},{4,5},{5,6},{6,7},{7,8},{8,9},{9,10},{10,1... | collective-permute-start | bytes 92168 | tf_op jit(solution)/shard_map/ppermute | solution.py:207
  13.9 17.2 %collective-permute-start = (bf16[40,384]{1,0:T(8,128)(2,1)S(1)}, bf16[40,384]{1,0:T(8,128)(2,1)S(1)}, u32[]{:S(2)}, u32[]{:S(2)}) collective-permute-start(bf16[40,384]{1,0:T(8,128)(2,1)S(1)} %get-tuple-element.8.own_ref.payload_ref), channel_id=1, source_target_pairs={{1,0},{2,1},{3,2},{4,3},{5,4},{6,5},{7,6},{8,7},{9,8},{10,9},{11,1... | collective-permute-start | bytes 92168 | tf_op jit(solution)/shard_map/ppermute | solution.py:207
  24.7 13.9 %collective-permute-start.3 = (bf16[384,256]{1,0:T(8,128)(2,1)S(1)}, bf16[384,256]{1,0:T(8,128)(2,1)S(1)}, u32[]{:S(2)}, u32[]{:S(2)}) collective-permute-start(bf16[384,256]{1,0:T(8,128)(2,1)S(1)} %bitcast.16), channel_id=1, source_target_pairs={{8,0},{16,8},{24,16},{32,24},{40,32},{48,40},{56,48},{64,56},{72,6... | collective-permute-start | bytes 589832 | tf_op jit(solution)/shard_map/ppermute | solution.py:207
  29.2 9.4 %collective-permute-start.2 = (bf16[384,256]{1,0:T(8,128)(2,1)S(1)}, bf16[384,256]{1,0:T(8,128)(2,1)S(1)}, u32[]{:S(2)}, u32[]{:S(2)}) collective-permute-start(bf16[384,256]{1,0:T(8,128)(2,1)S(1)} %bitcast.17), channel_id=1, source_target_pairs={{0,8},{8,16},{16,24},{24,32},{32,40},{40,48},{48,56},{56,64},{64,7... | collective-permute-start | bytes 589832 | tf_op jit(solution)/shard_map/ppermute | solution.py:207
  31.2 7.4 %copy-start.1 = (bf16[16,169,169]{2,0,1:T(8,128)(2,1)S(1)}, bf16[16,169,169]{2,0,1:T(8,128)(2,1)}, u32[]{:S(2)}) copy-start(bf16[16,169,169]{2,0,1:T(8,128)(2,1)} %param.21) | copy-start | bytes 2741860
  31.2 7.4 %copy-start.6 = (s32[48,16]{0,1:T(8,128)S(1)}, s32[48,16]{0,1:T(8,128)}, u32[]{:S(2)}) copy-start(s32[48,16]{0,1:T(8,128)} %param.20) | copy-start | bytes 9220
  31.2 7.4 %copy-start.7 = (bf16[176,1024]{1,0:T(8,128)(2,1)S(1)}, bf16[176,1024]{1,0:T(8,128)(2,1)}, u32[]{:S(2)}) copy-start(bf16[176,1024]{1,0:T(8,128)(2,1)} %get-tuple-element.10.table_ref) | copy-start | bytes 1081348

commit v9 on v8

--- a/solution.py
+++ b/solution.py
@@ -5,7 +5,7 @@
 from jax.experimental.pallas import tpu as pltpu
 from jax.sharding import PartitionSpec as P
 
-LEAF_GROUP = 8
+LEAF_GROUP = 16
 NEAR_GROUP = 14
 F32 = jnp.float32
 BF16 = jnp.bfloat16
@@ -120,7 +120,9 @@
     joined = joined_ref[...]
     classes = leaf_list_ref.shape[0]
     spread = dot(p2m_ref[...], joined, NT).astype(BF16)
-    by_eights(product, dot(m2l_ref[...], spread), classes)
+    half = m2l_ref.shape[0] // 2
+    halves = [dot(m2l_ref[i * half : (i + 1) * half], spread) for i in range(2)]
+    by_eights(product, jnp.concatenate(halves, axis=0), classes)
     for c in range(classes):
         group, at = c // LEAF_GROUP, c % LEAF_GROUP * width
         rows = product[c // 8, pl.ds(c % 8, order, stride=8), :]

time: 41.7 us -> 41.4 us (level)
  Pallas kernels: 13 us -> 12.2 us
  waiting for transfers between devices: 0.01 us -> 0.47 us
    pallas_call x3, Pallas kernels: 13 us -> 12.2 us  [call(): pl.pallas_call(kernel, out_shape=outs, in_specs=[pl.BlockSpec(memory_spac...]
    ppermute x4, waiting for transfers between devices: 0.01 us -> 0.46 us  [shifted(): lax.ppermute(block, axis, [(i, i + step) for i in range(count) if 0 <= i...]
  transfers between devices with their start and end apart: 5 -> 5, of which waited for: 0 -> 1; matrix products, arithmetic and copies ran while one was open for 0% -> 0% of each run, Pallas kernels for 18% -> 16%
where the time goes in v9:
time: 41.4 us; the launch traced here: 41 us
  starting transfers between devices  28.2 us (68%)
  Pallas kernels  12.2 us (29%)
  waiting for transfers between devices  0.47 us (1%)
    ppermute x4, starting transfers between devices, shifted(): lax.ppermute(block, axis, [(i, i + step) for i in range(count) if 0 <= i...  21.1 us
    pallas_call x3, Pallas kernels, call(): pl.pallas_call(kernel, out_shape=outs, in_specs=[pl.BlockSpec(memory_spac...  12.2 us
    all_to_all x1, starting transfers between devices, body(): slab = lax.all_to_all(mine, 'sub', 0, 0).reshape(subs * coarse, 256)  7.1 us
  transfers between devices with their start and end apart: 5, of which 1 were waited for; matrix products, arithmetic and copies ran while one was open for 0% of the time, Pallas kernels for 16%

profile of v9, /device:TPU:6, one launch (start us, length us, event | category | flops | bytes accessed | tf_op | source)
XLA Modules:
  0.0 41.0 jit_solution(16648772111158094514)
XLA Ops:
  0.0 0.0 copy-start.4
  0.0 0.0 copy-start.5
  0.0 2.8 %shard_map.109 = (bf16[40,384]{1,0:T(8,128)(2,1)S(1)}, bf16[8,48,256]{2,1,0:T(8,128)(2,1)}, bf16[176,1024]{1,0:T(8,128)(2,1)}) custom-call(bf16[32,384]{1,0:T(8,128)(2,1)} %dual_hbm.1, s32[384]{0:T(512)} %select_hbm.1, bf16[128,128]{1,0:T(8,128)(2,1)} %bitcast.24, bf16[169,128]{1,0:T(8,128)(2,1)} %p2m_ref.1, bf16[1352,169]{1,0:T(8,128)(2,1)} %bitcast.28), custom_call_target="tpu_custom_call" | custom-call | flops 10000000000 | bytes 1000000 | tf_op jit(solution)/shard_map/pallas_call | solution.py:191
  2.9 7.1 %all-to-all-start = ((bf16[8,48,256]{2,1,0:T(8,128)(2,1)}), bf16[8,48,256]{2,1,0:T(8,128)(2,1)S(1)}, u32[]{:S(2)}, u32[]{:S(2)}) async-start(bf16[8,48,256]{2,1,0:T(8,128)(2,1)} %get-tuple-element.9), calls=%async_computation | async-start | bytes 393216 | tf_op jit(solution)/shard_map/all_to_all | solution.py:242
  10.0 3.9 %collective-permute-start.1 = (bf16[40,384]{1,0:T(8,128)(2,1)S(1)}, bf16[40,384]{1,0:T(8,128)(2,1)S(1)}, u32[]{:S(2)}, u32[]{:S(2)}) collective-permute-start(bf16[40,384]{1,0:T(8,128)(2,1)S(1)} %get-tuple-element.8.own_ref.payload_ref), channel_id=1, source_target_pairs={{0,1},{1,2},{2,3},{3,4},{4,5},{5,6},{6,7},{7,8},{8,9},{9,10},{10,1... | collective-permute-start | bytes 92168 | tf_op jit(solution)/shard_map/ppermute | solution.py:209
  13.9 10.8 %collective-permute-start = (bf16[40,384]{1,0:T(8,128)(2,1)S(1)}, bf16[40,384]{1,0:T(8,128)(2,1)S(1)}, u32[]{:S(2)}, u32[]{:S(2)}) collective-permute-start(bf16[40,384]{1,0:T(8,128)(2,1)S(1)} %get-tuple-element.8.own_ref.payload_ref), channel_id=1, source_target_pairs={{1,0},{2,1},{3,2},{4,3},{5,4},{6,5},{7,6},{8,7},{9,8},{10,9},{11,1... | collective-permute-start | bytes 92168 | tf_op jit(solution)/shard_map/ppermute | solution.py:209
  24.7 0.0 all-to-all-done
  24.7 4.5 %collective-permute-start.3 = (bf16[384,256]{1,0:T(8,128)(2,1)S(1)}, bf16[384,256]{1,0:T(8,128)(2,1)S(1)}, u32[]{:S(2)}, u32[]{:S(2)}) collective-permute-start(bf16[384,256]{1,0:T(8,128)(2,1)S(1)} %bitcast.16), channel_id=1, source_target_pairs={{8,0},{16,8},{24,16},{32,24},{40,32},{48,40},{56,48},{64,56},{72,6... | collective-permute-start | bytes 589832 | tf_op jit(solution)/shard_map/ppermute | solution.py:209
  29.2 1.9 %collective-permute-start.2 = (bf16[384,256]{1,0:T(8,128)(2,1)S(1)}, bf16[384,256]{1,0:T(8,128)(2,1)S(1)}, u32[]{:S(2)}, u32[]{:S(2)}) collective-permute-start(bf16[384,256]{1,0:T(8,128)(2,1)S(1)} %bitcast.17), channel_id=1, source_target_pairs={{0,8},{8,16},{16,24},{24,32},{32,40},{40,48},{48,56},{56,64},{64,7... | collective-permute-start | bytes 589832 | tf_op jit(solution)/shard_map/ppermute | solution.py:209
  31.1 0.0 collective-permute-done.1.low_ref
  31.1 0.0 collective-permute-done.high_ref
  31.1 0.0 copy-done
  31.1 0.0 copy-done.2
  31.1 0.0 copy-done.3
  31.2 0.0 copy-done.4
  31.2 0.0 copy-done.5
  31.2 0.0 copy-start.1
  31.2 0.0 copy-start.6
  31.2 0.0 copy-start.7
  31.2 6.6 %shard_map.110.field_ref = f32[128,384]{1,0:T(8,128)S(1)} custom-call(bf16[40,384]{1,0:T(8,128)(2,1)S(1)} %get-tuple-element.8.own_ref.payload_ref, bf16[40,384]{1,0:T(8,128)(2,1)S(1)} %collective-permute-done.high_ref, bf16[40,384]{1,0:T(8,128)(2,1)S(1)} %collective-permute-done.1.low_ref, s32[32,384]{1,0:T(8,128)S(1)} %bitcast.22, s32[27,384]{1,0:T(8,128)S(1)} %bitcast.23, ...), custom_call_target="tpu_custom_call" | custom-call | flops 2000000000 | bytes 3000000 | tf_op jit(solution)/shard_map/pallas_call | solution.py:191
  37.8 0.0 collective-permute-done.3.high_ref
  37.8 0.5 %collective-permute-done.2.low_ref = bf16[384,256]{1,0:T(8,128)(2,1)S(1)} collective-permute-done((bf16[384,256]{1,0:T(8,128)(2,1)S(1)}, bf16[384,256]{1,0:T(8,128)(2,1)S(1)}, u32[]{:S(2)}, u32[]{:S(2)}) %collective-permute-start.2) | collective-permute-done | bytes 196640 | tf_op jit(solution)/shard_map/ppermute | solution.py:209
  38.3 0.0 copy-done.1
  38.3 2.8 %shard_map.111 = bf16[32,384]{1,0:T(8,128)(2,1)} custom-call(f32[128,384]{1,0:T(8,128)S(1)} %shard_map.110.field_ref, bf16[384,256]{1,0:T(8,128)(2,1)S(1)} %bitcast.19, bf16[384,256]{1,0:T(8,128)(2,1)S(1)} %collective-permute-done.2.low_ref, bf16[384,256]{1,0:T(8,128)(2,1)S(1)} %collective-permute-done.3.high_ref, s32[16,48]{1,0:T(8,128)S(1)} %bitcast.27, ...), custom_call_target="tpu_custom_call" | custom-call | flops 1000000000 | bytes 3000000 | tf_op jit(solution)/shard_map/pallas_call | solution.py:191
  (5 shorter events, 0.0 us)
Async XLA Ops:
  0.0 31.1 %copy-start = (bf16[32,169,169]{2,0,1:T(8,128)(2,1)S(1)}, bf16[32,169,169]{2,0,1:T(8,128)(2,1)}, u32[]{:S(2)}) copy-start(bf16[32,169,169]{2,0,1:T(8,128)(2,1)} %param.19) | copy-start | bytes 5483716
  0.0 31.1 %copy-start.2 = (s32[384,32]{0,1:T(8,128)S(1)}, s32[384,32]{0,1:T(8,128)}, u32[]{:S(2)}) copy-start(s32[384,32]{0,1:T(8,128)} %param.16) | copy-start | bytes 147460
  0.0 31.1 %copy-start.3 = (s32[384,27]{0,1:T(8,128)S(1)}, s32[384,27]{0,1:T(8,128)}, u32[]{:S(2)}) copy-start(s32[384,27]{0,1:T(8,128)} %param.14) | copy-start | bytes 124420
  0.0 31.1 %copy-start.4 = (bf16[169,128]{1,0:T(8,128)(2,1)S(1)}, bf16[169,128]{1,0:T(8,128)(2,1)}, u32[]{:S(2)}) copy-start(bf16[169,128]{1,0:T(8,128)(2,1)} %p2m_ref.1) | copy-start | bytes 129796
  0.0 31.1 %copy-start.5 = (bf16[4,128,32]{1,2,0:T(8,128)(2,1)S(1)}, bf16[4,128,32]{1,2,0:T(8,128)(2,1)}, u32[]{:S(2)}) copy-start(bf16[4,128,32]{1,2,0:T(8,128)(2,1)} %param.13) | copy-start | bytes 98308
  2.9 21.8 %all-to-all-start = ((bf16[8,48,256]{2,1,0:T(8,128)(2,1)}), bf16[8,48,256]{2,1,0:T(8,128)(2,1)S(1)}, u32[]{:S(2)}, u32[]{:S(2)}) async-start(bf16[8,48,256]{2,1,0:T(8,128)(2,1)} %get-tuple-element.9), calls=%async_computation | async-start | bytes 393216 | tf_op jit(solution)/shard_map/all_to_all | solution.py:242
  10.0 21.2 %collective-permute-start.1 = (bf16[40,384]{1,0:T(8,128)(2,1)S(1)}, bf16[40,384]{1,0:T(8,128)(2,1)S(1)}, u32[]{:S(2)}, u32[]{:S(2)}) collective-permute-start(bf16[40,384]{1,0:T(8,128)(2,1)S(1)} %get-tuple-element.8.own_ref.payload_ref), channel_id=1, source_target_pairs={{0,1},{1,2},{2,3},{3,4},{4,5},{5,6},{6,7},{7,8},{8,9},{9,10},{10,1... | collective-permute-start | bytes 92168 | tf_op jit(solution)/shard_map/ppermute | solution.py:209
  13.9 17.2 %collective-permute-start = (bf16[40,384]{1,0:T(8,128)(2,1)S(1)}, bf16[40,384]{1,0:T(8,128)(2,1)S(1)}, u32[]{:S(2)}, u32[]{:S(2)}) collective-permute-start(bf16[40,384]{1,0:T(8,128)(2,1)S(1)} %get-tuple-element.8.own_ref.payload_ref), channel_id=1, source_target_pairs={{1,0},{2,1},{3,2},{4,3},{5,4},{6,5},{7,6},{8,7},{9,8},{10,9},{11,1... | collective-permute-start | bytes 92168 | tf_op jit(solution)/shard_map/ppermute | solution.py:209
  24.7 13.1 %collective-permute-start.3 = (bf16[384,256]{1,0:T(8,128)(2,1)S(1)}, bf16[384,256]{1,0:T(8,128)(2,1)S(1)}, u32[]{:S(2)}, u32[]{:S(2)}) collective-permute-start(bf16[384,256]{1,0:T(8,128)(2,1)S(1)} %bitcast.16), channel_id=1, source_target_pairs={{8,0},{16,8},{24,16},{32,24},{40,32},{48,40},{56,48},{64,56},{72,6... | collective-permute-start | bytes 589832 | tf_op jit(solution)/shard_map/ppermute | solution.py:209
  29.2 9.1 %collective-permute-start.2 = (bf16[384,256]{1,0:T(8,128)(2,1)S(1)}, bf16[384,256]{1,0:T(8,128)(2,1)S(1)}, u32[]{:S(2)}, u32[]{:S(2)}) collective-permute-start(bf16[384,256]{1,0:T(8,128)(2,1)S(1)} %bitcast.17), channel_id=1, source_target_pairs={{0,8},{8,16},{16,24},{24,32},{32,40},{40,48},{48,56},{56,64},{64,7... | collective-permute-start | bytes 589832 | tf_op jit(solution)/shard_map/ppermute | solution.py:209
  31.2 7.1 %copy-start.1 = (bf16[16,169,169]{2,0,1:T(8,128)(2,1)S(1)}, bf16[16,169,169]{2,0,1:T(8,128)(2,1)}, u32[]{:S(2)}) copy-start(bf16[16,169,169]{2,0,1:T(8,128)(2,1)} %param.21) | copy-start | bytes 2741860
  31.2 7.1 %copy-start.6 = (s32[48,16]{0,1:T(8,128)S(1)}, s32[48,16]{0,1:T(8,128)}, u32[]{:S(2)}) copy-start(s32[48,16]{0,1:T(8,128)} %param.20) | copy-start | bytes 9220
  31.2 7.1 %copy-start.7 = (bf16[176,1024]{1,0:T(8,128)(2,1)S(1)}, bf16[176,1024]{1,0:T(8,128)(2,1)}, u32[]{:S(2)}) copy-start(bf16[176,1024]{1,0:T(8,128)(2,1)} %get-tuple-element.10.table_ref) | copy-start | bytes 1081348
